TPU v7x, 512 devices: a whole 4x4x16 slice. The times are simulated.
512 devices in a mesh: island: 4 (over y_hi, core), fsdp: 32 (over y_lo, z), tp: 4 (over x).
Axes of the slice: x: 4, y: 4 (y_hi: 2, y_lo: 2; y = y_hi * 2 + y_lo), z: 16, core: 2. Of those that a mesh axis runs over, the one named last changes fastest.
Arguments:
- weights: bfloat16 [4, 6144, 4096], P('island', 'fsdp', 'tp'), may hold values from -6 to 6
- grads: bfloat16 [4, 6144, 4096], P('island', 'fsdp', 'tp'), may hold values from -200 to 200
- first_moment: bfloat16 [4, 6144, 4096], P('island', 'fsdp', 'tp'), may hold values from -3 to 3
- second_moment: bfloat16 [4, 6144, 4096], P('island', 'fsdp', 'tp'), may hold values from 0.049804688 to 0.5
- bases: bfloat16 [4, 4, 4096, 4096], P('island', None, 'tp', 'fsdp'), may hold values from -0.09375 to 0.09375
- outer_delta: bfloat16 [4, 6144, 4096], P('island', 'fsdp', 'tp'), may hold values from -3 to 3
- outer_momentum: bfloat16 [6144, 4096], P('fsdp', 'tp'), may hold values from -3 to 3
- row_fragment: int32 [6144], P('fsdp'), may hold values from 0 to 3
- sync_fragment: int32 [1], replicated, may hold values from 0 to 3
- block_map: int32 [4], P('island'), may hold values from 0 to 3
Outputs:
- new_weights: bfloat16 [4, 6144, 4096], P('island', 'fsdp', 'tp')
- new_first: bfloat16 [4, 6144, 4096], P('island', 'fsdp', 'tp')
- new_second: bfloat16 [4, 6144, 4096], P('island', 'fsdp', 'tp')
- new_momentum: bfloat16 [6144, 4096], P('fsdp', 'tp')
All inputs are finite; a program needn't handle non-finite values.
Results may differ from a plain program's by a relative error of at most 0.0049.
Values may be sent and summed in bfloat16 or wider, within the bound.
No kernel may reach another device: no remote copies, remote signals or barrier semaphores. Data moves between devices by JAX's collectives and lax.ppermute only.
A program may use at most 64 MiB of HBM per device.

v0:
```python
import jax
import jax.numpy as jnp
from jax import lax
from jax.sharding import PartitionSpec as P

K = 4096
N = 6144


beta_first = 0.9
beta_second = 0.95
adam_epsilon = 1e-08
inner_rate = 0.3
outer_rate = 0.7
nesterov = 0.9
clip_ratio = 0.5


def total_squares(grad):
    return lax.psum(jnp.sum(jnp.square(grad.astype(jnp.float32))), ("fsdp", "tp"))


def on_device(
    weights,
    grads,
    first_moment,
    second_moment,
    bases,
    outer_delta,
    outer_momentum,
    row_fragment,
    sync_fragment,
    block_map,
):
    grad = grads[0]
    squares = total_squares(grad)
    chosen = lax.dynamic_index_in_dim(bases[0], block_map[0], 0, keepdims=False)
    basis_rows = lax.all_gather(chosen, "fsdp", axis=1, tiled=True)
    partial_value = jnp.dot(grad, basis_rows, preferred_element_type=jnp.float32)
    rotated = lax.psum_scatter(partial_value, "tp", scatter_dimension=1, tiled=True)
    limit = clip_ratio * jnp.sqrt(jnp.float32(N * K))
    clip = jnp.minimum(jnp.float32(1.0), limit / jnp.sqrt(squares + 1e-06))
    scaled = clip * rotated
    first_new = beta_first * first_moment[0].astype(jnp.float32) + (1.0 - beta_first) * scaled
    second_new = (
        beta_second * second_moment[0].astype(jnp.float32) + (1.0 - beta_second) * scaled * scaled
    )
    direction = (first_new / (jnp.sqrt(second_new) + adam_epsilon)).astype(jnp.bfloat16)
    update = lax.dot_general(
        lax.all_gather(direction, "tp", axis=1, tiled=True),
        basis_rows,
        (((1,), (1,)), ((), ())),
        preferred_element_type=jnp.float32,
    )
    replicas = lax.axis_size("island")
    delta = outer_delta[0].astype(jnp.float32)
    momentum = outer_momentum.astype(jnp.float32)
    synced = (row_fragment == sync_fragment[0])[:, None]
    delta_mean = lax.psum(delta.astype(jnp.bfloat16), "island").astype(jnp.float32) / replicas
    new_momentum = jnp.where(synced, nesterov * momentum + delta_mean, momentum)
    correction = jnp.where(
        synced, outer_rate * (nesterov * new_momentum + delta_mean), jnp.float32(0.0)
    )
    weight_new = weights[0].astype(jnp.float32) - inner_rate * update - correction
    return (
        weight_new.astype(jnp.bfloat16)[None],
        first_new.astype(jnp.bfloat16)[None],
        second_new.astype(jnp.bfloat16)[None],
        new_momentum.astype(jnp.bfloat16),
    )


def solution(mesh):
    in_specs = (
        P("island", "fsdp", "tp"),
        P("island", "fsdp", "tp"),
        P("island", "fsdp", "tp"),
        P("island", "fsdp", "tp"),
        P("island", None, "tp", "fsdp"),
        P("island", "fsdp", "tp"),
        P("fsdp", "tp"),
        P("fsdp"),
        P(),
        P("island"),
    )
    out_specs = (
        P("island", "fsdp", "tp"),
        P("island", "fsdp", "tp"),
        P("island", "fsdp", "tp"),
        P("fsdp", "tp"),
    )
    return jax.shard_map(
        on_device, mesh=mesh, in_specs=in_specs, out_specs=out_specs, check_vma=False
    )
```

profile of v0, /device:TPU:1, one launch (start us, length us, event | category | flops | bytes accessed | tf_op | source)
XLA Modules:
  0.0 550.7 jit_solution(17703002636875189898)
XLA Ops:
  8.0 0.0 copy-start
  8.0 0.0 all-gather.6.cloned.1.call-start
  8.8 0.5 copy-done
  9.2 0.7 constant_dynamic-slice_fusion
  10.0 0.0 all-gather.6.cloned.1.call-update
  10.0 0.0 copy-start.1
  10.0 0.0 copy-start.3
  10.0 0.0 copy-start.4
  10.0 0.0 copy-start.5
  10.0 0.0 copy-start.2
  10.0 0.0 copy-start.6
  10.1 0.0 reduce-scatter.2.cloned.1.call-start
  10.1 161.3 %all-gather.6.cloned.1.call-done = bf16[1,1,1024,4096]{3,2,1,0:T(8,128)(2,1)} async-done(((bf16[1,1,1024,128]{3,2,1,0:T(8,128)(2,1)}), bf16[1,1,1024,4096]{3,2,1,0:T(8,128)(2,1)}) %all-gather.6.cloned.1.call-update) | async-done | bytes 8388624 | tf_op jit(solution)/shard_map/all_gather | solution.py:38
  171.4 7.1 %fusion.4 = f32[192,4096]{1,0:T(8,128)} fusion(bf16[1,1,1024,4096]{3,2,1,0:T(8,128)(2,1)} %all-gather.6.cloned.1.call-done, bf16[1,192,1024]{2,1,0:T(8,128)(2,1)} %param.11), kind=kOutput, calls=%fused_computation.4 | convolution fusion | flops 1610612736 | bytes 11927552 | tf_op jit(solution)/shard_map/dot_general | solution.py:39
  178.5 0.0 reduce-scatter.2.cloned.1.call-update
  178.5 0.0 all-reduce.2.cloned.1.call-start
  178.6 0.5 all-reduce.2.cloned.1.call-update
  179.1 0.0 all-gather.4.cloned.1.call-start
  179.2 0.0 copy-done.1
  179.2 0.8 multiply_reduce_fusion
  180.0 254.7 %psum.14 = f32[]{:T(128)} all-reduce(f32[]{:T(128)} %multiply_reduce_fusion), channel_id=1, replica_groups=mesh['island'=4,'fsdp'=32,'tp'=4] {'fsdp','tp'}, use_global_device_ids=true, to_apply=%region_1.0 | all-reduce | flops 1 | bytes 8 | tf_op jit(solution)/shard_map/psum | solution.py:20
  435.4 0.0 reduce-scatter.2.cloned.1.call-done
  435.4 0.0 copy-done.3
  435.4 0.0 copy-done.4
  435.5 2.7 convert_bitcast_fusion
  438.2 0.0 all-gather.4.cloned.1.call-update
  438.9 0.0 copy-done.5
  438.9 0.0 all-reduce.2.cloned.1.call-done
  438.9 0.0 copy-done.2
  438.9 2.0 fusion.24
  440.9 95.0 %all-gather.4.cloned.1.call-done = bf16[192,4096]{1,0:T(8,128)(2,1)} async-done(((bf16[192,1024]{1,0:T(8,128)(2,1)}), bf16[192,4096]{1,0:T(8,128)(2,1)}) %all-gather.4.cloned.1.call-update) | async-done | bytes 1572880 | tf_op jit(solution)/shard_map/all_gather | solution.py:50
  535.9 0.0 copy-done.6
  535.9 7.6 %fusion.19 = bf16[1,192,1024]{2,1,0:T(8,128)(2,1)} fusion(bf16[192,4096]{1,0:T(8,128)(2,1)} %all-gather.4.cloned.1.call-done, bf16[1,1,1024,4096]{3,2,1,0:T(8,128)(2,1)} %all-gather.6.cloned.1.call-done, bf16[192,1024]{1,0:T(8,128)(2,1)} %all-reduce.2.cloned.1.call-done, bf16[192,1024]{1,0:T(8,128)(2,1)S(1)} %copy-done.2, ...), kind=kOutput, calls=%fused_computation.9 | convolution fusion | flops 1613561856 | bytes 11534528 | tf_op jit(solution)/shard_map/dot_general | solution.py:49
  (1 shorter events, 0.0 us)
Async XLA Ops:
  8.0 1.2 copy-start
  8.0 163.4 %all-gather.6.cloned.1.call-start = ((), (), s32[]{:S(2)}) async-start(), calls=%async_computation.4 | async-start | bytes 8650752 | tf_op jit(solution)/shard_map/all_gather | solution.py:38
  10.0 169.2 %copy-start.1 = (bf16[1,192,1024]{2,1,0:T(8,128)(2,1)S(1)}, bf16[1,192,1024]{2,1,0:T(8,128)(2,1)}, u32[]{:S(2)}) copy-start(bf16[1,192,1024]{2,1,0:T(8,128)(2,1)} %param.11) | copy-start | bytes 1179652
  10.0 425.4 %copy-start.3 = (bf16[1,192,1024]{2,1,0:T(8,128)(2,1)S(1)}, bf16[1,192,1024]{2,1,0:T(8,128)(2,1)}, u32[]{:S(2)}) copy-start(bf16[1,192,1024]{2,1,0:T(8,128)(2,1)} %param.13) | copy-start | bytes 1179652
  10.0 425.4 %copy-start.4 = (bf16[1,192,1024]{2,1,0:T(8,128)(2,1)S(1)}, bf16[1,192,1024]{2,1,0:T(8,128)(2,1)}, u32[]{:S(2)}) copy-start(bf16[1,192,1024]{2,1,0:T(8,128)(2,1)} %param.12) | copy-start | bytes 1179652
  10.0 428.8 %copy-start.5 = (s32[192]{0:T(256)S(1)}, s32[192]{0:T(256)}, u32[]{:S(2)}) copy-start(s32[192]{0:T(256)} %param.17) | copy-start | bytes 2308
  10.0 428.9 %copy-start.2 = (bf16[192,1024]{1,0:T(8,128)(2,1)S(1)}, bf16[192,1024]{1,0:T(8,128)(2,1)}, u32[]{:S(2)}) copy-start(bf16[192,1024]{1,0:T(8,128)(2,1)} %param.16) | copy-start | bytes 1179652
  10.0 525.8 %copy-start.6 = (bf16[1,192,1024]{2,1,0:T(8,128)(2,1)S(1)}, bf16[1,192,1024]{2,1,0:T(8,128)(2,1)}, u32[]{:S(2)}) copy-start(bf16[1,192,1024]{2,1,0:T(8,128)(2,1)} %param.10) | copy-start | bytes 1179652
  10.1 425.4 %reduce-scatter.2.cloned.1.call-start = ((), (), s32[]{:S(2)}) async-start(), calls=%async_computation.1 | async-start | bytes 3932160 | tf_op jit(solution)/shard_map/reduce_scatter | solution.py:40
  178.5 260.4 %all-reduce.2.cloned.1.call-start = ((), (), s32[]{:S(2)}) async-start(), calls=%async_computation.3 | async-start | bytes 786432 | tf_op jit(solution)/shard_map/psum | solution.py:59
  179.1 356.8 %all-gather.4.cloned.1.call-start = ((), (), s32[]{:S(2)}) async-start(), calls=%async_computation.2 | async-start | bytes 1966080 | tf_op jit(solution)/shard_map/all_gather | solution.py:50
Sparse Core Ops, SparseCore 0:
  11.4 159.9 all-gather.5
  178.6 63.0 reduce-scatter.1
  438.3 97.5 all-gather.3
Sparse Core Ops, SparseCore 1:
  181.9 73.7 all-reduce.1
where the time goes:
time: 551 us
  waiting for transfers between devices  257 us (47%)
  blocking collectives  255 us (46%)
  between operations  17.4 us (3%)
  matrix products  14.7 us (3%)
    psum x1, blocking collectives, total_squares(): lax.psum(jnp.sum(jnp.square(grad.astype(jnp.float32))), ('fsdp', 'tp'))  255 us
    all_gather x1, waiting for transfers between devices, on_device(): basis_rows = lax.all_gather(chosen, 'fsdp', axis=1, tiled=True)  161 us
    all_gather x1, waiting for transfers between devices, on_device(): lax.all_gather(direction, 'tp', axis=1, tiled=True)  95 us
  transfers between devices with their start and end apart: 4, of which 2 were waited for; matrix products, arithmetic and copies ran while one was open for 1% of the time, Pallas kernels for 0%

commit v1 on v0

v1 whole, which is shorter than its diff:
```python
import jax
import jax.numpy as jnp
import numpy as np
from jax import lax
from jax.experimental import pallas as pl
from jax.experimental.pallas import tpu as pltpu
from jax.sharding import PartitionSpec as P

K = 4096
N = 6144

beta_first = 0.9
beta_second = 0.95
adam_epsilon = 1e-08
inner_rate = 0.3
outer_rate = 0.7
nesterov = 0.9
clip_ratio = 0.5

ZS = 16
YS = 2
XS = 4
PLANE = YS * XS
BOTH = ("fsdp", "tp")
PLANE_GROUPS = [[(y * ZS + z) * XS + x for y in range(YS) for x in range(XS)] for z in range(ZS)]
Z_GROUPS = [[y * ZS + z for z in range(ZS)] for y in range(YS)]
Y_SWAP = [(f, (f + ZS) % (YS * ZS)) for f in range(YS * ZS)]


def x_shift(s):
    return [(x, (x + s) % XS) for x in range(XS)]


def plane_exchange(value):
    return lax.all_to_all(
        value, BOTH, split_axis=0, concat_axis=0, axis_index_groups=PLANE_GROUPS, tiled=True
    )


def total_squares(grad):
    total = jnp.full((8, 128), jnp.sum(jnp.square(grad.astype(jnp.float32))))
    for bit in (1, 2):
        total = total + lax.ppermute(total, "tp", [(x, x ^ bit) for x in range(XS)])
    for bit in (1, 2, 4, 8, 16):
        total = total + lax.ppermute(total, "fsdp", [(f, f ^ bit) for f in range(YS * ZS)])
    return total[0, 0]


def swap_matrix():
    row = lax.broadcasted_iota(jnp.int32, (1024, 1024), 0)
    col = lax.broadcasted_iota(jnp.int32, (1024, 1024), 1)
    swapped = (col // 16 % 8) * 128 + (col // 128) * 16 + col % 16
    return (row == swapped).astype(jnp.bfloat16)


def core_kernel(where_ref, clip_ref, a0, a1, a2, a3, b_ref, m_ref, rot_ref, upd_ref, dir_ref):
    y = where_ref[0]
    x = where_ref[1]
    clip = clip_ref[0]
    pieces = (a0, a1, a2, a3)
    for u in range(YS):
        row = lax.rem(y + u, YS)
        acc = jnp.zeros((192, 512), jnp.float32)
        for s in range(XS):
            at = pl.multiple_of(lax.rem(x + XS - s, XS) * 1024, 1024)
            acc = acc + lax.dot_general(
                pieces[s][u],
                b_ref[:, pl.ds(at, 1024)],
                (((1,), (1,)), ((), ())),
                preferred_element_type=jnp.float32,
            )
        for t in range(XS):
            rotated = acc[:, t * 128 : (t + 1) * 128]
            rot_ref[row * XS + t] = rotated.astype(jnp.bfloat16)
            scaled = clip * rotated
            first = beta_first * m_ref[row * XS + t, 0].astype(jnp.float32) + (1.0 - beta_first) * scaled
            second = (
                beta_second * m_ref[row * XS + t, 1].astype(jnp.float32)
                + (1.0 - beta_second) * scaled * scaled
            )
            dir_ref[:, t * 128 : (t + 1) * 128] = (
                first / (jnp.sqrt(second) + adam_epsilon)
            ).astype(jnp.bfloat16)
        for t in range(XS):
            upd_ref[row * XS + t] = jnp.dot(
                dir_ref[...], b_ref[:, t * 1024 : (t + 1) * 1024], preferred_element_type=jnp.float32
            ).astype(jnp.bfloat16)


def core(where, clip, pieces, basis, moments):
    vmem = pl.BlockSpec(memory_space=pltpu.VMEM)
    smem = pl.BlockSpec(memory_space=pltpu.SMEM)
    return pl.pallas_call(
        core_kernel,
        out_shape=(
            jax.ShapeDtypeStruct((PLANE, 192, 128), jnp.bfloat16),
            jax.ShapeDtypeStruct((PLANE, 192, 1024), jnp.bfloat16),
        ),
        in_specs=[smem, smem] + [vmem] * 6,
        out_specs=(vmem, vmem),
        scratch_shapes=[pltpu.VMEM((192, 512), jnp.bfloat16)],
        compiler_params=pltpu.CompilerParams(vmem_limit_bytes=48 * 2**20),
        cost_estimate=pl.CostEstimate(
            flops=4 * 384 * 4096 * 512, bytes_accessed=11 * 2**20, transcendentals=384 * 512
        ),
    )(where, clip, *pieces, basis, moments)


def on_device(
    weights,
    grads,
    first_moment,
    second_moment,
    bases,
    outer_delta,
    outer_momentum,
    row_fragment,
    sync_fragment,
    block_map,
):
    chosen = lax.dynamic_index_in_dim(bases[0], block_map[0], 0, keepdims=False)
    mixed = plane_exchange(chosen.T)
    mixed = mixed.reshape(YS, XS, 16, 1024).transpose(0, 2, 1, 3).reshape(YS, 16, K)
    basis = lax.all_gather(mixed, "fsdp", axis=1, axis_index_groups=Z_GROUPS, tiled=True)
    basis = basis.reshape(512, K)
    mixed, grad, first, second, delta = lax.optimization_barrier(
        (mixed, grads[0], first_moment[0], second_moment[0], outer_delta[0])
    )

    y_index = lax.axis_index("fsdp") // ZS
    x_index = lax.axis_index("tp")
    where = jnp.stack([y_index, x_index]).astype(jnp.int32)
    own = jnp.stack([grad, lax.ppermute(grad, "fsdp", Y_SWAP)])
    pieces = [own] + [lax.ppermute(own, "tp", x_shift(s)) for s in range(1, XS)]

    swap = swap_matrix()
    both = jnp.concatenate([first, second], axis=0)
    both = jnp.dot(both, swap, preferred_element_type=jnp.float32).astype(jnp.bfloat16)
    both = both.reshape(2, 192, PLANE, 128).transpose(2, 0, 1, 3)
    moments = plane_exchange(both)

    squares = total_squares(grad)
    limit = clip_ratio * jnp.sqrt(jnp.float32(N * K))
    clip = jnp.minimum(jnp.float32(1.0), limit / jnp.sqrt(squares + 1e-06))

    total = delta.astype(jnp.float32)
    for bit in (1, 2, 3):
        total = total + lax.ppermute(delta, "island", [(i, i ^ bit) for i in range(4)]).astype(jnp.float32)
    delta_mean = total / 4
    momentum = outer_momentum.astype(jnp.float32)
    synced = (row_fragment == sync_fragment[0])[:, None]
    new_momentum = jnp.where(synced, nesterov * momentum + delta_mean, momentum)
    correction = jnp.where(
        synced, outer_rate * (nesterov * new_momentum + delta_mean), jnp.float32(0.0)
    )

    rotated, update = core(where, clip.reshape(1), pieces, basis, moments)
    update = plane_exchange(update)
    rotated = plane_exchange(rotated).transpose(1, 0, 2).reshape(192, 1024)
    rotated = jnp.dot(rotated, swap, preferred_element_type=jnp.float32)
    scaled = clip * rotated
    first_new = beta_first * first.astype(jnp.float32) + (1.0 - beta_first) * scaled
    second_new = beta_second * second.astype(jnp.float32) + (1.0 - beta_second) * scaled * scaled
    update = jnp.sum(update.astype(jnp.float32), axis=0)
    weight_new = weights[0].astype(jnp.float32) - inner_rate * update - correction
    return (
        weight_new.astype(jnp.bfloat16)[None],
        first_new.astype(jnp.bfloat16)[None],
        second_new.astype(jnp.bfloat16)[None],
        new_momentum.astype(jnp.bfloat16),
    )


def solution(mesh):
    in_specs = (
        P("island", "fsdp", "tp"),
        P("island", "fsdp", "tp"),
        P("island", "fsdp", "tp"),
        P("island", "fsdp", "tp"),
        P("island", None, "tp", "fsdp"),
        P("island", "fsdp", "tp"),
        P("fsdp", "tp"),
        P("fsdp"),
        P(),
        P("island"),
    )
    out_specs = (
        P("island", "fsdp", "tp"),
        P("island", "fsdp", "tp"),
        P("island", "fsdp", "tp"),
        P("fsdp", "tp"),
    )
    return jax.shard_map(
        on_device, mesh=mesh, in_specs=in_specs, out_specs=out_specs, check_vma=False
    )
```

time: 551 us -> 221 us (0.40)
  blocking collectives: 255 us -> 22.6 us
  waiting for transfers between devices: 257 us -> 59.7 us
  starting transfers between devices: 0.17 us -> 94 us
  matrix products: 14.7 us -> 4.33 us
  Pallas kernels: 0 us -> 9.51 us
    all_gather x2 -> x1, waiting for transfers between devices: 256 us -> 0.02 us  [on_device(): lax.all_gather(mixed, 'fsdp', axis=1, axis_index_groups=Z_GROUPS, tiled=T...]
    psum x1 -> x0, blocking collectives: 255 us -> none  [total_squares(): lax.psum(jnp.sum(jnp.square(grad.astype(jnp.float32))), ('fsdp', 'tp'))]
    ppermute x0 -> x14, starting transfers between devices: none -> 86 us  [the longest x5 38.1 us: total_squares(): lax.ppermute(total, 'fsdp', [(f, f ^ bit) for f in range(YS * ZS)])]
    ppermute x0 -> x14, waiting for transfers between devices: none -> 59.6 us  [the longest x3 23.7 us: on_device(): lax.ppermute(delta, 'island', [(i, i ^ bit) for i in range(4)])]
    all_to_all x0 -> x2, blocking collectives: none -> 22.6 us  [plane_exchange(): lax.all_to_all(value, BOTH, split_axis=0, concat_axis=0, axis_index_group...]
    dot_general x2, matrix products: 14.7 us -> 4.33 us  [the longest x1 2.23 us: on_device(): jnp.dot(both, swap, preferred_element_type=jnp.float32).astype(jnp.bfloat16)]
    pallas_call x0 -> x1, Pallas kernels: none -> 9.51 us  [core(): pl.pallas_call(core_kernel, out_shape=(jax.ShapeDtypeStruct((PLANE, 192,...]
    all_to_all x0 -> x2, starting transfers between devices: none -> 8 us  [plane_exchange(): lax.all_to_all(value, BOTH, split_axis=0, concat_axis=0, axis_index_group...]
  transfers between devices with their start and end apart: 4 -> 17, of which waited for: 2 -> 10; matrix products, arithmetic and copies ran while one was open for 1% -> 6% of each run, Pallas kernels for 0% -> 0%
where the time goes in v1:
time: 221 us; the launch traced here: 220 us
  starting transfers between devices  94 us (43%)
  waiting for transfers between devices  59.7 us (27%)
  blocking collectives  22.6 us (10%)
  between operations  16.4 us (7%)
  other arithmetic  9.54 us (4%)
  Pallas kernels  9.51 us (4%)
  matrix products  4.33 us (2%)
  local copies, waits for them, and re-layouts  3.76 us (2%)
    ppermute x5, starting transfers between devices, total_squares(): lax.ppermute(total, 'fsdp', [(f, f ^ bit) for f in range(YS * ZS)])  38.1 us
    ppermute x3, starting transfers between devices, on_device(): lax.ppermute(delta, 'island', [(i, i ^ bit) for i in range(4)])  31 us
    ppermute x3, waiting for transfers between devices, on_device(): lax.ppermute(delta, 'island', [(i, i ^ bit) for i in range(4)])  23.7 us
    ppermute x2, waiting for transfers between devices, total_squares(): total = total + lax.ppermute(total, 'tp', [(x, x ^ bit) for x in range(XS)])  23 us
    all_to_all x2, blocking collectives, plane_exchange(): lax.all_to_all(value, BOTH, split_axis=0, concat_axis=0, axis_index_group...  22.6 us
    pallas_call x1, Pallas kernels, core(): pl.pallas_call(core_kernel, out_shape=(jax.ShapeDtypeStruct((PLANE, 192,...  9.51 us
    ppermute x3, starting transfers between devices, on_device(): pieces = [own] + [lax.ppermute(own, 'tp', x_shift(s)) for s in range(1, XS)]  8.1 us
    all_to_all x2, starting transfers between devices, plane_exchange(): lax.all_to_all(value, BOTH, split_axis=0, concat_axis=0, axis_index_group...  8 us
  transfers between devices with their start and end apart: 17, of which 10 were waited for; matrix products, arithmetic and copies ran while one was open for 6% of the time, Pallas kernels for 0%

profile of v1, /device:TPU:1, one launch (start us, length us, event | category | flops | bytes accessed | tf_op | source)
XLA Modules:
  0.0 219.9 jit_solution(15433551796722397550)
XLA Ops:
  7.2 0.0 all-gather.2.cloned.1.call-start
  8.0 0.5 copy-done
  8.4 0.1 copy.17
  8.6 11.8 %all_to_all.24 = bf16[8,16,1024]{2,1,0:T(8,128)(2,1)S(1)} all-to-all(bf16[8,16,1024]{2,1,0:T(8,128)(2,1)S(1)} %bitcast.60), channel_id=1, replica_groups={{0,1,2,3,64,65,66,67},{4,5,6,7,68,69,70,71},{8,9,10,11,72,73,74,75},{12..., dimensions={0} | all-to-all | bytes 524288 | tf_op jit(solution)/shard_map/all_to_all | solution.py:35
  20.4 0.7 copy.21
  21.1 0.0 all-gather.2.cloned.1.call-update
  21.1 2.2 collective-permute-start.7
  23.4 6.5 %collective-permute-done.7 = bf16[192,1024]{1,0:T(8,128)(2,1)S(1)} collective-permute-done((bf16[192,1024]{1,0:T(8,128)(2,1)}, bf16[192,1024]{1,0:T(8,128)(2,1)S(1)}, u32[]{:S(2)}, u32[]{:S(2)}) %collective-permute-start.7) | collective-permute-done | bytes 393248 | tf_op jit(solution)/shard_map/ppermute | solution.py:133
  29.9 1.1 pad_maximum_fusion.a0
  30.9 2.7 %collective-permute-start.10 = (bf16[2,192,1024]{2,1,0:T(8,128)(2,1)S(1)}, bf16[2,192,1024]{2,1,0:T(8,128)(2,1)S(1)}, u32[]{:S(2)}, u32[]{:S(2)}) collective-permute-start(bf16[2,192,1024]{2,1,0:T(8,128)(2,1)S(1)} %pad_maximum_fusion.a0), channel_id=1, source_target_pairs={{0,3},{1,0},{2,1},{3,2},{4,7},{5,4},{6,5},{7,6},{8,11},{9,8},{10,9... | collective-permute-start | bytes 2359304 | tf_op jit(solution)/shard_map/ppermute | solution.py:134
  33.7 2.5 %collective-permute-start.8 = (bf16[2,192,1024]{2,1,0:T(8,128)(2,1)S(1)}, bf16[2,192,1024]{2,1,0:T(8,128)(2,1)}, u32[]{:S(2)}, u32[]{:S(2)}) collective-permute-start(bf16[2,192,1024]{2,1,0:T(8,128)(2,1)S(1)} %pad_maximum_fusion.a0), channel_id=1, source_target_pairs={{0,1},{1,2},{2,3},{3,0},{4,5},{5,6},{6,7},{7,4},{8,9},{9,10},{10,1... | collective-permute-start | bytes 2359304 | tf_op jit(solution)/shard_map/ppermute | solution.py:134
  36.2 2.8 %collective-permute-start.9 = (bf16[2,192,1024]{2,1,0:T(8,128)(2,1)S(1)}, bf16[2,192,1024]{2,1,0:T(8,128)(2,1)}, u32[]{:S(2)}, u32[]{:S(2)}) collective-permute-start(bf16[2,192,1024]{2,1,0:T(8,128)(2,1)S(1)} %pad_maximum_fusion.a0), channel_id=1, source_target_pairs={{0,2},{1,3},{2,0},{3,1},{4,6},{5,7},{6,4},{7,5},{8,10},{9,11},{10,... | collective-permute-start | bytes 2359304 | tf_op jit(solution)/shard_map/ppermute | solution.py:134
  39.1 2.2 %fusion.5 = bf16[48,8,8,128]{3,1,2,0:T(8,128)(2,1)S(1)} fusion(bf16[192,1024]{1,0:T(8,128)(2,1)} %bitcast.68, bf16[192,1024]{1,0:T(8,128)(2,1)} %bitcast.70, s32[1024]{0:T(1024)S(1)} %get-tuple-element.22, s32[1024]{0:T(1024)S(1)} %get-tuple-element.23, s32[1024]{0:T(1024)S(1)} %get-tuple-element.20, s32[1024]{0:T(1024)S(1)} %get-tuple-element.26, ...), kind=kOutput, calls=%fused_computation.12 | convolution fusion | flops 827195392 | bytes 1600512 | tf_op jit(solution)/shard_map/dot_general | solution.py:138
  41.3 0.2 copy.23
  41.5 1.1 copy.31
  42.5 3.5 %all-to-all-start.1 = ((bf16[8,2,192,128]{3,2,1,0:T(8,128)(2,1)}), bf16[8,2,192,128]{3,2,1,0:T(8,128)(2,1)S(1)}, u32[]{:S(2)}, u32[]{:S(2)}) async-start(bf16[8,2,192,128]{3,2,1,0:T(8,128)(2,1)} %bitcast.55), calls=%async_computation.1 | async-start | bytes 1572864 | tf_op jit(solution)/shard_map/all_to_all | solution.py:35
  46.1 1.8 multiply_reduce_fusion
  47.9 0.6 broadcast_in_dim.31
  48.6 3.6 %collective-permute-start = (f32[8,128]{1,0:T(8,128)S(1)}, f32[8,128]{1,0:T(8,128)S(1)}, u32[]{:S(2)}, u32[]{:S(2)}) collective-permute-start(f32[8,128]{1,0:T(8,128)S(1)} %broadcast_in_dim.31), channel_id=1, source_target_pairs={{0,1},{1,0},{2,3},{3,2},{4,5},{5,4},{6,7},{7,6},{8,9},{9,8},{10,11... | collective-permute-start | bytes 12296 | tf_op jit(solution)/shard_map/ppermute | solution.py:43
  52.1 20.1 %collective-permute-done = f32[8,128]{1,0:T(8,128)S(1)} collective-permute-done((f32[8,128]{1,0:T(8,128)S(1)}, f32[8,128]{1,0:T(8,128)S(1)}, u32[]{:S(2)}, u32[]{:S(2)}) %collective-permute-start) | collective-permute-done | bytes 4128 | tf_op jit(solution)/shard_map/ppermute | solution.py:43
  72.3 0.6 broadcast_add_fusion.2
  72.9 3.1 %collective-permute-start.1 = (f32[8,128]{1,0:T(8,128)S(1)}, f32[8,128]{1,0:T(8,128)S(1)}, u32[]{:S(2)}, u32[]{:S(2)}) collective-permute-start(f32[8,128]{1,0:T(8,128)S(1)} %broadcast_add_fusion.2), channel_id=1, source_target_pairs={{0,2},{1,3},{2,0},{3,1},{4,6},{5,7},{6,4},{7,5},{8,10},{9,11},{10,... | collective-permute-start | bytes 12296 | tf_op jit(solution)/shard_map/ppermute | solution.py:43
  76.0 2.9 %collective-permute-done.1 = f32[8,128]{1,0:T(8,128)S(1)} collective-permute-done((f32[8,128]{1,0:T(8,128)S(1)}, f32[8,128]{1,0:T(8,128)S(1)}, u32[]{:S(2)}, u32[]{:S(2)}) %collective-permute-start.1) | collective-permute-done | bytes 4128 | tf_op jit(solution)/shard_map/ppermute | solution.py:43
  78.9 0.6 fusion.35
  79.5 8.7 %collective-permute-start.2 = (f32[8,128]{1,0:T(8,128)S(1)}, f32[8,128]{1,0:T(8,128)S(1)}, u32[]{:S(2)}, u32[]{:S(2)}) collective-permute-start(f32[8,128]{1,0:T(8,128)S(1)} %fusion.35), channel_id=1, source_target_pairs={{0,4},{4,0},{8,12},{12,8},{16,20},{20,16},{24,28},{28,24},{32,36},... | collective-permute-start | bytes 12296 | tf_op jit(solution)/shard_map/ppermute | solution.py:45
  88.3 1.4 collective-permute-done.2
  89.7 4.9 %collective-permute-start.3 = (f32[8,128]{1,0:T(8,128)S(1)}, f32[8,128]{1,0:T(8,128)S(1)}, u32[]{:S(2)}, u32[]{:S(2)}) collective-permute-start(f32[8,128]{1,0:T(8,128)S(1)} %add.83), channel_id=1, source_target_pairs={{0,8},{4,12},{8,0},{12,4},{16,24},{20,28},{24,16},{28,20},{32,40},... | collective-permute-start | bytes 12296 | tf_op jit(solution)/shard_map/ppermute | solution.py:45
  94.6 1.3 collective-permute-done.3
  95.8 8.6 %collective-permute-start.4 = (f32[8,128]{1,0:T(8,128)S(1)}, f32[8,128]{1,0:T(8,128)S(1)}, u32[]{:S(2)}, u32[]{:S(2)}) collective-permute-start(f32[8,128]{1,0:T(8,128)S(1)} %add.84), channel_id=1, source_target_pairs={{0,16},{4,20},{8,24},{12,28},{16,0},{20,4},{24,8},{28,12},{32,48},... | collective-permute-start | bytes 12296 | tf_op jit(solution)/shard_map/ppermute | solution.py:45
  104.4 1.0 collective-permute-done.4
  105.4 13.2 %collective-permute-start.5 = (f32[8,128]{1,0:T(8,128)S(1)}, f32[8,128]{1,0:T(8,128)S(1)}, u32[]{:S(2)}, u32[]{:S(2)}) collective-permute-start(f32[8,128]{1,0:T(8,128)S(1)} %add.85), channel_id=1, source_target_pairs={{0,32},{4,36},{8,40},{12,44},{16,48},{20,52},{24,56},{28,60},{32,0... | collective-permute-start | bytes 12296 | tf_op jit(solution)/shard_map/ppermute | solution.py:45
  118.6 1.0 collective-permute-done.5
  119.6 2.7 %collective-permute-start.6 = (f32[8,128]{1,0:T(8,128)S(1)}, f32[8,128]{1,0:T(8,128)S(1)}, u32[]{:S(2)}, u32[]{:S(2)}) collective-permute-start(f32[8,128]{1,0:T(8,128)S(1)} %add.86), channel_id=1, source_target_pairs={{0,64},{4,68},{8,72},{12,76},{16,80},{20,84},{24,88},{28,92},{32,9... | collective-permute-start | bytes 12296 | tf_op jit(solution)/shard_map/ppermute | solution.py:45
  122.3 0.1 pad_add_fusion.where_ref
  122.3 1.9 collective-permute-done.6
  124.2 0.5 slice.3
  125.5 0.0 all-gather.2.cloned.1.call-done
  125.5 9.5 %shard_map.129 = (bf16[8,192,128]{2,1,0:T(8,128)(2,1)S(1)}, bf16[8,192,1024]{2,1,0:T(8,128)(2,1)}) custom-call(s32[2]{0:T(128)S(1)} %pad_add_fusion.where_ref, f32[1]{0:T(128)} %bitcast.13.clip_ref, bf16[2,192,1024]{2,1,0:T(8,128)(2,1)S(1)} %pad_maximum_fusion.a0, bf16[2,192,1024]{2,1,0:T(8,128)(2,1)} %collective-permute-done.8.a1, ...), custom_call_target="tpu_custom_call" | custom-call | flops 3221225472 | bytes 11534336 | tf_op jit(solution)/shard_map/pallas_call | solution.py:93
  135.0 10.8 %all_to_all.25 = bf16[8,192,128]{2,1,0:T(8,128)(2,1)S(1)} all-to-all(bf16[8,192,128]{2,1,0:T(8,128)(2,1)S(1)} %get-tuple-element.15), channel_id=1, replica_groups={{0,1,2,3,64,65,66,67},{4,5,6,7,68,69,70,71},{8,9,10,11,72,73,74,75},{12..., dimensions={0} | all-to-all | bytes 786432 | tf_op jit(solution)/shard_map/all_to_all | solution.py:35
  145.8 4.5 %all-to-all-start.2 = ((bf16[8,192,1024]{2,1,0:T(8,128)(2,1)}), bf16[8,192,1024]{2,1,0:T(8,128)(2,1)}, u32[]{:S(2)}, u32[]{:S(2)}) async-start(bf16[8,192,1024]{2,1,0:T(8,128)(2,1)} %get-tuple-element.13), calls=%async_computation.2 | async-start | bytes 6291456 | tf_op jit(solution)/shard_map/all_to_all | solution.py:35
  151.0 24.0 %collective-permute-start.11 = (bf16[192,1024]{1,0:T(8,128)(2,1)S(1)}, bf16[192,1024]{1,0:T(8,128)(2,1)S(1)}, u32[]{:S(2)}, u32[]{:S(2)}) collective-permute-start(bf16[192,1024]{1,0:T(8,128)(2,1)S(1)} %bitcast.62), channel_id=1, source_target_pairs={{0,128},{128,0},{256,384},{384,256},{1,129},{129,1},{257,385},{385... | collective-permute-start | bytes 1179656 | tf_op jit(solution)/shard_map/ppermute | solution.py:148
  175.0 4.6 %collective-permute-start.12 = (bf16[192,1024]{1,0:T(8,128)(2,1)S(1)}, bf16[192,1024]{1,0:T(8,128)(2,1)}, u32[]{:S(2)}, u32[]{:S(2)}) collective-permute-start(bf16[192,1024]{1,0:T(8,128)(2,1)S(1)} %bitcast.63), channel_id=1, source_target_pairs={{0,256},{128,384},{256,0},{384,128},{1,257},{129,385},{257,1},{385... | collective-permute-start | bytes 1179656 | tf_op jit(solution)/shard_map/ppermute | solution.py:148
  179.7 2.4 %collective-permute-start.13 = (bf16[192,1024]{1,0:T(8,128)(2,1)S(1)}, bf16[192,1024]{1,0:T(8,128)(2,1)}, u32[]{:S(2)}, u32[]{:S(2)}) collective-permute-start(bf16[192,1024]{1,0:T(8,128)(2,1)S(1)} %bitcast.64), channel_id=1, source_target_pairs={{0,384},{128,256},{256,128},{384,0},{1,385},{129,257},{257,129},{3... | collective-permute-start | bytes 1179656 | tf_op jit(solution)/shard_map/ppermute | solution.py:148
  182.0 2.1 fusion.16
  184.1 2.6 %convert_reduce_fusion = f32[192,1024]{1,0:T(8,128)S(1)} fusion(bf16[8,192,1024]{2,1,0:T(8,128)(2,1)} %all-to-all-done.2), kind=kLoop, calls=%fused_computation.3 | loop fusion | flops 2949120 | bytes 3932160 | tf_op jit(solution)/shard_map/reduce_sum | solution.py:164
  186.8 15.1 %collective-permute-done.12 = bf16[192,1024]{1,0:T(8,128)(2,1)} collective-permute-done((bf16[192,1024]{1,0:T(8,128)(2,1)S(1)}, bf16[192,1024]{1,0:T(8,128)(2,1)}, u32[]{:S(2)}, u32[]{:S(2)}) %collective-permute-start.12) | collective-permute-done | bytes 393248 | tf_op jit(solution)/shard_map/ppermute | solution.py:148
  201.9 8.5 %collective-permute-done.13 = bf16[192,1024]{1,0:T(8,128)(2,1)} collective-permute-done((bf16[192,1024]{1,0:T(8,128)(2,1)S(1)}, bf16[192,1024]{1,0:T(8,128)(2,1)}, u32[]{:S(2)}, u32[]{:S(2)}) %collective-permute-start.13) | collective-permute-done | bytes 393248 | tf_op jit(solution)/shard_map/ppermute | solution.py:148
  210.4 2.6 %fusion.14 = (bf16[192,1024]{1,0:T(8,128)(2,1)}, bf16[1,192,1024]{2,1,0:T(8,128)(2,1)}) fusion(bf16[192,1024]{1,0:T(8,128)(2,1)S(1)} %copy-done.1, pred[192]{0:T(512)(128)(4,1)S(1)} %broadcast_compare_fusion, bf16[192,1024]{1,0:T(8,128)(2,1)} %collective-permute-done.13, bf16[192,1024]{1,0:T(8,128)(2,1)} %collective-permute-done.12, ...), kind=kLoop, calls=%fused_computation.31 | loop fusion | flops 4325376 | bytes 3932352 | tf_op jit(solution)/shard_map/convert_element_type | solution.py:170
  (31 shorter events, 0.1 us)
Async XLA Ops:
  7.2 1.2 copy-start
  7.2 118.3 %all-gather.2.cloned.1.call-start = ((), (), s32[]{:S(2)}) async-start(), calls=%async_computation.4 | async-start | bytes 4456448 | tf_op jit(solution)/shard_map/all_gather | solution.py:124
  21.1 8.7 %collective-permute-start.7 = (bf16[192,1024]{1,0:T(8,128)(2,1)}, bf16[192,1024]{1,0:T(8,128)(2,1)S(1)}, u32[]{:S(2)}, u32[]{:S(2)}) collective-permute-start(bf16[192,1024]{1,0:T(8,128)(2,1)} %bitcast.57), channel_id=1, source_target_pairs={{0,64},{4,68},{8,72},{12,76},{16,80},{20,84},{24,88},{28,92},{32,9... | collective-permute-start | bytes 1179656 | tf_op jit(solution)/shard_map/ppermute | solution.py:133
  30.9 94.5 %collective-permute-start.10 = (bf16[2,192,1024]{2,1,0:T(8,128)(2,1)S(1)}, bf16[2,192,1024]{2,1,0:T(8,128)(2,1)S(1)}, u32[]{:S(2)}, u32[]{:S(2)}) collective-permute-start(bf16[2,192,1024]{2,1,0:T(8,128)(2,1)S(1)} %pad_maximum_fusion.a0), channel_id=1, source_target_pairs={{0,3},{1,0},{2,1},{3,2},{4,7},{5,4},{6,5},{7,6},{8,11},{9,8},{10,9... | collective-permute-start | bytes 2359304 | tf_op jit(solution)/shard_map/ppermute | solution.py:134
  33.7 91.8 %collective-permute-start.8 = (bf16[2,192,1024]{2,1,0:T(8,128)(2,1)S(1)}, bf16[2,192,1024]{2,1,0:T(8,128)(2,1)}, u32[]{:S(2)}, u32[]{:S(2)}) collective-permute-start(bf16[2,192,1024]{2,1,0:T(8,128)(2,1)S(1)} %pad_maximum_fusion.a0), channel_id=1, source_target_pairs={{0,1},{1,2},{2,3},{3,0},{4,5},{5,6},{6,7},{7,4},{8,9},{9,10},{10,1... | collective-permute-start | bytes 2359304 | tf_op jit(solution)/shard_map/ppermute | solution.py:134
  36.2 89.2 %collective-permute-start.9 = (bf16[2,192,1024]{2,1,0:T(8,128)(2,1)S(1)}, bf16[2,192,1024]{2,1,0:T(8,128)(2,1)}, u32[]{:S(2)}, u32[]{:S(2)}) collective-permute-start(bf16[2,192,1024]{2,1,0:T(8,128)(2,1)S(1)} %pad_maximum_fusion.a0), channel_id=1, source_target_pairs={{0,2},{1,3},{2,0},{3,1},{4,6},{5,7},{6,4},{7,5},{8,10},{9,11},{10,... | collective-permute-start | bytes 2359304 | tf_op jit(solution)/shard_map/ppermute | solution.py:134
  42.5 82.9 %all-to-all-start.1 = ((bf16[8,2,192,128]{3,2,1,0:T(8,128)(2,1)}), bf16[8,2,192,128]{3,2,1,0:T(8,128)(2,1)S(1)}, u32[]{:S(2)}, u32[]{:S(2)}) async-start(bf16[8,2,192,128]{3,2,1,0:T(8,128)(2,1)} %bitcast.55), calls=%async_computation.1 | async-start | bytes 1572864 | tf_op jit(solution)/shard_map/all_to_all | solution.py:35
  48.6 23.7 %collective-permute-start = (f32[8,128]{1,0:T(8,128)S(1)}, f32[8,128]{1,0:T(8,128)S(1)}, u32[]{:S(2)}, u32[]{:S(2)}) collective-permute-start(f32[8,128]{1,0:T(8,128)S(1)} %broadcast_in_dim.31), channel_id=1, source_target_pairs={{0,1},{1,0},{2,3},{3,2},{4,5},{5,4},{6,7},{7,6},{8,9},{9,8},{10,11... | collective-permute-start | bytes 12296 | tf_op jit(solution)/shard_map/ppermute | solution.py:43
  72.9 6.0 %collective-permute-start.1 = (f32[8,128]{1,0:T(8,128)S(1)}, f32[8,128]{1,0:T(8,128)S(1)}, u32[]{:S(2)}, u32[]{:S(2)}) collective-permute-start(f32[8,128]{1,0:T(8,128)S(1)} %broadcast_add_fusion.2), channel_id=1, source_target_pairs={{0,2},{1,3},{2,0},{3,1},{4,6},{5,7},{6,4},{7,5},{8,10},{9,11},{10,... | collective-permute-start | bytes 12296 | tf_op jit(solution)/shard_map/ppermute | solution.py:43
  79.5 10.1 %collective-permute-start.2 = (f32[8,128]{1,0:T(8,128)S(1)}, f32[8,128]{1,0:T(8,128)S(1)}, u32[]{:S(2)}, u32[]{:S(2)}) collective-permute-start(f32[8,128]{1,0:T(8,128)S(1)} %fusion.35), channel_id=1, source_target_pairs={{0,4},{4,0},{8,12},{12,8},{16,20},{20,16},{24,28},{28,24},{32,36},... | collective-permute-start | bytes 12296 | tf_op jit(solution)/shard_map/ppermute | solution.py:45
  89.7 6.2 %collective-permute-start.3 = (f32[8,128]{1,0:T(8,128)S(1)}, f32[8,128]{1,0:T(8,128)S(1)}, u32[]{:S(2)}, u32[]{:S(2)}) collective-permute-start(f32[8,128]{1,0:T(8,128)S(1)} %add.83), channel_id=1, source_target_pairs={{0,8},{4,12},{8,0},{12,4},{16,24},{20,28},{24,16},{28,20},{32,40},... | collective-permute-start | bytes 12296 | tf_op jit(solution)/shard_map/ppermute | solution.py:45
  95.8 9.6 %collective-permute-start.4 = (f32[8,128]{1,0:T(8,128)S(1)}, f32[8,128]{1,0:T(8,128)S(1)}, u32[]{:S(2)}, u32[]{:S(2)}) collective-permute-start(f32[8,128]{1,0:T(8,128)S(1)} %add.84), channel_id=1, source_target_pairs={{0,16},{4,20},{8,24},{12,28},{16,0},{20,4},{24,8},{28,12},{32,48},... | collective-permute-start | bytes 12296 | tf_op jit(solution)/shard_map/ppermute | solution.py:45
  105.4 14.2 %collective-permute-start.5 = (f32[8,128]{1,0:T(8,128)S(1)}, f32[8,128]{1,0:T(8,128)S(1)}, u32[]{:S(2)}, u32[]{:S(2)}) collective-permute-start(f32[8,128]{1,0:T(8,128)S(1)} %add.85), channel_id=1, source_target_pairs={{0,32},{4,36},{8,40},{12,44},{16,48},{20,52},{24,56},{28,60},{32,0... | collective-permute-start | bytes 12296 | tf_op jit(solution)/shard_map/ppermute | solution.py:45
  119.6 4.6 %collective-permute-start.6 = (f32[8,128]{1,0:T(8,128)S(1)}, f32[8,128]{1,0:T(8,128)S(1)}, u32[]{:S(2)}, u32[]{:S(2)}) collective-permute-start(f32[8,128]{1,0:T(8,128)S(1)} %add.86), channel_id=1, source_target_pairs={{0,64},{4,68},{8,72},{12,76},{16,80},{20,84},{24,88},{28,92},{32,9... | collective-permute-start | bytes 12296 | tf_op jit(solution)/shard_map/ppermute | solution.py:45
  135.0 15.9 %copy-start.4 = (s32[192]{0:T(256)S(1)}, s32[192]{0:T(256)}, u32[]{:S(2)}) copy-start(s32[192]{0:T(256)} %param.17) | copy-start | bytes 2308
  135.0 16.0 %copy-start.2 = (bf16[1,192,1024]{2,1,0:T(8,128)(2,1)S(1)}, bf16[1,192,1024]{2,1,0:T(8,128)(2,1)}, u32[]{:S(2)}) copy-start(bf16[1,192,1024]{2,1,0:T(8,128)(2,1)} %param.15) | copy-start | bytes 1179652
  135.0 47.0 %copy-start.5 = (bf16[1,192,1024]{2,1,0:T(8,128)(2,1)S(1)}, bf16[1,192,1024]{2,1,0:T(8,128)(2,1)}, u32[]{:S(2)}) copy-start(bf16[1,192,1024]{2,1,0:T(8,128)(2,1)} %param.13) | copy-start | bytes 1179652
  135.0 47.0 %copy-start.6 = (bf16[1,192,1024]{2,1,0:T(8,128)(2,1)S(1)}, bf16[1,192,1024]{2,1,0:T(8,128)(2,1)}, u32[]{:S(2)}) copy-start(bf16[1,192,1024]{2,1,0:T(8,128)(2,1)} %param.12) | copy-start | bytes 1179652
  145.8 38.3 %all-to-all-start.2 = ((bf16[8,192,1024]{2,1,0:T(8,128)(2,1)}), bf16[8,192,1024]{2,1,0:T(8,128)(2,1)}, u32[]{:S(2)}, u32[]{:S(2)}) async-start(bf16[8,192,1024]{2,1,0:T(8,128)(2,1)} %get-tuple-element.13), calls=%async_computation.2 | async-start | bytes 6291456 | tf_op jit(solution)/shard_map/all_to_all | solution.py:35
  151.0 35.8 %collective-permute-start.11 = (bf16[192,1024]{1,0:T(8,128)(2,1)S(1)}, bf16[192,1024]{1,0:T(8,128)(2,1)S(1)}, u32[]{:S(2)}, u32[]{:S(2)}) collective-permute-start(bf16[192,1024]{1,0:T(8,128)(2,1)S(1)} %bitcast.62), channel_id=1, source_target_pairs={{0,128},{128,0},{256,384},{384,256},{1,129},{129,1},{257,385},{385... | collective-permute-start | bytes 1179656 | tf_op jit(solution)/shard_map/ppermute | solution.py:148
  175.0 26.9 %collective-permute-start.12 = (bf16[192,1024]{1,0:T(8,128)(2,1)S(1)}, bf16[192,1024]{1,0:T(8,128)(2,1)}, u32[]{:S(2)}, u32[]{:S(2)}) collective-permute-start(bf16[192,1024]{1,0:T(8,128)(2,1)S(1)} %bitcast.63), channel_id=1, source_target_pairs={{0,256},{128,384},{256,0},{384,128},{1,257},{129,385},{257,1},{385... | collective-permute-start | bytes 1179656 | tf_op jit(solution)/shard_map/ppermute | solution.py:148
  179.7 30.8 %collective-permute-start.13 = (bf16[192,1024]{1,0:T(8,128)(2,1)S(1)}, bf16[192,1024]{1,0:T(8,128)(2,1)}, u32[]{:S(2)}, u32[]{:S(2)}) collective-permute-start(bf16[192,1024]{1,0:T(8,128)(2,1)S(1)} %bitcast.64), channel_id=1, source_target_pairs={{0,384},{128,256},{256,128},{384,0},{1,385},{129,257},{257,129},{3... | collective-permute-start | bytes 1179656 | tf_op jit(solution)/shard_map/ppermute | solution.py:148
  184.1 26.3 %copy-start.1 = (bf16[192,1024]{1,0:T(8,128)(2,1)S(1)}, bf16[192,1024]{1,0:T(8,128)(2,1)}, u32[]{:S(2)}) copy-start(bf16[192,1024]{1,0:T(8,128)(2,1)} %param.16) | copy-start | bytes 1179652
  184.1 26.3 %copy-start.3 = (bf16[1,192,1024]{2,1,0:T(8,128)(2,1)S(1)}, bf16[1,192,1024]{2,1,0:T(8,128)(2,1)}, u32[]{:S(2)}) copy-start(bf16[1,192,1024]{2,1,0:T(8,128)(2,1)} %param.10) | copy-start | bytes 1179652
Sparse Core Ops, SparseCore 0:
  21.2 74.1 all-gather.1

commit v2 on v1

v2 whole, which is shorter than its diff:
```python
import jax
import jax.numpy as jnp
import numpy as np
from jax import lax
from jax.experimental import pallas as pl
from jax.experimental.pallas import tpu as pltpu
from jax.sharding import PartitionSpec as P

K = 4096
N = 6144

beta_first = 0.9
beta_second = 0.95
adam_epsilon = 1e-08
inner_rate = 0.3
outer_rate = 0.7
nesterov = 0.9
clip_ratio = 0.5

ZS = 16
YS = 2
XS = 4
PLANE = YS * XS
BOTH = ("fsdp", "tp")
PLANE_GROUPS = [[(y * ZS + z) * XS + x for y in range(YS) for x in range(XS)] for z in range(ZS)]
Z_GROUPS = [[y * ZS + z for z in range(ZS)] for y in range(YS)]
Y_SWAP = [(f, (f + ZS) % (YS * ZS)) for f in range(YS * ZS)]


def x_shift(s):
    return [(x, (x + s) % XS) for x in range(XS)]


def plane_exchange(value):
    return lax.all_to_all(
        value, BOTH, split_axis=0, concat_axis=0, axis_index_groups=PLANE_GROUPS, tiled=True
    )


def ring_squares(grad):
    total = jnp.full((8, 128), jnp.sum(jnp.square(grad.astype(jnp.float32))))
    for bit in (1, 2, 4, 8):
        total = total + lax.ppermute(total, "fsdp", [(f, f ^ bit) for f in range(YS * ZS)])
    return total[0:1, 0:1]


def three_pieces(value):
    high = lax.reduce_precision(value, 8, 7)
    middle = lax.reduce_precision(value - high, 8, 7)
    low = lax.reduce_precision(value - high - middle, 8, 7)
    rows = jnp.concatenate([high, middle, low, jnp.zeros((13, 1), jnp.float32)], axis=0)
    return jnp.broadcast_to(rows.astype(jnp.bfloat16), (PLANE, 16, 128))


def swap_matrix():
    row = lax.broadcasted_iota(jnp.int32, (1024, 1024), 0)
    col = lax.broadcasted_iota(jnp.int32, (1024, 1024), 1)
    swapped = (col // 16 % 8) * 128 + (col // 128) * 16 + col % 16
    return (row == swapped).astype(jnp.bfloat16)


def core_kernel(where_ref, clip_ref, a0, a1, a2, a3, b_ref, m_ref, out_ref, dir_ref):
    y = where_ref[0]
    x = where_ref[1]
    clip = clip_ref[0]
    acc = jnp.zeros((384, 512), jnp.float32)
    for s, piece in enumerate((a0, a1, a2, a3)):
        at = pl.multiple_of(lax.rem(x + XS - s, XS) * 1024, 1024)
        acc = acc + lax.dot_general(
            piece[...].reshape(384, 1024),
            b_ref[:, pl.ds(at, 1024)],
            (((1,), (1,)), ((), ())),
            preferred_element_type=jnp.float32,
        )
    for u in range(YS):
        row = lax.rem(y + u, YS)
        for t in range(XS):
            rotated = acc[u * 192 : (u + 1) * 192, t * 128 : (t + 1) * 128]
            out_ref[row * XS + t, :, 1024:1152] = rotated.astype(jnp.bfloat16)
            scaled = clip * rotated
            first = m_ref[row * XS + t, 0:192].astype(jnp.float32)
            second = m_ref[row * XS + t, 192:384].astype(jnp.float32)
            first = beta_first * first + (1.0 - beta_first) * scaled
            second = beta_second * second + (1.0 - beta_second) * scaled * scaled
            dir_ref[u * 192 : (u + 1) * 192, t * 128 : (t + 1) * 128] = (
                first / (jnp.sqrt(second) + adam_epsilon)
            ).astype(jnp.bfloat16)
    for t in range(XS):
        update = jnp.dot(
            dir_ref[...], b_ref[:, t * 1024 : (t + 1) * 1024], preferred_element_type=jnp.float32
        ).astype(jnp.bfloat16)
        for u in range(YS):
            out_ref[lax.rem(y + u, YS) * XS + t, :, 0:1024] = update[u * 192 : (u + 1) * 192]


def core(where, clip, pieces, basis, moments):
    vmem = pl.BlockSpec(memory_space=pltpu.VMEM)
    smem = pl.BlockSpec(memory_space=pltpu.SMEM)
    return pl.pallas_call(
        core_kernel,
        out_shape=jax.ShapeDtypeStruct((PLANE, 192, 1152), jnp.bfloat16),
        in_specs=[smem, smem] + [vmem] * 6,
        out_specs=vmem,
        scratch_shapes=[pltpu.VMEM((384, 512), jnp.bfloat16)],
        compiler_params=pltpu.CompilerParams(vmem_limit_bytes=48 * 2**20),
        cost_estimate=pl.CostEstimate(
            flops=4 * 384 * 4096 * 512, bytes_accessed=11 * 2**20, transcendentals=384 * 512
        ),
    )(where, clip, *pieces, basis, moments)


def on_device(
    weights,
    grads,
    first_moment,
    second_moment,
    bases,
    outer_delta,
    outer_momentum,
    row_fragment,
    sync_fragment,
    block_map,
):
    chosen = lax.dynamic_index_in_dim(bases[0], block_map[0], 0, keepdims=False)
    mixed = plane_exchange(chosen.T)
    mixed = mixed.reshape(YS, XS, 16, 1024).transpose(0, 2, 1, 3).reshape(YS, 16, K)
    basis = lax.all_gather(mixed, "fsdp", axis=1, axis_index_groups=Z_GROUPS, tiled=True)
    basis = basis.reshape(512, K)
    mixed, grad = lax.optimization_barrier((mixed, grads[0]))

    y_index = lax.axis_index("fsdp") // ZS
    x_index = lax.axis_index("tp")
    where = jnp.stack([y_index, x_index]).astype(jnp.int32)
    own = jnp.stack([grad, lax.ppermute(grad, "fsdp", Y_SWAP)])
    pieces = [own] + [lax.ppermute(own, "tp", x_shift(s)) for s in range(1, XS)]

    squares = ring_squares(grad)
    squares, first, second, delta = lax.optimization_barrier(
        (squares, first_moment[0], second_moment[0], outer_delta[0])
    )
    swap = swap_matrix()
    both = jnp.concatenate([first, second], axis=0)
    both = jnp.dot(both, swap, preferred_element_type=jnp.float32).astype(jnp.bfloat16)
    both = both.reshape(384, PLANE, 128).transpose(1, 0, 2)
    moments = plane_exchange(jnp.concatenate([both, three_pieces(squares)], axis=1))
    squares = jnp.sum(moments[:, 384:387, 0].astype(jnp.float32))
    limit = clip_ratio * jnp.sqrt(jnp.float32(N * K))
    clip = jnp.minimum(jnp.float32(1.0), limit / jnp.sqrt(squares + 1e-06))

    total = delta.astype(jnp.float32)
    for bit in (1, 2, 3):
        total = total + lax.ppermute(delta, "island", [(i, i ^ bit) for i in range(4)]).astype(jnp.float32)
    delta_mean = total / 4
    momentum = outer_momentum.astype(jnp.float32)
    synced = (row_fragment == sync_fragment[0])[:, None]
    new_momentum = jnp.where(synced, nesterov * momentum + delta_mean, momentum)
    correction = jnp.where(
        synced, outer_rate * (nesterov * new_momentum + delta_mean), jnp.float32(0.0)
    )
    new_momentum = new_momentum.astype(jnp.bfloat16)
    kept = weights[0].astype(jnp.float32) - correction
    kept, new_momentum, moments = lax.optimization_barrier((kept, new_momentum, moments))

    mine = plane_exchange(core(where, clip.reshape(1), pieces, basis, moments))
    rotated = mine[:, :, 1024:].transpose(1, 0, 2).reshape(192, 1024)
    rotated = jnp.dot(rotated, swap, preferred_element_type=jnp.float32)
    scaled = clip * rotated
    first_new = beta_first * first.astype(jnp.float32) + (1.0 - beta_first) * scaled
    second_new = beta_second * second.astype(jnp.float32) + (1.0 - beta_second) * scaled * scaled
    update = jnp.sum(mine[:, :, :1024].astype(jnp.float32), axis=0)
    weight_new = kept - inner_rate * update
    return (
        weight_new.astype(jnp.bfloat16)[None],
        first_new.astype(jnp.bfloat16)[None],
        second_new.astype(jnp.bfloat16)[None],
        new_momentum,
    )


def solution(mesh):
    in_specs = (
        P("island", "fsdp", "tp"),
        P("island", "fsdp", "tp"),
        P("island", "fsdp", "tp"),
        P("island", "fsdp", "tp"),
        P("island", None, "tp", "fsdp"),
        P("island", "fsdp", "tp"),
        P("fsdp", "tp"),
        P("fsdp"),
        P(),
        P("island"),
    )
    out_specs = (
        P("island", "fsdp", "tp"),
        P("island", "fsdp", "tp"),
        P("island", "fsdp", "tp"),
        P("fsdp", "tp"),
    )
    return jax.shard_map(
        on_device, mesh=mesh, in_specs=in_specs, out_specs=out_specs, check_vma=False
    )
```

time: 221 us -> 201 us (0.910)
  blocking collectives: 22.6 us -> 56.8 us
  starting transfers between devices: 94 us -> 60.3 us
  waiting for transfers between devices: 59.7 us -> 34.2 us
  between operations: 16.4 us -> 21.9 us
    all_to_all x2, blocking collectives: 22.6 us -> 56.8 us  [plane_exchange(): lax.all_to_all(value, BOTH, split_axis=0, concat_axis=0, axis_index_group...]
    ppermute x3, waiting for transfers between devices: 0.01 us -> 31.2 us  [on_device(): pieces = [own] + [lax.ppermute(own, 'tp', x_shift(s)) for s in range(1, XS)]]
    ppermute x7 -> x4, waiting for transfers between devices: 29.5 us -> 3.02 us  [ring_squares(): lax.ppermute(total, 'fsdp', [(f, f ^ bit) for f in range(YS * ZS)])]
    ppermute x3, waiting for transfers between devices: 23.7 us -> 0.01 us  [on_device(): lax.ppermute(delta, 'island', [(i, i ^ bit) for i in range(4)])]
    ppermute x3, starting transfers between devices: 31 us -> 14.6 us  [on_device(): lax.ppermute(delta, 'island', [(i, i ^ bit) for i in range(4)])]
    ppermute x7 -> x4, starting transfers between devices: 44.7 us -> 30.5 us  [ring_squares(): lax.ppermute(total, 'fsdp', [(f, f ^ bit) for f in range(YS * ZS)])]
    ppermute x1, waiting for transfers between devices: 6.49 us -> 0.01 us  [on_device(): own = jnp.stack([grad, lax.ppermute(grad, 'fsdp', Y_SWAP)])]
    all_to_all x2 -> x1, starting transfers between devices: 8 us -> 3.55 us  [plane_exchange(): lax.all_to_all(value, BOTH, split_axis=0, concat_axis=0, axis_index_group...]
  transfers between devices with their start and end apart: 17 -> 13, of which waited for: 10 -> 6; matrix products, arithmetic and copies ran while one was open for 6% -> 7% of each run, Pallas kernels for 0% -> 0%
where the time goes in v2:
time: 201 us; the launch traced here: 200 us
  starting transfers between devices  60.3 us (30%)
  blocking collectives  56.8 us (28%)
  waiting for transfers between devices  34.2 us (17%)
  between operations  21.9 us (11%)
  other arithmetic  10.4 us (5%)
  Pallas kernels  8.43 us (4%)
  matrix products  4.31 us (2%)
  local copies, waits for them, and re-layouts  3.27 us (2%)
    all_to_all x2, blocking collectives, plane_exchange(): lax.all_to_all(value, BOTH, split_axis=0, concat_axis=0, axis_index_group...  56.8 us
    ppermute x3, waiting for transfers between devices, on_device(): pieces = [own] + [lax.ppermute(own, 'tp', x_shift(s)) for s in range(1, XS)]  31.2 us
    ppermute x4, starting transfers between devices, ring_squares(): lax.ppermute(total, 'fsdp', [(f, f ^ bit) for f in range(YS * ZS)])  30.5 us
    ppermute x3, starting transfers between devices, on_device(): lax.ppermute(delta, 'island', [(i, i ^ bit) for i in range(4)])  14.6 us
    ppermute x3, starting transfers between devices, on_device(): pieces = [own] + [lax.ppermute(own, 'tp', x_shift(s)) for s in range(1, XS)]  9.45 us
    pallas_call x1, Pallas kernels, core(): pl.pallas_call(core_kernel, out_shape=jax.ShapeDtypeStruct((PLANE, 192, 1...  8.43 us
  transfers between devices with their start and end apart: 13, of which 6 were waited for; matrix products, arithmetic and copies ran while one was open for 7% of the time, Pallas kernels for 0%

profile of v2, /device:TPU:1, one launch (start us, length us, event | category | flops | bytes accessed | tf_op | source)
XLA Modules:
  0.0 199.5 jit_solution(5408244202552942626)
XLA Ops:
  7.2 0.0 copy-start
  7.2 0.0 all-gather.2.cloned.1.call-start
  8.0 0.5 copy-done
  8.4 0.1 copy.18
  8.6 11.8 %all_to_all.19 = bf16[8,16,1024]{2,1,0:T(8,128)(2,1)S(1)} all-to-all(bf16[8,16,1024]{2,1,0:T(8,128)(2,1)S(1)} %bitcast.55), channel_id=1, replica_groups={{0,1,2,3,64,65,66,67},{4,5,6,7,68,69,70,71},{8,9,10,11,72,73,74,75},{12..., dimensions={0} | all-to-all | bytes 524288 | tf_op jit(solution)/shard_map/all_to_all | solution.py:35
  20.4 0.7 copy.23
  21.1 0.0 all-gather.2.cloned.1.call-update
  21.1 1.8 multiply_reduce_fusion
  22.9 0.6 broadcast_in_dim.37
  23.6 3.7 %collective-permute-start = (f32[8,128]{1,0:T(8,128)S(1)}, f32[8,128]{1,0:T(8,128)S(1)}, u32[]{:S(2)}, u32[]{:S(2)}) collective-permute-start(f32[8,128]{1,0:T(8,128)S(1)} %broadcast_in_dim.37), channel_id=1, source_target_pairs={{0,4},{4,0},{8,12},{12,8},{16,20},{20,16},{24,28},{28,24},{32,36},... | collective-permute-start | bytes 12296 | tf_op jit(solution)/shard_map/ppermute | solution.py:43
  27.3 1.0 collective-permute-done
  28.3 0.6 broadcast_add_fusion.2
  28.9 4.9 %collective-permute-start.1 = (f32[8,128]{1,0:T(8,128)S(1)}, f32[8,128]{1,0:T(8,128)S(1)}, u32[]{:S(2)}, u32[]{:S(2)}) collective-permute-start(f32[8,128]{1,0:T(8,128)S(1)} %broadcast_add_fusion.2), channel_id=1, source_target_pairs={{0,8},{4,12},{8,0},{12,4},{16,24},{20,28},{24,16},{28,20},{32,40},... | collective-permute-start | bytes 12296 | tf_op jit(solution)/shard_map/ppermute | solution.py:43
  33.9 1.0 collective-permute-done.1
  34.8 0.6 fusion.32
  35.5 8.8 %collective-permute-start.2 = (f32[8,128]{1,0:T(8,128)S(1)}, f32[8,128]{1,0:T(8,128)S(1)}, u32[]{:S(2)}, u32[]{:S(2)}) collective-permute-start(f32[8,128]{1,0:T(8,128)S(1)} %fusion.32), channel_id=1, source_target_pairs={{0,16},{4,20},{8,24},{12,28},{16,0},{20,4},{24,8},{28,12},{32,48},... | collective-permute-start | bytes 12296 | tf_op jit(solution)/shard_map/ppermute | solution.py:43
  44.3 1.1 collective-permute-done.2
  45.4 13.1 %collective-permute-start.3 = (f32[8,128]{1,0:T(8,128)S(1)}, f32[8,128]{1,0:T(8,128)S(1)}, u32[]{:S(2)}, u32[]{:S(2)}) collective-permute-start(f32[8,128]{1,0:T(8,128)S(1)} %add.73), channel_id=1, source_target_pairs={{0,32},{4,36},{8,40},{12,44},{16,48},{20,52},{24,56},{28,60},{32,0... | collective-permute-start | bytes 12296 | tf_op jit(solution)/shard_map/ppermute | solution.py:43
  58.5 2.2 %collective-permute-start.7 = (bf16[192,1024]{1,0:T(8,128)(2,1)}, bf16[192,1024]{1,0:T(8,128)(2,1)S(1)}, u32[]{:S(2)}, u32[]{:S(2)}) collective-permute-start(bf16[192,1024]{1,0:T(8,128)(2,1)} %bitcast.53), channel_id=1, source_target_pairs={{0,64},{4,68},{8,72},{12,76},{16,80},{20,84},{24,88},{28,92},{32,9... | collective-permute-start | bytes 1179656 | tf_op jit(solution)/shard_map/ppermute | solution.py:134
  60.7 0.0 collective-permute-done.3
  60.7 0.5 slice.12
  61.2 10.4 %collective-permute-start.6 = (bf16[192,1024]{1,0:T(8,128)(2,1)}, bf16[192,1024]{1,0:T(8,128)(2,1)}, u32[]{:S(2)}, u32[]{:S(2)}) collective-permute-start(bf16[192,1024]{1,0:T(8,128)(2,1)} %bitcast.58), channel_id=1, source_target_pairs={{0,384},{128,256},{256,128},{384,0},{1,385},{129,257},{257,129},{3... | collective-permute-start | bytes 1179656 | tf_op jit(solution)/shard_map/ppermute | solution.py:152
  71.6 2.2 %collective-permute-start.5 = (bf16[192,1024]{1,0:T(8,128)(2,1)}, bf16[192,1024]{1,0:T(8,128)(2,1)}, u32[]{:S(2)}, u32[]{:S(2)}) collective-permute-start(bf16[192,1024]{1,0:T(8,128)(2,1)} %bitcast.59), channel_id=1, source_target_pairs={{0,256},{128,384},{256,0},{384,128},{1,257},{129,385},{257,1},{385... | collective-permute-start | bytes 1179656 | tf_op jit(solution)/shard_map/ppermute | solution.py:152
  73.8 2.0 %collective-permute-start.4 = (bf16[192,1024]{1,0:T(8,128)(2,1)}, bf16[192,1024]{1,0:T(8,128)(2,1)}, u32[]{:S(2)}, u32[]{:S(2)}) collective-permute-start(bf16[192,1024]{1,0:T(8,128)(2,1)} %bitcast.60), channel_id=1, source_target_pairs={{0,128},{128,0},{256,384},{384,256},{1,129},{129,1},{257,385},{385... | collective-permute-start | bytes 1179656 | tf_op jit(solution)/shard_map/ppermute | solution.py:152
  75.8 2.2 %convolution_convert_fusion = bf16[384,1024]{1,0:T(8,128)(2,1)S(1)} fusion(bf16[192,1024]{1,0:T(8,128)(2,1)} %bitcast.63, bf16[192,1024]{1,0:T(8,128)(2,1)} %bitcast.65, s32[1024]{0:T(1024)S(1)} %get-tuple-element.26, s32[1024]{0:T(1024)S(1)} %get-tuple-element.27, s32[1024]{0:T(1024)S(1)} %get-tuple-element.24, s32[1024]{0:T(1024)S(1)} %get-tuple-element.30, ...), kind=kOutput, calls=%fused_computation.11 | convolution fusion | flops 827195392 | bytes 1600512 | tf_op jit(solution)/shard_map/dot_general | solution.py:143
  78.1 0.0 copy-start.2
  78.1 0.0 copy-start.3
  83.6 0.7 pad_maximum_fusion.2
  84.3 0.4 copy.20
  84.7 0.4 copy.21
  85.0 1.1 pad_maximum_fusion
  86.2 3.5 %all-to-all-start.1 = ((bf16[8,400,128]{2,1,0:T(8,128)(2,1)}), bf16[8,400,128]{2,1,0:T(8,128)(2,1)S(1)}, u32[]{:S(2)}, u32[]{:S(2)}) async-start(bf16[8,400,128]{2,1,0:T(8,128)(2,1)} %pad_maximum_fusion), calls=%async_computation.1 | async-start | bytes 1638400 | tf_op jit(solution)/shard_map/all_to_all | solution.py:35
  89.7 0.1 pad_maximum_fusion.1.a0
  89.8 4.5 %collective-permute-start.10 = (bf16[2,192,1024]{2,1,0:T(8,128)(2,1)S(1)}, bf16[2,192,1024]{2,1,0:T(8,128)(2,1)S(1)}, u32[]{:S(2)}, u32[]{:S(2)}) collective-permute-start(bf16[2,192,1024]{2,1,0:T(8,128)(2,1)S(1)} %pad_maximum_fusion.1.a0), channel_id=1, source_target_pairs={{0,3},{1,0},{2,1},{3,2},{4,7},{5,4},{6,5},{7,6},{8,11},{9,8},{10,9... | collective-permute-start | bytes 2359304 | tf_op jit(solution)/shard_map/ppermute | solution.py:135
  94.3 2.5 %collective-permute-start.9 = (bf16[2,192,1024]{2,1,0:T(8,128)(2,1)S(1)}, bf16[2,192,1024]{2,1,0:T(8,128)(2,1)}, u32[]{:S(2)}, u32[]{:S(2)}) collective-permute-start(bf16[2,192,1024]{2,1,0:T(8,128)(2,1)S(1)} %pad_maximum_fusion.1.a0), channel_id=1, source_target_pairs={{0,2},{1,3},{2,0},{3,1},{4,6},{5,7},{6,4},{7,5},{8,10},{9,11},{10,... | collective-permute-start | bytes 2359304 | tf_op jit(solution)/shard_map/ppermute | solution.py:135
  96.8 0.0 collective-permute-done.6
  96.8 2.5 %collective-permute-start.8 = (bf16[2,192,1024]{2,1,0:T(8,128)(2,1)S(1)}, bf16[2,192,1024]{2,1,0:T(8,128)(2,1)}, u32[]{:S(2)}, u32[]{:S(2)}) collective-permute-start(bf16[2,192,1024]{2,1,0:T(8,128)(2,1)S(1)} %pad_maximum_fusion.1.a0), channel_id=1, source_target_pairs={{0,1},{1,2},{2,3},{3,0},{4,5},{5,6},{6,7},{7,4},{8,9},{9,10},{10,1... | collective-permute-start | bytes 2359304 | tf_op jit(solution)/shard_map/ppermute | solution.py:135
  100.0 0.1 pad_add_fusion.where_ref
  100.1 3.3 %fusion.11 = (bf16[192,1024]{1,0:T(8,128)(2,1)}, f32[192,1024]{1,0:T(8,128)}) fusion(bf16[192,1024]{1,0:T(8,128)(2,1)} %param.16, pred[192]{0:T(512)(128)(4,1)S(1)} %broadcast_compare_fusion, bf16[192,1024]{1,0:T(8,128)(2,1)} %collective-permute-done.6, bf16[192,1024]{1,0:T(8,128)(2,1)} %collective-permute-done.5, ...), kind=kLoop, calls=%fused_computation.29 | loop fusion | flops 3735552 | bytes 3539136 | tf_op jit(solution)/shard_map/convert_element_type | solution.py:160
  103.4 0.6 convert_reduce_fusion.1
  104.7 12.8 %collective-permute-done.10.a3 = bf16[2,192,1024]{2,1,0:T(8,128)(2,1)S(1)} collective-permute-done((bf16[2,192,1024]{2,1,0:T(8,128)(2,1)S(1)}, bf16[2,192,1024]{2,1,0:T(8,128)(2,1)S(1)}, u32[]{:S(2)}, u32[]{:S(2)}) %collective-permute-start.10) | collective-permute-done | bytes 786464 | tf_op jit(solution)/shard_map/ppermute | solution.py:135
  117.5 1.6 collective-permute-done.9.a2
  119.0 16.8 %collective-permute-done.8.a1 = bf16[2,192,1024]{2,1,0:T(8,128)(2,1)} collective-permute-done((bf16[2,192,1024]{2,1,0:T(8,128)(2,1)S(1)}, bf16[2,192,1024]{2,1,0:T(8,128)(2,1)}, u32[]{:S(2)}, u32[]{:S(2)}) %collective-permute-start.8) | collective-permute-done | bytes 786464 | tf_op jit(solution)/shard_map/ppermute | solution.py:135
  135.8 8.4 %shard_map.129 = bf16[8,192,1152]{2,1,0:T(8,128)(2,1)} custom-call(s32[2]{0:T(128)S(1)} %pad_add_fusion.where_ref, f32[1]{0:T(128)} %bitcast.19.clip_ref, bf16[2,192,1024]{2,1,0:T(8,128)(2,1)S(1)} %pad_maximum_fusion.1.a0, bf16[2,192,1024]{2,1,0:T(8,128)(2,1)} %collective-permute-done.8.a1, bf16[2,192,1024]{2,1,0:T(8,128)(2,1)} %collective-permute-done.9.a2, ...), custom_call_target="tpu_custom_call" | custom-call | flops 3221225472 | bytes 11534336 | tf_op jit(solution)/shard_map/pallas_call | solution.py:99
  144.3 45.0 %all_to_all.20 = bf16[8,192,1152]{2,1,0:T(8,128)(2,1)S(1)} all-to-all(bf16[8,192,1152]{2,1,0:T(8,128)(2,1)} %shard_map.129), channel_id=1, replica_groups={{0,1,2,3,64,65,66,67},{4,5,6,7,68,69,70,71},{8,9,10,11,72,73,74,75},{12..., dimensions={0} | all-to-all | bytes 7077888 | tf_op jit(solution)/shard_map/all_to_all | solution.py:35
  189.3 0.4 convert_reduce_fusion
  189.7 0.9 fusion.12
  190.6 2.1 %fusion.14 = (bf16[1,192,1024]{2,1,0:T(8,128)(2,1)}, bf16[1,192,1024]{2,1,0:T(8,128)(2,1)}) fusion(bf16[192,1024]{1,0:T(8,128)(2,1)S(1)} %bitcast.64, bf16[192,1024]{1,0:T(8,128)(2,1)S(1)} %bitcast.66, s32[1024]{0:T(1024)S(1)} %get-tuple-element.26, s32[1024]{0:T(1024)S(1)} %get-tuple-element.27, s32[1024]{0:T(1024)S(1)} %get-tuple-element.24, ...), kind=kOutput, calls=%fused_computation.32 | convolution fusion | flops 424935424 | bytes 1993732 | tf_op jit(solution)/shard_map/dot_general | solution.py:166
  (23 shorter events, 0.1 us)
Async XLA Ops:
  7.2 1.2 copy-start
  7.2 128.7 %all-gather.2.cloned.1.call-start = ((), (), s32[]{:S(2)}) async-start(), calls=%async_computation.3 | async-start | bytes 4456448 | tf_op jit(solution)/shard_map/all_gather | solution.py:127
  23.6 4.7 %collective-permute-start = (f32[8,128]{1,0:T(8,128)S(1)}, f32[8,128]{1,0:T(8,128)S(1)}, u32[]{:S(2)}, u32[]{:S(2)}) collective-permute-start(f32[8,128]{1,0:T(8,128)S(1)} %broadcast_in_dim.37), channel_id=1, source_target_pairs={{0,4},{4,0},{8,12},{12,8},{16,20},{20,16},{24,28},{28,24},{32,36},... | collective-permute-start | bytes 12296 | tf_op jit(solution)/shard_map/ppermute | solution.py:43
  28.9 5.9 %collective-permute-start.1 = (f32[8,128]{1,0:T(8,128)S(1)}, f32[8,128]{1,0:T(8,128)S(1)}, u32[]{:S(2)}, u32[]{:S(2)}) collective-permute-start(f32[8,128]{1,0:T(8,128)S(1)} %broadcast_add_fusion.2), channel_id=1, source_target_pairs={{0,8},{4,12},{8,0},{12,4},{16,24},{20,28},{24,16},{28,20},{32,40},... | collective-permute-start | bytes 12296 | tf_op jit(solution)/shard_map/ppermute | solution.py:43
  35.5 9.9 %collective-permute-start.2 = (f32[8,128]{1,0:T(8,128)S(1)}, f32[8,128]{1,0:T(8,128)S(1)}, u32[]{:S(2)}, u32[]{:S(2)}) collective-permute-start(f32[8,128]{1,0:T(8,128)S(1)} %fusion.32), channel_id=1, source_target_pairs={{0,16},{4,20},{8,24},{12,28},{16,0},{20,4},{24,8},{28,12},{32,48},... | collective-permute-start | bytes 12296 | tf_op jit(solution)/shard_map/ppermute | solution.py:43
  45.4 15.3 %collective-permute-start.3 = (f32[8,128]{1,0:T(8,128)S(1)}, f32[8,128]{1,0:T(8,128)S(1)}, u32[]{:S(2)}, u32[]{:S(2)}) collective-permute-start(f32[8,128]{1,0:T(8,128)S(1)} %add.73), channel_id=1, source_target_pairs={{0,32},{4,36},{8,40},{12,44},{16,48},{20,52},{24,56},{28,60},{32,0... | collective-permute-start | bytes 12296 | tf_op jit(solution)/shard_map/ppermute | solution.py:43
  58.5 31.2 %collective-permute-start.7 = (bf16[192,1024]{1,0:T(8,128)(2,1)}, bf16[192,1024]{1,0:T(8,128)(2,1)S(1)}, u32[]{:S(2)}, u32[]{:S(2)}) collective-permute-start(bf16[192,1024]{1,0:T(8,128)(2,1)} %bitcast.53), channel_id=1, source_target_pairs={{0,64},{4,68},{8,72},{12,76},{16,80},{20,84},{24,88},{28,92},{32,9... | collective-permute-start | bytes 1179656 | tf_op jit(solution)/shard_map/ppermute | solution.py:134
  61.2 35.6 %collective-permute-start.6 = (bf16[192,1024]{1,0:T(8,128)(2,1)}, bf16[192,1024]{1,0:T(8,128)(2,1)}, u32[]{:S(2)}, u32[]{:S(2)}) collective-permute-start(bf16[192,1024]{1,0:T(8,128)(2,1)} %bitcast.58), channel_id=1, source_target_pairs={{0,384},{128,256},{256,128},{384,0},{1,385},{129,257},{257,129},{3... | collective-permute-start | bytes 1179656 | tf_op jit(solution)/shard_map/ppermute | solution.py:152
  71.6 28.5 %collective-permute-start.5 = (bf16[192,1024]{1,0:T(8,128)(2,1)}, bf16[192,1024]{1,0:T(8,128)(2,1)}, u32[]{:S(2)}, u32[]{:S(2)}) collective-permute-start(bf16[192,1024]{1,0:T(8,128)(2,1)} %bitcast.59), channel_id=1, source_target_pairs={{0,256},{128,384},{256,0},{384,128},{1,257},{129,385},{257,1},{385... | collective-permute-start | bytes 1179656 | tf_op jit(solution)/shard_map/ppermute | solution.py:152
  73.8 26.3 %collective-permute-start.4 = (bf16[192,1024]{1,0:T(8,128)(2,1)}, bf16[192,1024]{1,0:T(8,128)(2,1)}, u32[]{:S(2)}, u32[]{:S(2)}) collective-permute-start(bf16[192,1024]{1,0:T(8,128)(2,1)} %bitcast.60), channel_id=1, source_target_pairs={{0,128},{128,0},{256,384},{384,256},{1,129},{129,1},{257,385},{385... | collective-permute-start | bytes 1179656 | tf_op jit(solution)/shard_map/ppermute | solution.py:152
  78.1 11.7 %copy-start.2 = (bf16[1,192,1024]{2,1,0:T(8,128)(2,1)S(1)}, bf16[1,192,1024]{2,1,0:T(8,128)(2,1)}, u32[]{:S(2)}) copy-start(bf16[1,192,1024]{2,1,0:T(8,128)(2,1)} %param.11) | copy-start | bytes 1179652
  78.1 22.0 %copy-start.3 = (s32[192]{0:T(256)S(1)}, s32[192]{0:T(256)}, u32[]{:S(2)}) copy-start(s32[192]{0:T(256)} %param.17) | copy-start | bytes 2308
  86.2 17.2 %all-to-all-start.1 = ((bf16[8,400,128]{2,1,0:T(8,128)(2,1)}), bf16[8,400,128]{2,1,0:T(8,128)(2,1)S(1)}, u32[]{:S(2)}, u32[]{:S(2)}) async-start(bf16[8,400,128]{2,1,0:T(8,128)(2,1)} %pad_maximum_fusion), calls=%async_computation.1 | async-start | bytes 1638400 | tf_op jit(solution)/shard_map/all_to_all | solution.py:35
  89.8 27.7 %collective-permute-start.10 = (bf16[2,192,1024]{2,1,0:T(8,128)(2,1)S(1)}, bf16[2,192,1024]{2,1,0:T(8,128)(2,1)S(1)}, u32[]{:S(2)}, u32[]{:S(2)}) collective-permute-start(bf16[2,192,1024]{2,1,0:T(8,128)(2,1)S(1)} %pad_maximum_fusion.1.a0), channel_id=1, source_target_pairs={{0,3},{1,0},{2,1},{3,2},{4,7},{5,4},{6,5},{7,6},{8,11},{9,8},{10,9... | collective-permute-start | bytes 2359304 | tf_op jit(solution)/shard_map/ppermute | solution.py:135
  94.3 24.7 %collective-permute-start.9 = (bf16[2,192,1024]{2,1,0:T(8,128)(2,1)S(1)}, bf16[2,192,1024]{2,1,0:T(8,128)(2,1)}, u32[]{:S(2)}, u32[]{:S(2)}) collective-permute-start(bf16[2,192,1024]{2,1,0:T(8,128)(2,1)S(1)} %pad_maximum_fusion.1.a0), channel_id=1, source_target_pairs={{0,2},{1,3},{2,0},{3,1},{4,6},{5,7},{6,4},{7,5},{8,10},{9,11},{10,... | collective-permute-start | bytes 2359304 | tf_op jit(solution)/shard_map/ppermute | solution.py:135
  96.8 39.0 %collective-permute-start.8 = (bf16[2,192,1024]{2,1,0:T(8,128)(2,1)S(1)}, bf16[2,192,1024]{2,1,0:T(8,128)(2,1)}, u32[]{:S(2)}, u32[]{:S(2)}) collective-permute-start(bf16[2,192,1024]{2,1,0:T(8,128)(2,1)S(1)} %pad_maximum_fusion.1.a0), channel_id=1, source_target_pairs={{0,1},{1,2},{2,3},{3,0},{4,5},{5,6},{6,7},{7,4},{8,9},{9,10},{10,1... | collective-permute-start | bytes 2359304 | tf_op jit(solution)/shard_map/ppermute | solution.py:135
  144.3 45.4 %copy-start.1 = (f32[192,1024]{1,0:T(8,128)S(1)}, f32[192,1024]{1,0:T(8,128)}, u32[]{:S(2)}) copy-start(f32[192,1024]{1,0:T(8,128)} %get-tuple-element.17) | copy-start | bytes 2359300
  189.3 1.3 copy-start.4
  189.3 1.3 copy-start.5
Sparse Core Ops, SparseCore 0:
  21.2 74.1 all-gather.1

commit v3 on v2

--- a/solution.py
+++ b/solution.py
@@ -24,11 +24,6 @@
 BOTH = ("fsdp", "tp")
 PLANE_GROUPS = [[(y * ZS + z) * XS + x for y in range(YS) for x in range(XS)] for z in range(ZS)]
 Z_GROUPS = [[y * ZS + z for z in range(ZS)] for y in range(YS)]
-Y_SWAP = [(f, (f + ZS) % (YS * ZS)) for f in range(YS * ZS)]
-
-
-def x_shift(s):
-    return [(x, (x + s) % XS) for x in range(XS)]
 
 
 def plane_exchange(value):
@@ -37,19 +32,13 @@
     )
 
 
-def ring_squares(grad):
+def total_squares(grad):
     total = jnp.full((8, 128), jnp.sum(jnp.square(grad.astype(jnp.float32))))
-    for bit in (1, 2, 4, 8):
+    for bit in (1, 2, 4, 8, 16):
         total = total + lax.ppermute(total, "fsdp", [(f, f ^ bit) for f in range(YS * ZS)])
-    return total[0:1, 0:1]
-
-
-def three_pieces(value):
-    high = lax.reduce_precision(value, 8, 7)
-    middle = lax.reduce_precision(value - high, 8, 7)
-    low = lax.reduce_precision(value - high - middle, 8, 7)
-    rows = jnp.concatenate([high, middle, low, jnp.zeros((13, 1), jnp.float32)], axis=0)
-    return jnp.broadcast_to(rows.astype(jnp.bfloat16), (PLANE, 16, 128))
+    for bit in (1, 2):
+        total = total + lax.ppermute(total, "tp", [(x, x ^ bit) for x in range(XS)])
+    return total[0, 0]
 
 
 def swap_matrix():
@@ -59,27 +48,24 @@
     return (row == swapped).astype(jnp.bfloat16)
 
 
-def core_kernel(where_ref, clip_ref, a0, a1, a2, a3, b_ref, m_ref, out_ref, dir_ref):
-    y = where_ref[0]
-    x = where_ref[1]
+def core_kernel(clip_ref, b_ref, m_ref, out_ref, dir_ref):
     clip = clip_ref[0]
     acc = jnp.zeros((384, 512), jnp.float32)
-    for s, piece in enumerate((a0, a1, a2, a3)):
-        at = pl.multiple_of(lax.rem(x + XS - s, XS) * 1024, 1024)
+    for t in range(XS):
+        rows = jnp.concatenate([m_ref[u * XS + t, :, 0:1024] for u in range(YS)], axis=0)
         acc = acc + lax.dot_general(
-            piece[...].reshape(384, 1024),
-            b_ref[:, pl.ds(at, 1024)],
+            rows,
+            b_ref[:, t * 1024 : (t + 1) * 1024],
             (((1,), (1,)), ((), ())),
             preferred_element_type=jnp.float32,
         )
     for u in range(YS):
-        row = lax.rem(y + u, YS)
         for t in range(XS):
             rotated = acc[u * 192 : (u + 1) * 192, t * 128 : (t + 1) * 128]
-            out_ref[row * XS + t, :, 1024:1152] = rotated.astype(jnp.bfloat16)
+            out_ref[u * XS + t, :, 1024:1152] = rotated.astype(jnp.bfloat16)
             scaled = clip * rotated
-            first = m_ref[row * XS + t, 0:192].astype(jnp.float32)
-            second = m_ref[row * XS + t, 192:384].astype(jnp.float32)
+            first = m_ref[u * XS + t, :, 1024:1152].astype(jnp.float32)
+            second = m_ref[u * XS + t, :, 1152:1280].astype(jnp.float32)
             first = beta_first * first + (1.0 - beta_first) * scaled
             second = beta_second * second + (1.0 - beta_second) * scaled * scaled
             dir_ref[u * 192 : (u + 1) * 192, t * 128 : (t + 1) * 128] = (
@@ -90,23 +76,23 @@
             dir_ref[...], b_ref[:, t * 1024 : (t + 1) * 1024], preferred_element_type=jnp.float32
         ).astype(jnp.bfloat16)
         for u in range(YS):
-            out_ref[lax.rem(y + u, YS) * XS + t, :, 0:1024] = update[u * 192 : (u + 1) * 192]
+            out_ref[u * XS + t, :, 0:1024] = update[u * 192 : (u + 1) * 192]
 
 
-def core(where, clip, pieces, basis, moments):
+def core(clip, basis, arrived):
     vmem = pl.BlockSpec(memory_space=pltpu.VMEM)
     smem = pl.BlockSpec(memory_space=pltpu.SMEM)
     return pl.pallas_call(
         core_kernel,
         out_shape=jax.ShapeDtypeStruct((PLANE, 192, 1152), jnp.bfloat16),
-        in_specs=[smem, smem] + [vmem] * 6,
+        in_specs=[smem, vmem, vmem],
         out_specs=vmem,
         scratch_shapes=[pltpu.VMEM((384, 512), jnp.bfloat16)],
         compiler_params=pltpu.CompilerParams(vmem_limit_bytes=48 * 2**20),
         cost_estimate=pl.CostEstimate(
             flops=4 * 384 * 4096 * 512, bytes_accessed=11 * 2**20, transcendentals=384 * 512
         ),
-    )(where, clip, *pieces, basis, moments)
+    )(clip, basis, arrived)
 
 
 def on_device(
@@ -126,24 +112,19 @@
     mixed = mixed.reshape(YS, XS, 16, 1024).transpose(0, 2, 1, 3).reshape(YS, 16, K)
     basis = lax.all_gather(mixed, "fsdp", axis=1, axis_index_groups=Z_GROUPS, tiled=True)
     basis = basis.reshape(512, K)
-    mixed, grad = lax.optimization_barrier((mixed, grads[0]))
+    mixed, grad, first, second = lax.optimization_barrier(
+        (mixed, grads[0], first_moment[0], second_moment[0])
+    )
 
-    y_index = lax.axis_index("fsdp") // ZS
-    x_index = lax.axis_index("tp")
-    where = jnp.stack([y_index, x_index]).astype(jnp.int32)
-    own = jnp.stack([grad, lax.ppermute(grad, "fsdp", Y_SWAP)])
-    pieces = [own] + [lax.ppermute(own, "tp", x_shift(s)) for s in range(1, XS)]
-
-    squares = ring_squares(grad)
-    squares, first, second, delta = lax.optimization_barrier(
-        (squares, first_moment[0], second_moment[0], outer_delta[0])
-    )
     swap = swap_matrix()
     both = jnp.concatenate([first, second], axis=0)
     both = jnp.dot(both, swap, preferred_element_type=jnp.float32).astype(jnp.bfloat16)
-    both = both.reshape(384, PLANE, 128).transpose(1, 0, 2)
-    moments = plane_exchange(jnp.concatenate([both, three_pieces(squares)], axis=1))
-    squares = jnp.sum(moments[:, 384:387, 0].astype(jnp.float32))
+    both = both.reshape(2, 192, PLANE, 128).transpose(2, 0, 1, 3)
+    rows = jnp.broadcast_to(grad, (PLANE, 192, 1024))
+    leaving = jnp.concatenate([rows, both[:, 0], both[:, 1]], axis=2)
+    leaving, grad, delta = lax.optimization_barrier((leaving, grad, outer_delta[0]))
+    arrived = plane_exchange(leaving)
+    squares = total_squares(grad)
     limit = clip_ratio * jnp.sqrt(jnp.float32(N * K))
     clip = jnp.minimum(jnp.float32(1.0), limit / jnp.sqrt(squares + 1e-06))
 
@@ -159,9 +140,9 @@
     )
     new_momentum = new_momentum.astype(jnp.bfloat16)
     kept = weights[0].astype(jnp.float32) - correction
-    kept, new_momentum, moments = lax.optimization_barrier((kept, new_momentum, moments))
+    kept, new_momentum, clip = lax.optimization_barrier((kept, new_momentum, clip))
 
-    mine = plane_exchange(core(where, clip.reshape(1), pieces, basis, moments))
+    mine = plane_exchange(core(clip.reshape(1), basis, arrived))
     rotated = mine[:, :, 1024:].transpose(1, 0, 2).reshape(192, 1024)
     rotated = jnp.dot(rotated, swap, preferred_element_type=jnp.float32)
     scaled = clip * rotated

time: 201 us -> 171 us (0.85)
  waiting for transfers between devices: 34.2 us -> 12.7 us
  between operations: 21.9 us -> 16.4 us
  other arithmetic: 10.4 us -> 6.89 us
    ppermute x8 -> x7, waiting for transfers between devices: 34.2 us -> 12.6 us  [the longest x5 10.9 us: total_squares(): lax.ppermute(total, 'fsdp', [(f, f ^ bit) for f in range(YS * ZS)])]
    ppermute x3, starting transfers between devices: 14.6 us -> 11.4 us  [on_device(): lax.ppermute(delta, 'island', [(i, i ^ bit) for i in range(4)])]
    ppermute x8 -> x7, starting transfers between devices: 42.1 us -> 44.9 us  [the longest x5 33.4 us: total_squares(): lax.ppermute(total, 'fsdp', [(f, f ^ bit) for f in range(YS * ZS)])]
  transfers between devices with their start and end apart: 13 -> 12, of which waited for: 6 -> 6; matrix products, arithmetic and copies ran while one was open for 7% -> 6% of each run, Pallas kernels for 0% -> 0%
where the time goes in v3:
time: 171 us; the launch traced here: 168 us
  starting transfers between devices  61.1 us (36%)
  blocking collectives  55.5 us (32%)
  between operations  16.4 us (10%)
  waiting for transfers between devices  12.7 us (7%)
  Pallas kernels  7.35 us (4%)
  other arithmetic  6.89 us (4%)
  matrix products  4.31 us (3%)
  local copies, waits for them, and re-layouts  3.89 us (2%)
    all_to_all x2, blocking collectives, plane_exchange(): lax.all_to_all(value, BOTH, split_axis=0, concat_axis=0, axis_index_group...  55.5 us
    ppermute x5, starting transfers between devices, total_squares(): lax.ppermute(total, 'fsdp', [(f, f ^ bit) for f in range(YS * ZS)])  33.4 us
    ppermute x2, starting transfers between devices, total_squares(): total = total + lax.ppermute(total, 'tp', [(x, x ^ bit) for x in range(XS)])  11.5 us
    ppermute x3, starting transfers between devices, on_device(): lax.ppermute(delta, 'island', [(i, i ^ bit) for i in range(4)])  11.4 us
    ppermute x5, waiting for transfers between devices, total_squares(): lax.ppermute(total, 'fsdp', [(f, f ^ bit) for f in range(YS * ZS)])  10.9 us
    pallas_call x1, Pallas kernels, core(): pl.pallas_call(core_kernel, out_shape=jax.ShapeDtypeStruct((PLANE, 192, 1...  7.35 us
    all_to_all x1, starting transfers between devices, plane_exchange(): lax.all_to_all(value, BOTH, split_axis=0, concat_axis=0, axis_index_group...  4.68 us
  transfers between devices with their start and end apart: 12, of which 6 were waited for; matrix products, arithmetic and copies ran while one was open for 6% of the time, Pallas kernels for 0%

profile of v3, /device:TPU:1, one launch (start us, length us, event | category | flops | bytes accessed | tf_op | source)
XLA Modules:
  0.0 168.1 jit_solution(4089430318499687148)
XLA Ops:
  7.2 0.0 copy-start
  7.2 0.0 all-gather.2.cloned.1.call-start
  8.0 0.5 copy-done
  8.4 0.1 copy.17
  8.6 11.8 %all_to_all.19 = bf16[8,16,1024]{2,1,0:T(8,128)(2,1)S(1)} all-to-all(bf16[8,16,1024]{2,1,0:T(8,128)(2,1)S(1)} %bitcast.58), channel_id=1, replica_groups={{0,1,2,3,64,65,66,67},{4,5,6,7,68,69,70,71},{8,9,10,11,72,73,74,75},{12..., dimensions={0} | all-to-all | bytes 524288 | tf_op jit(solution)/shard_map/all_to_all | solution.py:30
  20.4 0.7 copy.21
  21.1 0.0 all-gather.2.cloned.1.call-update
  21.2 2.2 %fusion.5 = bf16[48,8,8,128]{3,1,2,0:T(8,128)(2,1)S(1)} fusion(bf16[192,1024]{1,0:T(8,128)(2,1)} %bitcast.65, bf16[192,1024]{1,0:T(8,128)(2,1)} %bitcast.67, s32[1024]{0:T(1024)S(1)} %get-tuple-element.30, s32[1024]{0:T(1024)S(1)} %get-tuple-element.31, s32[1024]{0:T(1024)S(1)} %get-tuple-element.28, s32[1024]{0:T(1024)S(1)} %get-tuple-element.34, ...), kind=kOutput, calls=%fused_computation.13 | convolution fusion | flops 827195392 | bytes 1600512 | tf_op jit(solution)/shard_map/dot_general | solution.py:121
  23.4 0.0 copy-start.1
  23.4 0.2 copy.23
  23.6 0.1 copy.31
  23.8 0.1 slice_bitcast_fusion.2
  23.8 0.6 copy-done.1
  24.4 0.4 broadcast_in_dim.35
  24.8 2.1 %pad_maximum_fusion = bf16[8,192,1280]{2,1,0:T(8,128)(2,1)} fusion(bf16[8,192,128]{2,1,0:T(8,128)(2,1)S(1)} %get-tuple-element.27, bf16[8,192,128]{2,1,0:T(8,128)(2,1)S(1)} %get-tuple-element.26, bf16[8,192,1024]{2,1,0:T(8,128)(2,1)S(1)} %broadcast_in_dim.35), kind=kLoop, calls=%fused_computation.11 | loop fusion | flops 11796480 | bytes 7864320 | tf_op jit(solution)/shard_map/concatenate | solution.py:124
  26.9 4.7 %all-to-all-start.1 = ((bf16[8,192,1280]{2,1,0:T(8,128)(2,1)}), bf16[8,192,1280]{2,1,0:T(8,128)(2,1)}, u32[]{:S(2)}, u32[]{:S(2)}) async-start(bf16[8,192,1280]{2,1,0:T(8,128)(2,1)} %pad_maximum_fusion), calls=%async_computation.1 | async-start | bytes 7864320 | tf_op jit(solution)/shard_map/all_to_all | solution.py:30
  31.6 0.8 multiply_reduce_fusion
  32.4 0.6 broadcast_in_dim.37
  33.0 3.7 %collective-permute-start.3 = (f32[8,128]{1,0:T(8,128)S(1)}, f32[8,128]{1,0:T(8,128)S(1)}, u32[]{:S(2)}, u32[]{:S(2)}) collective-permute-start(f32[8,128]{1,0:T(8,128)S(1)} %broadcast_in_dim.37), channel_id=1, source_target_pairs={{0,4},{4,0},{8,12},{12,8},{16,20},{20,16},{24,28},{28,24},{32,36},... | collective-permute-start | bytes 12296 | tf_op jit(solution)/shard_map/ppermute | solution.py:38
  36.8 1.0 collective-permute-done.3
  37.8 0.6 broadcast_add_fusion
  38.4 5.3 %collective-permute-start.4 = (f32[8,128]{1,0:T(8,128)S(1)}, f32[8,128]{1,0:T(8,128)S(1)}, u32[]{:S(2)}, u32[]{:S(2)}) collective-permute-start(f32[8,128]{1,0:T(8,128)S(1)} %broadcast_add_fusion), channel_id=1, source_target_pairs={{0,8},{4,12},{8,0},{12,4},{16,24},{20,28},{24,16},{28,20},{32,40},... | collective-permute-start | bytes 12296 | tf_op jit(solution)/shard_map/ppermute | solution.py:38
  43.7 7.2 %collective-permute-start.2 = (bf16[192,1024]{1,0:T(8,128)(2,1)S(1)}, bf16[192,1024]{1,0:T(8,128)(2,1)S(1)}, u32[]{:S(2)}, u32[]{:S(2)}) collective-permute-start(bf16[192,1024]{1,0:T(8,128)(2,1)S(1)} %bitcast.60), channel_id=1, source_target_pairs={{0,384},{128,256},{256,128},{384,0},{1,385},{129,257},{257,129},{3... | collective-permute-start | bytes 1179656 | tf_op jit(solution)/shard_map/ppermute | solution.py:133
  50.9 2.3 %collective-permute-start.1 = (bf16[192,1024]{1,0:T(8,128)(2,1)S(1)}, bf16[192,1024]{1,0:T(8,128)(2,1)S(1)}, u32[]{:S(2)}, u32[]{:S(2)}) collective-permute-start(bf16[192,1024]{1,0:T(8,128)(2,1)S(1)} %bitcast.61), channel_id=1, source_target_pairs={{0,256},{128,384},{256,0},{384,128},{1,257},{129,385},{257,1},{385... | collective-permute-start | bytes 1179656 | tf_op jit(solution)/shard_map/ppermute | solution.py:133
  53.2 2.0 %collective-permute-start = (bf16[192,1024]{1,0:T(8,128)(2,1)S(1)}, bf16[192,1024]{1,0:T(8,128)(2,1)S(1)}, u32[]{:S(2)}, u32[]{:S(2)}) collective-permute-start(bf16[192,1024]{1,0:T(8,128)(2,1)S(1)} %bitcast.62), channel_id=1, source_target_pairs={{0,128},{128,0},{256,384},{384,256},{1,129},{129,1},{257,385},{385... | collective-permute-start | bytes 1179656 | tf_op jit(solution)/shard_map/ppermute | solution.py:133
  55.2 0.0 collective-permute-done.4
  55.2 0.7 fusion.33
  55.9 8.8 %collective-permute-start.5 = (f32[8,128]{1,0:T(8,128)S(1)}, f32[8,128]{1,0:T(8,128)S(1)}, u32[]{:S(2)}, u32[]{:S(2)}) collective-permute-start(f32[8,128]{1,0:T(8,128)S(1)} %fusion.33), channel_id=1, source_target_pairs={{0,16},{4,20},{8,24},{12,28},{16,0},{20,4},{24,8},{28,12},{32,48},... | collective-permute-start | bytes 12296 | tf_op jit(solution)/shard_map/ppermute | solution.py:38
  64.7 1.1 collective-permute-done.5
  65.8 12.1 %collective-permute-start.6 = (f32[8,128]{1,0:T(8,128)S(1)}, f32[8,128]{1,0:T(8,128)S(1)}, u32[]{:S(2)}, u32[]{:S(2)}) collective-permute-start(f32[8,128]{1,0:T(8,128)S(1)} %add.91), channel_id=1, source_target_pairs={{0,32},{4,36},{8,40},{12,44},{16,48},{20,52},{24,56},{28,60},{32,0... | collective-permute-start | bytes 12296 | tf_op jit(solution)/shard_map/ppermute | solution.py:38
  77.9 1.1 collective-permute-done.6
  79.0 3.5 %collective-permute-start.7 = (f32[8,128]{1,0:T(8,128)S(1)}, f32[8,128]{1,0:T(8,128)S(1)}, u32[]{:S(2)}, u32[]{:S(2)}) collective-permute-start(f32[8,128]{1,0:T(8,128)S(1)} %add.92), channel_id=1, source_target_pairs={{0,64},{4,68},{8,72},{12,76},{16,80},{20,84},{24,88},{28,92},{32,9... | collective-permute-start | bytes 12296 | tf_op jit(solution)/shard_map/ppermute | solution.py:38
  82.5 7.7 %collective-permute-done.7 = f32[8,128]{1,0:T(8,128)S(1)} collective-permute-done((f32[8,128]{1,0:T(8,128)S(1)}, f32[8,128]{1,0:T(8,128)S(1)}, u32[]{:S(2)}, u32[]{:S(2)}) %collective-permute-start.7) | collective-permute-done | bytes 4128 | tf_op jit(solution)/shard_map/ppermute | solution.py:38
  90.2 7.1 %collective-permute-start.8 = (f32[8,128]{1,0:T(8,128)S(1)}, f32[8,128]{1,0:T(8,128)S(1)}, u32[]{:S(2)}, u32[]{:S(2)}) collective-permute-start(f32[8,128]{1,0:T(8,128)S(1)} %add.93), channel_id=1, source_target_pairs={{0,1},{1,0},{2,3},{3,2},{4,5},{5,4},{6,7},{7,6},{8,9},{9,8},{10,11... | collective-permute-start | bytes 12296 | tf_op jit(solution)/shard_map/ppermute | solution.py:40
  97.9 0.3 collective-permute-done.8
  98.3 4.4 %collective-permute-start.9 = (f32[8,128]{1,0:T(8,128)S(1)}, f32[8,128]{1,0:T(8,128)S(1)}, u32[]{:S(2)}, u32[]{:S(2)}) collective-permute-start(f32[8,128]{1,0:T(8,128)S(1)} %add.94), channel_id=1, source_target_pairs={{0,2},{1,3},{2,0},{3,1},{4,6},{5,7},{6,4},{7,5},{8,10},{9,11},{10,... | collective-permute-start | bytes 12296 | tf_op jit(solution)/shard_map/ppermute | solution.py:40
  102.7 1.4 collective-permute-done.9
  104.1 0.5 slice.17
  105.3 0.0 collective-permute-done.2
  105.3 0.0 collective-permute-done.1
  105.4 0.0 collective-permute-done
  105.4 1.4 fusion.12
  106.7 0.0 all-to-all-done.1.m_ref
  106.7 7.4 %shard_map.129 = bf16[8,192,1152]{2,1,0:T(8,128)(2,1)S(1)} custom-call(f32[1]{0:T(128)} %bitcast.16.clip_ref, bf16[512,4096]{1,0:T(8,128)(2,1)} %bitcast.64, bf16[8,192,1280]{2,1,0:T(8,128)(2,1)} %all-to-all-done.1.m_ref), custom_call_target="tpu_custom_call" | custom-call | flops 3221225472 | bytes 11534336 | tf_op jit(solution)/shard_map/pallas_call | solution.py:85
  114.1 43.7 %all_to_all.20 = bf16[8,192,1152]{2,1,0:T(8,128)(2,1)S(1)} all-to-all(bf16[8,192,1152]{2,1,0:T(8,128)(2,1)S(1)} %shard_map.129), channel_id=1, replica_groups={{0,1,2,3,64,65,66,67},{4,5,6,7,68,69,70,71},{8,9,10,11,72,73,74,75},{12..., dimensions={0} | all-to-all | bytes 7077888 | tf_op jit(solution)/shard_map/all_to_all | solution.py:30
  157.9 0.4 convert_reduce_fusion
  158.3 0.9 fusion.13
  159.2 2.1 %fusion.15 = (bf16[1,192,1024]{2,1,0:T(8,128)(2,1)}, bf16[1,192,1024]{2,1,0:T(8,128)(2,1)}) fusion(bf16[192,1024]{1,0:T(8,128)(2,1)S(1)} %bitcast.66, bf16[192,1024]{1,0:T(8,128)(2,1)S(1)} %bitcast.68, s32[1024]{0:T(1024)S(1)} %get-tuple-element.30, s32[1024]{0:T(1024)S(1)} %get-tuple-element.31, s32[1024]{0:T(1024)S(1)} %get-tuple-element.28, ...), kind=kOutput, calls=%fused_computation.33 | convolution fusion | flops 424935424 | bytes 1993732 | tf_op jit(solution)/shard_map/dot_general | solution.py:147
  (25 shorter events, 0.1 us)
Async XLA Ops:
  7.2 1.2 copy-start
  7.2 99.6 %all-gather.2.cloned.1.call-start = ((), (), s32[]{:S(2)}) async-start(), calls=%async_computation.3 | async-start | bytes 4456448 | tf_op jit(solution)/shard_map/all_gather | solution.py:113
  23.4 1.0 copy-start.1
  26.9 16.8 %copy-start.3 = (bf16[1,192,1024]{2,1,0:T(8,128)(2,1)S(1)}, bf16[1,192,1024]{2,1,0:T(8,128)(2,1)}, u32[]{:S(2)}) copy-start(bf16[1,192,1024]{2,1,0:T(8,128)(2,1)} %param.15) | copy-start | bytes 1179652
  26.9 75.8 %copy-start.5 = (s32[192]{0:T(256)S(1)}, s32[192]{0:T(256)}, u32[]{:S(2)}) copy-start(s32[192]{0:T(256)} %param.17) | copy-start | bytes 2308
  26.9 78.5 %copy-start.2 = (bf16[192,1024]{1,0:T(8,128)(2,1)S(1)}, bf16[192,1024]{1,0:T(8,128)(2,1)}, u32[]{:S(2)}) copy-start(bf16[192,1024]{1,0:T(8,128)(2,1)} %param.16) | copy-start | bytes 1179652
  26.9 78.5 %copy-start.4 = (bf16[1,192,1024]{2,1,0:T(8,128)(2,1)S(1)}, bf16[1,192,1024]{2,1,0:T(8,128)(2,1)}, u32[]{:S(2)}) copy-start(bf16[1,192,1024]{2,1,0:T(8,128)(2,1)} %param.10) | copy-start | bytes 1179652
  26.9 79.8 %all-to-all-start.1 = ((bf16[8,192,1280]{2,1,0:T(8,128)(2,1)}), bf16[8,192,1280]{2,1,0:T(8,128)(2,1)}, u32[]{:S(2)}, u32[]{:S(2)}) async-start(bf16[8,192,1280]{2,1,0:T(8,128)(2,1)} %pad_maximum_fusion), calls=%async_computation.1 | async-start | bytes 7864320 | tf_op jit(solution)/shard_map/all_to_all | solution.py:30
  33.0 4.7 %collective-permute-start.3 = (f32[8,128]{1,0:T(8,128)S(1)}, f32[8,128]{1,0:T(8,128)S(1)}, u32[]{:S(2)}, u32[]{:S(2)}) collective-permute-start(f32[8,128]{1,0:T(8,128)S(1)} %broadcast_in_dim.37), channel_id=1, source_target_pairs={{0,4},{4,0},{8,12},{12,8},{16,20},{20,16},{24,28},{28,24},{32,36},... | collective-permute-start | bytes 12296 | tf_op jit(solution)/shard_map/ppermute | solution.py:38
  38.4 16.8 %collective-permute-start.4 = (f32[8,128]{1,0:T(8,128)S(1)}, f32[8,128]{1,0:T(8,128)S(1)}, u32[]{:S(2)}, u32[]{:S(2)}) collective-permute-start(f32[8,128]{1,0:T(8,128)S(1)} %broadcast_add_fusion), channel_id=1, source_target_pairs={{0,8},{4,12},{8,0},{12,4},{16,24},{20,28},{24,16},{28,20},{32,40},... | collective-permute-start | bytes 12296 | tf_op jit(solution)/shard_map/ppermute | solution.py:38
  43.7 61.6 %collective-permute-start.2 = (bf16[192,1024]{1,0:T(8,128)(2,1)S(1)}, bf16[192,1024]{1,0:T(8,128)(2,1)S(1)}, u32[]{:S(2)}, u32[]{:S(2)}) collective-permute-start(bf16[192,1024]{1,0:T(8,128)(2,1)S(1)} %bitcast.60), channel_id=1, source_target_pairs={{0,384},{128,256},{256,128},{384,0},{1,385},{129,257},{257,129},{3... | collective-permute-start | bytes 1179656 | tf_op jit(solution)/shard_map/ppermute | solution.py:133
  50.9 54.4 %collective-permute-start.1 = (bf16[192,1024]{1,0:T(8,128)(2,1)S(1)}, bf16[192,1024]{1,0:T(8,128)(2,1)S(1)}, u32[]{:S(2)}, u32[]{:S(2)}) collective-permute-start(bf16[192,1024]{1,0:T(8,128)(2,1)S(1)} %bitcast.61), channel_id=1, source_target_pairs={{0,256},{128,384},{256,0},{384,128},{1,257},{129,385},{257,1},{385... | collective-permute-start | bytes 1179656 | tf_op jit(solution)/shard_map/ppermute | solution.py:133
  53.2 52.1 %collective-permute-start = (bf16[192,1024]{1,0:T(8,128)(2,1)S(1)}, bf16[192,1024]{1,0:T(8,128)(2,1)S(1)}, u32[]{:S(2)}, u32[]{:S(2)}) collective-permute-start(bf16[192,1024]{1,0:T(8,128)(2,1)S(1)} %bitcast.62), channel_id=1, source_target_pairs={{0,128},{128,0},{256,384},{384,256},{1,129},{129,1},{257,385},{385... | collective-permute-start | bytes 1179656 | tf_op jit(solution)/shard_map/ppermute | solution.py:133
  55.9 9.9 %collective-permute-start.5 = (f32[8,128]{1,0:T(8,128)S(1)}, f32[8,128]{1,0:T(8,128)S(1)}, u32[]{:S(2)}, u32[]{:S(2)}) collective-permute-start(f32[8,128]{1,0:T(8,128)S(1)} %fusion.33), channel_id=1, source_target_pairs={{0,16},{4,20},{8,24},{12,28},{16,0},{20,4},{24,8},{28,12},{32,48},... | collective-permute-start | bytes 12296 | tf_op jit(solution)/shard_map/ppermute | solution.py:38
  65.8 13.2 %collective-permute-start.6 = (f32[8,128]{1,0:T(8,128)S(1)}, f32[8,128]{1,0:T(8,128)S(1)}, u32[]{:S(2)}, u32[]{:S(2)}) collective-permute-start(f32[8,128]{1,0:T(8,128)S(1)} %add.91), channel_id=1, source_target_pairs={{0,32},{4,36},{8,40},{12,44},{16,48},{20,52},{24,56},{28,60},{32,0... | collective-permute-start | bytes 12296 | tf_op jit(solution)/shard_map/ppermute | solution.py:38
  79.0 11.2 %collective-permute-start.7 = (f32[8,128]{1,0:T(8,128)S(1)}, f32[8,128]{1,0:T(8,128)S(1)}, u32[]{:S(2)}, u32[]{:S(2)}) collective-permute-start(f32[8,128]{1,0:T(8,128)S(1)} %add.92), channel_id=1, source_target_pairs={{0,64},{4,68},{8,72},{12,76},{16,80},{20,84},{24,88},{28,92},{32,9... | collective-permute-start | bytes 12296 | tf_op jit(solution)/shard_map/ppermute | solution.py:38
  90.2 8.1 %collective-permute-start.8 = (f32[8,128]{1,0:T(8,128)S(1)}, f32[8,128]{1,0:T(8,128)S(1)}, u32[]{:S(2)}, u32[]{:S(2)}) collective-permute-start(f32[8,128]{1,0:T(8,128)S(1)} %add.93), channel_id=1, source_target_pairs={{0,1},{1,0},{2,3},{3,2},{4,5},{5,4},{6,7},{7,6},{8,9},{9,8},{10,11... | collective-permute-start | bytes 12296 | tf_op jit(solution)/shard_map/ppermute | solution.py:40
  98.3 5.8 %collective-permute-start.9 = (f32[8,128]{1,0:T(8,128)S(1)}, f32[8,128]{1,0:T(8,128)S(1)}, u32[]{:S(2)}, u32[]{:S(2)}) collective-permute-start(f32[8,128]{1,0:T(8,128)S(1)} %add.94), channel_id=1, source_target_pairs={{0,2},{1,3},{2,0},{3,1},{4,6},{5,7},{6,4},{7,5},{8,10},{9,11},{10,... | collective-permute-start | bytes 12296 | tf_op jit(solution)/shard_map/ppermute | solution.py:40
  157.9 1.3 copy-start.6
  157.9 1.3 copy-start.7
Sparse Core Ops, SparseCore 0:
  21.2 74.8 all-gather.1

commit v4 on v3

--- a/solution.py
+++ b/solution.py
@@ -23,6 +23,7 @@
 PLANE = YS * XS
 BOTH = ("fsdp", "tp")
 PLANE_GROUPS = [[(y * ZS + z) * XS + x for y in range(YS) for x in range(XS)] for z in range(ZS)]
+Y_GROUPS = [[f, f + ZS] for f in range(ZS)]
 Z_GROUPS = [[y * ZS + z for z in range(ZS)] for y in range(YS)]
 
 
@@ -34,11 +35,10 @@
 
 def total_squares(grad):
     total = jnp.full((8, 128), jnp.sum(jnp.square(grad.astype(jnp.float32))))
-    for bit in (1, 2, 4, 8, 16):
+    for bit in (1, 2, 4, 8):
         total = total + lax.ppermute(total, "fsdp", [(f, f ^ bit) for f in range(YS * ZS)])
-    for bit in (1, 2):
-        total = total + lax.ppermute(total, "tp", [(x, x ^ bit) for x in range(XS)])
-    return total[0, 0]
+    total = lax.psum(lax.psum(total[0, 0], "tp"), "fsdp", axis_index_groups=Y_GROUPS)
+    return total
 
 
 def swap_matrix():
@@ -48,46 +48,72 @@
     return (row == swapped).astype(jnp.bfloat16)
 
 
-def core_kernel(clip_ref, b_ref, m_ref, out_ref, dir_ref):
+def core_kernel(clip_ref, b_hbm, m_hbm, out_hbm, b_ref, m_ref, dir_ref, out_ref, b_sem, m_sem, out_sem):
     clip = clip_ref[0]
+    b_copies = []
+    m_copies = []
+    for t in range(XS):
+        b_copies.append(
+            pltpu.make_async_copy(b_hbm.at[:, pl.ds(t * 1024, 1024)], b_ref.at[t], b_sem.at[t])
+        )
+        b_copies[t].start()
+        for u in range(YS):
+            m_copies.append(
+                pltpu.make_async_copy(
+                    m_hbm.at[u * XS + t], m_ref.at[t, pl.ds(u * 192, 192)], m_sem.at[t * YS + u]
+                )
+            )
+            m_copies[t * YS + u].start()
     acc = jnp.zeros((384, 512), jnp.float32)
     for t in range(XS):
-        rows = jnp.concatenate([m_ref[u * XS + t, :, 0:1024] for u in range(YS)], axis=0)
+        b_copies[t].wait()
+        for u in range(YS):
+            m_copies[t * YS + u].wait()
         acc = acc + lax.dot_general(
-            rows,
-            b_ref[:, t * 1024 : (t + 1) * 1024],
+            m_ref[t, :, 0:1024],
+            b_ref[t],
             (((1,), (1,)), ((), ())),
             preferred_element_type=jnp.float32,
         )
-    for u in range(YS):
-        for t in range(XS):
-            rotated = acc[u * 192 : (u + 1) * 192, t * 128 : (t + 1) * 128]
-            out_ref[u * XS + t, :, 1024:1152] = rotated.astype(jnp.bfloat16)
-            scaled = clip * rotated
-            first = m_ref[u * XS + t, :, 1024:1152].astype(jnp.float32)
-            second = m_ref[u * XS + t, :, 1152:1280].astype(jnp.float32)
-            first = beta_first * first + (1.0 - beta_first) * scaled
-            second = beta_second * second + (1.0 - beta_second) * scaled * scaled
-            dir_ref[u * 192 : (u + 1) * 192, t * 128 : (t + 1) * 128] = (
-                first / (jnp.sqrt(second) + adam_epsilon)
-            ).astype(jnp.bfloat16)
-    for t in range(XS):
-        update = jnp.dot(
-            dir_ref[...], b_ref[:, t * 1024 : (t + 1) * 1024], preferred_element_type=jnp.float32
-        ).astype(jnp.bfloat16)
-        for u in range(YS):
-            out_ref[u * XS + t, :, 0:1024] = update[u * 192 : (u + 1) * 192]
+    for t in range(XS):
+        rotated = acc[:, t * 128 : (t + 1) * 128]
+        for u in range(YS):
+            out_ref[u * XS + t, :, 1024:1152] = rotated[u * 192 : (u + 1) * 192].astype(jnp.bfloat16)
+        scaled = clip * rotated
+        first = m_ref[t, :, 1024:1152].astype(jnp.float32)
+        second = m_ref[t, :, 1152:1280].astype(jnp.float32)
+        first = beta_first * first + (1.0 - beta_first) * scaled
+        second = beta_second * second + (1.0 - beta_second) * scaled * scaled
+        dir_ref[:, t * 128 : (t + 1) * 128] = (first / (jnp.sqrt(second) + adam_epsilon)).astype(jnp.bfloat16)
+    out_copies = []
+    for t in range(XS):
+        update = jnp.dot(dir_ref[...], b_ref[t], preferred_element_type=jnp.float32).astype(jnp.bfloat16)
+        for u in range(YS):
+            at = u * XS + t
+            out_ref[at, :, 0:1024] = update[u * 192 : (u + 1) * 192]
+            out_copies.append(pltpu.make_async_copy(out_ref.at[at], out_hbm.at[at], out_sem.at[at]))
+            out_copies[-1].start()
+    for copy in out_copies:
+        copy.wait()
 
 
 def core(clip, basis, arrived):
-    vmem = pl.BlockSpec(memory_space=pltpu.VMEM)
     smem = pl.BlockSpec(memory_space=pltpu.SMEM)
+    hbm = pl.BlockSpec(memory_space=pl.ANY)
     return pl.pallas_call(
         core_kernel,
         out_shape=jax.ShapeDtypeStruct((PLANE, 192, 1152), jnp.bfloat16),
-        in_specs=[smem, vmem, vmem],
-        out_specs=vmem,
-        scratch_shapes=[pltpu.VMEM((384, 512), jnp.bfloat16)],
+        in_specs=[smem, hbm, hbm],
+        out_specs=hbm,
+        scratch_shapes=[
+            pltpu.VMEM((XS, 512, 1024), jnp.bfloat16),
+            pltpu.VMEM((XS, 384, 1280), jnp.bfloat16),
+            pltpu.VMEM((384, 512), jnp.bfloat16),
+            pltpu.VMEM((PLANE, 192, 1152), jnp.bfloat16),
+            pltpu.SemaphoreType.DMA((XS,)),
+            pltpu.SemaphoreType.DMA((PLANE,)),
+            pltpu.SemaphoreType.DMA((PLANE,)),
+        ],
         compiler_params=pltpu.CompilerParams(vmem_limit_bytes=48 * 2**20),
         cost_estimate=pl.CostEstimate(
             flops=4 * 384 * 4096 * 512, bytes_accessed=11 * 2**20, transcendentals=384 * 512

time: 171 us -> 165 us (0.965)
  the two profiles are of different devices: /device:TPU:1 before, /device:TPU:224 now
where the time goes in v4:
time: 165 us; the launch traced here: 164 us
  blocking collectives  76.9 us (47%)
  starting transfers between devices  29.3 us (18%)
  between operations  16.4 us (10%)
  waiting for transfers between devices  15.3 us (9%)
  Pallas kernels  9.27 us (6%)
  other arithmetic  8.02 us (5%)
  local copies, waits for them, and re-layouts  4.63 us (3%)
  matrix products  4.32 us (3%)
    all_to_all x2, blocking collectives, plane_exchange(): lax.all_to_all(value, BOTH, split_axis=0, concat_axis=0, axis_index_group...  59.7 us
    ppermute x4, starting transfers between devices, total_squares(): lax.ppermute(total, 'fsdp', [(f, f ^ bit) for f in range(YS * ZS)])  15.5 us
    ppermute x4, waiting for transfers between devices, total_squares(): lax.ppermute(total, 'fsdp', [(f, f ^ bit) for f in range(YS * ZS)])  15.3 us
    psum x1, blocking collectives, total_squares(): lax.psum(total[0, 0], 'tp')  11.7 us
    pallas_call x1, Pallas kernels, core(): pl.pallas_call(core_kernel, out_shape=jax.ShapeDtypeStruct((PLANE, 192, 1...  9.27 us
    ppermute x3, starting transfers between devices, on_device(): lax.ppermute(delta, 'island', [(i, i ^ bit) for i in range(4)])  9.09 us
    psum x1, blocking collectives, total_squares(): lax.psum(lax.psum(total[0, 0], 'tp'), 'fsdp', axis_index_groups=Y_GROUPS)  5.56 us
    all_to_all x1, starting transfers between devices, plane_exchange(): lax.all_to_all(value, BOTH, split_axis=0, concat_axis=0, axis_index_group...  4.67 us
  transfers between devices with their start and end apart: 9, of which 3 were waited for; matrix products, arithmetic and copies ran while one was open for 7% of the time, Pallas kernels for 0%

profile of v4, /device:TPU:224, one launch (start us, length us, event | category | flops | bytes accessed | tf_op | source)
XLA Modules:
  0.0 164.1 jit_solution(15961131556809034665)
XLA Ops:
  7.2 0.0 copy-start
  7.2 0.0 all-gather.2.cloned.1.call-start
  8.0 0.5 copy-done
  8.4 0.1 copy.17
  8.6 12.4 %all_to_all.19 = bf16[8,16,1024]{2,1,0:T(8,128)(2,1)S(1)} all-to-all(bf16[8,16,1024]{2,1,0:T(8,128)(2,1)S(1)} %bitcast.58), channel_id=1, replica_groups={{0,1,2,3,64,65,66,67},{4,5,6,7,68,69,70,71},{8,9,10,11,72,73,74,75},{12..., dimensions={0} | all-to-all | bytes 524288 | tf_op jit(solution)/shard_map/all_to_all | solution.py:31
  21.0 0.7 copy.21
  21.7 0.0 all-gather.2.cloned.1.call-update
  21.8 2.2 %fusion.5 = bf16[48,8,8,128]{3,1,2,0:T(8,128)(2,1)S(1)} fusion(bf16[192,1024]{1,0:T(8,128)(2,1)} %bitcast.65, bf16[192,1024]{1,0:T(8,128)(2,1)} %bitcast.67, s32[1024]{0:T(1024)S(1)} %get-tuple-element.30, s32[1024]{0:T(1024)S(1)} %get-tuple-element.31, s32[1024]{0:T(1024)S(1)} %get-tuple-element.28, s32[1024]{0:T(1024)S(1)} %get-tuple-element.34, ...), kind=kOutput, calls=%fused_computation.13 | convolution fusion | flops 827195392 | bytes 1600512 | tf_op jit(solution)/shard_map/dot_general | solution.py:147
  24.0 0.0 copy-start.1
  24.0 0.2 copy.23
  24.2 0.1 copy.31
  24.4 0.1 slice_bitcast_fusion.2
  24.4 0.6 copy-done.1
  25.0 0.4 broadcast_in_dim.35
  25.4 2.1 %pad_maximum_fusion = bf16[8,192,1280]{2,1,0:T(8,128)(2,1)} fusion(bf16[8,192,128]{2,1,0:T(8,128)(2,1)S(1)} %get-tuple-element.27, bf16[8,192,128]{2,1,0:T(8,128)(2,1)S(1)} %get-tuple-element.26, bf16[8,192,1024]{2,1,0:T(8,128)(2,1)S(1)} %broadcast_in_dim.35), kind=kLoop, calls=%fused_computation.11 | loop fusion | flops 11796480 | bytes 7864320 | tf_op jit(solution)/shard_map/concatenate | solution.py:150
  27.5 4.7 %all-to-all-start.1 = ((bf16[8,192,1280]{2,1,0:T(8,128)(2,1)}), bf16[8,192,1280]{2,1,0:T(8,128)(2,1)}, u32[]{:S(2)}, u32[]{:S(2)}) async-start(bf16[8,192,1280]{2,1,0:T(8,128)(2,1)} %pad_maximum_fusion), calls=%async_computation.1 | async-start | bytes 7864320 | tf_op jit(solution)/shard_map/all_to_all | solution.py:31
  32.2 0.8 multiply_reduce_fusion
  33.0 0.6 broadcast_in_dim.37
  33.7 2.0 %collective-permute-start.3 = (f32[8,128]{1,0:T(8,128)S(1)}, f32[8,128]{1,0:T(8,128)S(1)}, u32[]{:S(2)}, u32[]{:S(2)}) collective-permute-start(f32[8,128]{1,0:T(8,128)S(1)} %broadcast_in_dim.37), channel_id=1, source_target_pairs={{0,4},{4,0},{8,12},{12,8},{16,20},{20,16},{24,28},{28,24},{32,36},... | collective-permute-start | bytes 12296 | tf_op jit(solution)/shard_map/ppermute | solution.py:39
  35.7 3.5 %collective-permute-done.3 = f32[8,128]{1,0:T(8,128)S(1)} collective-permute-done((f32[8,128]{1,0:T(8,128)S(1)}, f32[8,128]{1,0:T(8,128)S(1)}, u32[]{:S(2)}, u32[]{:S(2)}) %collective-permute-start.3) | collective-permute-done | bytes 4128 | tf_op jit(solution)/shard_map/ppermute | solution.py:39
  39.2 0.6 broadcast_add_fusion
  39.9 1.9 %collective-permute-start.4 = (f32[8,128]{1,0:T(8,128)S(1)}, f32[8,128]{1,0:T(8,128)S(1)}, u32[]{:S(2)}, u32[]{:S(2)}) collective-permute-start(f32[8,128]{1,0:T(8,128)S(1)} %broadcast_add_fusion), channel_id=1, source_target_pairs={{0,8},{4,12},{8,0},{12,4},{16,24},{20,28},{24,16},{28,20},{32,40},... | collective-permute-start | bytes 12296 | tf_op jit(solution)/shard_map/ppermute | solution.py:39
  41.8 2.2 %collective-permute-start.2 = (bf16[192,1024]{1,0:T(8,128)(2,1)S(1)}, bf16[192,1024]{1,0:T(8,128)(2,1)S(1)}, u32[]{:S(2)}, u32[]{:S(2)}) collective-permute-start(bf16[192,1024]{1,0:T(8,128)(2,1)S(1)} %bitcast.60), channel_id=1, source_target_pairs={{0,384},{128,256},{256,128},{384,0},{1,385},{129,257},{257,129},{3... | collective-permute-start | bytes 1179656 | tf_op jit(solution)/shard_map/ppermute | solution.py:159
  44.0 4.5 %collective-permute-start.1 = (bf16[192,1024]{1,0:T(8,128)(2,1)S(1)}, bf16[192,1024]{1,0:T(8,128)(2,1)S(1)}, u32[]{:S(2)}, u32[]{:S(2)}) collective-permute-start(bf16[192,1024]{1,0:T(8,128)(2,1)S(1)} %bitcast.61), channel_id=1, source_target_pairs={{0,256},{128,384},{256,0},{384,128},{1,257},{129,385},{257,1},{385... | collective-permute-start | bytes 1179656 | tf_op jit(solution)/shard_map/ppermute | solution.py:159
  48.5 2.4 %collective-permute-start = (bf16[192,1024]{1,0:T(8,128)(2,1)S(1)}, bf16[192,1024]{1,0:T(8,128)(2,1)}, u32[]{:S(2)}, u32[]{:S(2)}) collective-permute-start(bf16[192,1024]{1,0:T(8,128)(2,1)S(1)} %bitcast.62), channel_id=1, source_target_pairs={{0,128},{128,0},{256,384},{384,256},{1,129},{129,1},{257,385},{385... | collective-permute-start | bytes 1179656 | tf_op jit(solution)/shard_map/ppermute | solution.py:159
  50.9 0.0 collective-permute-done.4
  50.9 0.7 fusion.33
  51.6 1.9 %collective-permute-start.5 = (f32[8,128]{1,0:T(8,128)S(1)}, f32[8,128]{1,0:T(8,128)S(1)}, u32[]{:S(2)}, u32[]{:S(2)}) collective-permute-start(f32[8,128]{1,0:T(8,128)S(1)} %fusion.33), channel_id=1, source_target_pairs={{0,16},{4,20},{8,24},{12,28},{16,0},{20,4},{24,8},{28,12},{32,48},... | collective-permute-start | bytes 12296 | tf_op jit(solution)/shard_map/ppermute | solution.py:39
  53.5 7.6 %collective-permute-done.5 = f32[8,128]{1,0:T(8,128)S(1)} collective-permute-done((f32[8,128]{1,0:T(8,128)S(1)}, f32[8,128]{1,0:T(8,128)S(1)}, u32[]{:S(2)}, u32[]{:S(2)}) %collective-permute-start.5) | collective-permute-done | bytes 4128 | tf_op jit(solution)/shard_map/ppermute | solution.py:39
  61.1 9.6 %collective-permute-start.6 = (f32[8,128]{1,0:T(8,128)S(1)}, f32[8,128]{1,0:T(8,128)S(1)}, u32[]{:S(2)}, u32[]{:S(2)}) collective-permute-start(f32[8,128]{1,0:T(8,128)S(1)} %add.85), channel_id=1, source_target_pairs={{0,32},{4,36},{8,40},{12,44},{16,48},{20,52},{24,56},{28,60},{32,0... | collective-permute-start | bytes 12296 | tf_op jit(solution)/shard_map/ppermute | solution.py:39
  71.4 4.2 %collective-permute-done.6 = f32[8,128]{1,0:T(8,128)S(1)} collective-permute-done((f32[8,128]{1,0:T(8,128)S(1)}, f32[8,128]{1,0:T(8,128)S(1)}, u32[]{:S(2)}, u32[]{:S(2)}) %collective-permute-start.6) | collective-permute-done | bytes 4128 | tf_op jit(solution)/shard_map/ppermute | solution.py:39
  75.5 0.5 slice.17
  76.1 11.7 %psum.14 = f32[]{:T(128)} all-reduce(f32[]{:T(128)} %bitcast.15), channel_id=1, replica_groups=mesh['island'=4,'fsdp'=32,'tp'=4] {'tp'}, use_global_device_ids=true, to_apply=%region_1.2 | all-reduce | flops 1 | bytes 8 | tf_op jit(solution)/shard_map/psum | solution.py:40
  87.7 5.6 %psum.15 = f32[]{:T(128)} all-reduce(f32[]{:T(128)} %psum.14), channel_id=1, replica_groups={{0,64},{4,68},{8,72},{12,76},{16,80},{20,84},{24,88},{28,92},{32,96},{3..., use_global_device_ids=true, to_apply=%region_2.3 | all-reduce | flops 1 | bytes 8 | tf_op jit(solution)/shard_map/psum | solution.py:40
  94.0 0.0 collective-permute-done.2
  94.0 0.0 collective-permute-done.1
  94.0 0.0 copy-start.5
  94.0 0.7 copy-done.5
  94.7 0.0 collective-permute-done
  94.7 0.0 copy-done.2
  94.7 2.5 %fusion.12 = (bf16[192,1024]{1,0:T(8,128)(2,1)}, f32[192,1024]{1,0:T(8,128)S(1)}) fusion(bf16[192,1024]{1,0:T(8,128)(2,1)S(1)} %copy-done.2, pred[192]{0:T(512)(128)(4,1)S(1)} %broadcast_compare_fusion, bf16[192,1024]{1,0:T(8,128)(2,1)S(1)} %collective-permute-done.2, bf16[192,1024]{1,0:T(8,128)(2,1)} %copy-done.5, ...), kind=kLoop, calls=%fused_computation.30 | loop fusion | flops 3735552 | bytes 3539136 | tf_op jit(solution)/shard_map/convert_element_type | solution.py:167
  97.2 0.0 all-to-all-done.1.m_hbm
  97.2 0.0 all-gather.2.cloned.1.call-done
  97.2 9.3 %shard_map.129 = bf16[8,192,1152]{2,1,0:T(8,128)(2,1)S(1)} custom-call(f32[1]{0:T(128)} %bitcast.16.clip_ref, bf16[512,4096]{1,0:T(8,128)(2,1)} %bitcast.64, bf16[8,192,1280]{2,1,0:T(8,128)(2,1)} %all-to-all-done.1.m_hbm), custom_call_target="tpu_custom_call" | custom-call | flops 3221225472 | bytes 11534336 | tf_op jit(solution)/shard_map/pallas_call | solution.py:103
  106.5 47.3 %all_to_all.20 = bf16[8,192,1152]{2,1,0:T(8,128)(2,1)S(1)} all-to-all(bf16[8,192,1152]{2,1,0:T(8,128)(2,1)S(1)} %shard_map.129), channel_id=1, replica_groups={{0,1,2,3,64,65,66,67},{4,5,6,7,68,69,70,71},{8,9,10,11,72,73,74,75},{12..., dimensions={0} | all-to-all | bytes 7077888 | tf_op jit(solution)/shard_map/all_to_all | solution.py:31
  153.8 0.4 convert_reduce_fusion
  154.3 0.9 fusion.13
  155.2 2.1 %fusion.15 = (bf16[1,192,1024]{2,1,0:T(8,128)(2,1)}, bf16[1,192,1024]{2,1,0:T(8,128)(2,1)}) fusion(bf16[192,1024]{1,0:T(8,128)(2,1)S(1)} %bitcast.66, bf16[192,1024]{1,0:T(8,128)(2,1)S(1)} %bitcast.68, s32[1024]{0:T(1024)S(1)} %get-tuple-element.30, s32[1024]{0:T(1024)S(1)} %get-tuple-element.31, s32[1024]{0:T(1024)S(1)} %get-tuple-element.28, ...), kind=kOutput, calls=%fused_computation.33 | convolution fusion | flops 424935424 | bytes 1993732 | tf_op jit(solution)/shard_map/dot_general | solution.py:173
  (20 shorter events, 0.1 us)
Async XLA Ops:
  7.2 1.2 copy-start
  7.2 90.0 %all-gather.2.cloned.1.call-start = ((), (), s32[]{:S(2)}) async-start(), calls=%async_computation.3 | async-start | bytes 4456448 | tf_op jit(solution)/shard_map/all_gather | solution.py:139
  24.0 1.0 copy-start.1
  27.5 14.3 %copy-start.3 = (bf16[1,192,1024]{2,1,0:T(8,128)(2,1)S(1)}, bf16[1,192,1024]{2,1,0:T(8,128)(2,1)}, u32[]{:S(2)}) copy-start(bf16[1,192,1024]{2,1,0:T(8,128)(2,1)} %param.15) | copy-start | bytes 1179652
  27.5 60.2 %copy-start.6 = (s32[192]{0:T(256)S(1)}, s32[192]{0:T(256)}, u32[]{:S(2)}) copy-start(s32[192]{0:T(256)} %param.17) | copy-start | bytes 2308
  27.5 67.2 %copy-start.2 = (bf16[192,1024]{1,0:T(8,128)(2,1)S(1)}, bf16[192,1024]{1,0:T(8,128)(2,1)}, u32[]{:S(2)}) copy-start(bf16[192,1024]{1,0:T(8,128)(2,1)} %param.16) | copy-start | bytes 1179652
  27.5 67.2 %copy-start.4 = (bf16[1,192,1024]{2,1,0:T(8,128)(2,1)S(1)}, bf16[1,192,1024]{2,1,0:T(8,128)(2,1)}, u32[]{:S(2)}) copy-start(bf16[1,192,1024]{2,1,0:T(8,128)(2,1)} %param.10) | copy-start | bytes 1179652
  27.5 69.7 %all-to-all-start.1 = ((bf16[8,192,1280]{2,1,0:T(8,128)(2,1)}), bf16[8,192,1280]{2,1,0:T(8,128)(2,1)}, u32[]{:S(2)}, u32[]{:S(2)}) async-start(bf16[8,192,1280]{2,1,0:T(8,128)(2,1)} %pad_maximum_fusion), calls=%async_computation.1 | async-start | bytes 7864320 | tf_op jit(solution)/shard_map/all_to_all | solution.py:31
  33.7 5.5 %collective-permute-start.3 = (f32[8,128]{1,0:T(8,128)S(1)}, f32[8,128]{1,0:T(8,128)S(1)}, u32[]{:S(2)}, u32[]{:S(2)}) collective-permute-start(f32[8,128]{1,0:T(8,128)S(1)} %broadcast_in_dim.37), channel_id=1, source_target_pairs={{0,4},{4,0},{8,12},{12,8},{16,20},{20,16},{24,28},{28,24},{32,36},... | collective-permute-start | bytes 12296 | tf_op jit(solution)/shard_map/ppermute | solution.py:39
  39.9 11.1 %collective-permute-start.4 = (f32[8,128]{1,0:T(8,128)S(1)}, f32[8,128]{1,0:T(8,128)S(1)}, u32[]{:S(2)}, u32[]{:S(2)}) collective-permute-start(f32[8,128]{1,0:T(8,128)S(1)} %broadcast_add_fusion), channel_id=1, source_target_pairs={{0,8},{4,12},{8,0},{12,4},{16,24},{20,28},{24,16},{28,20},{32,40},... | collective-permute-start | bytes 12296 | tf_op jit(solution)/shard_map/ppermute | solution.py:39
  41.8 52.2 %collective-permute-start.2 = (bf16[192,1024]{1,0:T(8,128)(2,1)S(1)}, bf16[192,1024]{1,0:T(8,128)(2,1)S(1)}, u32[]{:S(2)}, u32[]{:S(2)}) collective-permute-start(bf16[192,1024]{1,0:T(8,128)(2,1)S(1)} %bitcast.60), channel_id=1, source_target_pairs={{0,384},{128,256},{256,128},{384,0},{1,385},{129,257},{257,129},{3... | collective-permute-start | bytes 1179656 | tf_op jit(solution)/shard_map/ppermute | solution.py:159
  44.0 50.0 %collective-permute-start.1 = (bf16[192,1024]{1,0:T(8,128)(2,1)S(1)}, bf16[192,1024]{1,0:T(8,128)(2,1)S(1)}, u32[]{:S(2)}, u32[]{:S(2)}) collective-permute-start(bf16[192,1024]{1,0:T(8,128)(2,1)S(1)} %bitcast.61), channel_id=1, source_target_pairs={{0,256},{128,384},{256,0},{384,128},{1,257},{129,385},{257,1},{385... | collective-permute-start | bytes 1179656 | tf_op jit(solution)/shard_map/ppermute | solution.py:159
  48.5 46.2 %collective-permute-start = (bf16[192,1024]{1,0:T(8,128)(2,1)S(1)}, bf16[192,1024]{1,0:T(8,128)(2,1)}, u32[]{:S(2)}, u32[]{:S(2)}) collective-permute-start(bf16[192,1024]{1,0:T(8,128)(2,1)S(1)} %bitcast.62), channel_id=1, source_target_pairs={{0,128},{128,0},{256,384},{384,256},{1,129},{129,1},{257,385},{385... | collective-permute-start | bytes 1179656 | tf_op jit(solution)/shard_map/ppermute | solution.py:159
  51.6 9.5 %collective-permute-start.5 = (f32[8,128]{1,0:T(8,128)S(1)}, f32[8,128]{1,0:T(8,128)S(1)}, u32[]{:S(2)}, u32[]{:S(2)}) collective-permute-start(f32[8,128]{1,0:T(8,128)S(1)} %fusion.33), channel_id=1, source_target_pairs={{0,16},{4,20},{8,24},{12,28},{16,0},{20,4},{24,8},{28,12},{32,48},... | collective-permute-start | bytes 12296 | tf_op jit(solution)/shard_map/ppermute | solution.py:39
  61.1 14.4 %collective-permute-start.6 = (f32[8,128]{1,0:T(8,128)S(1)}, f32[8,128]{1,0:T(8,128)S(1)}, u32[]{:S(2)}, u32[]{:S(2)}) collective-permute-start(f32[8,128]{1,0:T(8,128)S(1)} %add.85), channel_id=1, source_target_pairs={{0,32},{4,36},{8,40},{12,44},{16,48},{20,52},{24,56},{28,60},{32,0... | collective-permute-start | bytes 12296 | tf_op jit(solution)/shard_map/ppermute | solution.py:39
  94.0 0.7 copy-start.5
  153.8 1.3 copy-start.7
  153.8 1.3 copy-start.8
Sparse Core Ops, SparseCore 0:
  21.8 75.3 all-gather.1

commit v5 on v4

--- a/solution.py
+++ b/solution.py
@@ -48,46 +48,63 @@
     return (row == swapped).astype(jnp.bfloat16)
 
 
-def core_kernel(clip_ref, b_hbm, m_hbm, out_hbm, b_ref, m_ref, dir_ref, out_ref, b_sem, m_sem, out_sem):
+def core_kernel(
+    clip_ref, b_hbm, m_hbm, out_hbm, b_ref, a_ref, m_ref, dir_ref, out_ref, b_sem, a_sem, m_sem, out_sem
+):
     clip = clip_ref[0]
     b_copies = []
+    a_copies = []
     m_copies = []
     for t in range(XS):
-        b_copies.append(
-            pltpu.make_async_copy(b_hbm.at[:, pl.ds(t * 1024, 1024)], b_ref.at[t], b_sem.at[t])
-        )
-        b_copies[t].start()
-        for u in range(YS):
+        lanes = pl.ds(t * 1024, 1024)
+        b_copies.append(pltpu.make_async_copy(b_hbm.at[:, lanes], b_ref.at[:, lanes], b_sem.at[t]))
+        b_copies[-1].start()
+        for u in range(YS):
+            at = u * XS + t
+            a_copies.append(
+                pltpu.make_async_copy(
+                    m_hbm.at[at, :, pl.ds(0, 1024)], a_ref.at[pl.ds(u * 192, 192), lanes], a_sem.at[at]
+                )
+            )
+            a_copies[-1].start()
+    for t in range(XS):
+        for u in range(YS):
+            at = u * XS + t
             m_copies.append(
                 pltpu.make_async_copy(
-                    m_hbm.at[u * XS + t], m_ref.at[t, pl.ds(u * 192, 192)], m_sem.at[t * YS + u]
+                    m_hbm.at[at, :, pl.ds(1024, 256)], m_ref.at[t, pl.ds(u * 192, 192)], m_sem.at[at]
                 )
             )
-            m_copies[t * YS + u].start()
-    acc = jnp.zeros((384, 512), jnp.float32)
+            m_copies[-1].start()
+    acc = None
     for t in range(XS):
         b_copies[t].wait()
         for u in range(YS):
-            m_copies[t * YS + u].wait()
-        acc = acc + lax.dot_general(
-            m_ref[t, :, 0:1024],
-            b_ref[t],
+            a_copies[t * YS + u].wait()
+        part = lax.dot_general(
+            a_ref[:, t * 1024 : (t + 1) * 1024],
+            b_ref[:, t * 1024 : (t + 1) * 1024],
             (((1,), (1,)), ((), ())),
             preferred_element_type=jnp.float32,
         )
+        acc = part if acc is None else acc + part
+    for copy in m_copies:
+        copy.wait()
     for t in range(XS):
         rotated = acc[:, t * 128 : (t + 1) * 128]
         for u in range(YS):
             out_ref[u * XS + t, :, 1024:1152] = rotated[u * 192 : (u + 1) * 192].astype(jnp.bfloat16)
         scaled = clip * rotated
-        first = m_ref[t, :, 1024:1152].astype(jnp.float32)
-        second = m_ref[t, :, 1152:1280].astype(jnp.float32)
+        first = m_ref[t, :, 0:128].astype(jnp.float32)
+        second = m_ref[t, :, 128:256].astype(jnp.float32)
         first = beta_first * first + (1.0 - beta_first) * scaled
         second = beta_second * second + (1.0 - beta_second) * scaled * scaled
         dir_ref[:, t * 128 : (t + 1) * 128] = (first / (jnp.sqrt(second) + adam_epsilon)).astype(jnp.bfloat16)
     out_copies = []
     for t in range(XS):
-        update = jnp.dot(dir_ref[...], b_ref[t], preferred_element_type=jnp.float32).astype(jnp.bfloat16)
+        update = jnp.dot(
+            dir_ref[...], b_ref[:, t * 1024 : (t + 1) * 1024], preferred_element_type=jnp.float32
+        ).astype(jnp.bfloat16)
         for u in range(YS):
             at = u * XS + t
             out_ref[at, :, 0:1024] = update[u * 192 : (u + 1) * 192]
@@ -106,11 +123,13 @@
         in_specs=[smem, hbm, hbm],
         out_specs=hbm,
         scratch_shapes=[
-            pltpu.VMEM((XS, 512, 1024), jnp.bfloat16),
-            pltpu.VMEM((XS, 384, 1280), jnp.bfloat16),
+            pltpu.VMEM((512, K), jnp.bfloat16),
+            pltpu.VMEM((384, K), jnp.bfloat16),
+            pltpu.VMEM((XS, 384, 256), jnp.bfloat16),
             pltpu.VMEM((384, 512), jnp.bfloat16),
             pltpu.VMEM((PLANE, 192, 1152), jnp.bfloat16),
             pltpu.SemaphoreType.DMA((XS,)),
+            pltpu.SemaphoreType.DMA((PLANE,)),
             pltpu.SemaphoreType.DMA((PLANE,)),
             pltpu.SemaphoreType.DMA((PLANE,)),
         ],

time: 165 us -> 165 us (level)
  no operation moved by 1% of the time
where the time goes in v5:
time: 165 us; the launch traced here: 164 us
  blocking collectives  76.9 us (47%)
  starting transfers between devices  29.3 us (18%)
  between operations  16.4 us (10%)
  waiting for transfers between devices  15.3 us (9%)
  Pallas kernels  9.53 us (6%)
  other arithmetic  8.02 us (5%)
  local copies, waits for them, and re-layouts  4.63 us (3%)
  matrix products  4.32 us (3%)
    all_to_all x2, blocking collectives, plane_exchange(): lax.all_to_all(value, BOTH, split_axis=0, concat_axis=0, axis_index_group...  59.7 us
    ppermute x4, starting transfers between devices, total_squares(): lax.ppermute(total, 'fsdp', [(f, f ^ bit) for f in range(YS * ZS)])  15.5 us
    ppermute x4, waiting for transfers between devices, total_squares(): lax.ppermute(total, 'fsdp', [(f, f ^ bit) for f in range(YS * ZS)])  15.3 us
    psum x1, blocking collectives, total_squares(): lax.psum(total[0, 0], 'tp')  11.7 us
    pallas_call x1, Pallas kernels, core(): pl.pallas_call(core_kernel, out_shape=jax.ShapeDtypeStruct((PLANE, 192, 1...  9.53 us
    ppermute x3, starting transfers between devices, on_device(): lax.ppermute(delta, 'island', [(i, i ^ bit) for i in range(4)])  9.09 us
    psum x1, blocking collectives, total_squares(): lax.psum(lax.psum(total[0, 0], 'tp'), 'fsdp', axis_index_groups=Y_GROUPS)  5.56 us
    all_to_all x1, starting transfers between devices, plane_exchange(): lax.all_to_all(value, BOTH, split_axis=0, concat_axis=0, axis_index_group...  4.67 us
  transfers between devices with their start and end apart: 9, of which 3 were waited for; matrix products, arithmetic and copies ran while one was open for 7% of the time, Pallas kernels for 0%

profile of v5, /device:TPU:224, one launch (start us, length us, event | category | flops | bytes accessed | tf_op | source)
XLA Modules:
  0.0 164.4 jit_solution(15178210013379915079)
XLA Ops:
  7.2 0.0 copy-start
  7.2 0.0 all-gather.2.cloned.1.call-start
  8.0 0.5 copy-done
  8.4 0.1 copy.17
  8.6 12.4 %all_to_all.19 = bf16[8,16,1024]{2,1,0:T(8,128)(2,1)S(1)} all-to-all(bf16[8,16,1024]{2,1,0:T(8,128)(2,1)S(1)} %bitcast.58), channel_id=1, replica_groups={{0,1,2,3,64,65,66,67},{4,5,6,7,68,69,70,71},{8,9,10,11,72,73,74,75},{12..., dimensions={0} | all-to-all | bytes 524288 | tf_op jit(solution)/shard_map/all_to_all | solution.py:31
  21.0 0.7 copy.21
  21.7 0.0 all-gather.2.cloned.1.call-update
  21.8 2.2 %fusion.5 = bf16[48,8,8,128]{3,1,2,0:T(8,128)(2,1)S(1)} fusion(bf16[192,1024]{1,0:T(8,128)(2,1)} %bitcast.65, bf16[192,1024]{1,0:T(8,128)(2,1)} %bitcast.67, s32[1024]{0:T(1024)S(1)} %get-tuple-element.30, s32[1024]{0:T(1024)S(1)} %get-tuple-element.31, s32[1024]{0:T(1024)S(1)} %get-tuple-element.28, s32[1024]{0:T(1024)S(1)} %get-tuple-element.34, ...), kind=kOutput, calls=%fused_computation.13 | convolution fusion | flops 827195392 | bytes 1600512 | tf_op jit(solution)/shard_map/dot_general | solution.py:166
  24.0 0.0 copy-start.1
  24.0 0.2 copy.23
  24.2 0.1 copy.31
  24.4 0.1 slice_bitcast_fusion.2
  24.4 0.6 copy-done.1
  25.0 0.4 broadcast_in_dim.35
  25.4 2.1 %pad_maximum_fusion = bf16[8,192,1280]{2,1,0:T(8,128)(2,1)} fusion(bf16[8,192,128]{2,1,0:T(8,128)(2,1)S(1)} %get-tuple-element.27, bf16[8,192,128]{2,1,0:T(8,128)(2,1)S(1)} %get-tuple-element.26, bf16[8,192,1024]{2,1,0:T(8,128)(2,1)S(1)} %broadcast_in_dim.35), kind=kLoop, calls=%fused_computation.11 | loop fusion | flops 11796480 | bytes 7864320 | tf_op jit(solution)/shard_map/concatenate | solution.py:169
  27.5 4.7 %all-to-all-start.1 = ((bf16[8,192,1280]{2,1,0:T(8,128)(2,1)}), bf16[8,192,1280]{2,1,0:T(8,128)(2,1)}, u32[]{:S(2)}, u32[]{:S(2)}) async-start(bf16[8,192,1280]{2,1,0:T(8,128)(2,1)} %pad_maximum_fusion), calls=%async_computation.1 | async-start | bytes 7864320 | tf_op jit(solution)/shard_map/all_to_all | solution.py:31
  32.2 0.8 multiply_reduce_fusion
  33.0 0.6 broadcast_in_dim.37
  33.7 2.0 %collective-permute-start.3 = (f32[8,128]{1,0:T(8,128)S(1)}, f32[8,128]{1,0:T(8,128)S(1)}, u32[]{:S(2)}, u32[]{:S(2)}) collective-permute-start(f32[8,128]{1,0:T(8,128)S(1)} %broadcast_in_dim.37), channel_id=1, source_target_pairs={{0,4},{4,0},{8,12},{12,8},{16,20},{20,16},{24,28},{28,24},{32,36},... | collective-permute-start | bytes 12296 | tf_op jit(solution)/shard_map/ppermute | solution.py:39
  35.7 3.5 %collective-permute-done.3 = f32[8,128]{1,0:T(8,128)S(1)} collective-permute-done((f32[8,128]{1,0:T(8,128)S(1)}, f32[8,128]{1,0:T(8,128)S(1)}, u32[]{:S(2)}, u32[]{:S(2)}) %collective-permute-start.3) | collective-permute-done | bytes 4128 | tf_op jit(solution)/shard_map/ppermute | solution.py:39
  39.2 0.6 broadcast_add_fusion
  39.9 1.9 %collective-permute-start.4 = (f32[8,128]{1,0:T(8,128)S(1)}, f32[8,128]{1,0:T(8,128)S(1)}, u32[]{:S(2)}, u32[]{:S(2)}) collective-permute-start(f32[8,128]{1,0:T(8,128)S(1)} %broadcast_add_fusion), channel_id=1, source_target_pairs={{0,8},{4,12},{8,0},{12,4},{16,24},{20,28},{24,16},{28,20},{32,40},... | collective-permute-start | bytes 12296 | tf_op jit(solution)/shard_map/ppermute | solution.py:39
  41.8 2.2 %collective-permute-start.2 = (bf16[192,1024]{1,0:T(8,128)(2,1)S(1)}, bf16[192,1024]{1,0:T(8,128)(2,1)S(1)}, u32[]{:S(2)}, u32[]{:S(2)}) collective-permute-start(bf16[192,1024]{1,0:T(8,128)(2,1)S(1)} %bitcast.60), channel_id=1, source_target_pairs={{0,384},{128,256},{256,128},{384,0},{1,385},{129,257},{257,129},{3... | collective-permute-start | bytes 1179656 | tf_op jit(solution)/shard_map/ppermute | solution.py:178
  44.0 4.5 %collective-permute-start.1 = (bf16[192,1024]{1,0:T(8,128)(2,1)S(1)}, bf16[192,1024]{1,0:T(8,128)(2,1)S(1)}, u32[]{:S(2)}, u32[]{:S(2)}) collective-permute-start(bf16[192,1024]{1,0:T(8,128)(2,1)S(1)} %bitcast.61), channel_id=1, source_target_pairs={{0,256},{128,384},{256,0},{384,128},{1,257},{129,385},{257,1},{385... | collective-permute-start | bytes 1179656 | tf_op jit(solution)/shard_map/ppermute | solution.py:178
  48.5 2.4 %collective-permute-start = (bf16[192,1024]{1,0:T(8,128)(2,1)S(1)}, bf16[192,1024]{1,0:T(8,128)(2,1)}, u32[]{:S(2)}, u32[]{:S(2)}) collective-permute-start(bf16[192,1024]{1,0:T(8,128)(2,1)S(1)} %bitcast.62), channel_id=1, source_target_pairs={{0,128},{128,0},{256,384},{384,256},{1,129},{129,1},{257,385},{385... | collective-permute-start | bytes 1179656 | tf_op jit(solution)/shard_map/ppermute | solution.py:178
  50.9 0.0 collective-permute-done.4
  50.9 0.7 fusion.33
  51.6 1.9 %collective-permute-start.5 = (f32[8,128]{1,0:T(8,128)S(1)}, f32[8,128]{1,0:T(8,128)S(1)}, u32[]{:S(2)}, u32[]{:S(2)}) collective-permute-start(f32[8,128]{1,0:T(8,128)S(1)} %fusion.33), channel_id=1, source_target_pairs={{0,16},{4,20},{8,24},{12,28},{16,0},{20,4},{24,8},{28,12},{32,48},... | collective-permute-start | bytes 12296 | tf_op jit(solution)/shard_map/ppermute | solution.py:39
  53.5 7.6 %collective-permute-done.5 = f32[8,128]{1,0:T(8,128)S(1)} collective-permute-done((f32[8,128]{1,0:T(8,128)S(1)}, f32[8,128]{1,0:T(8,128)S(1)}, u32[]{:S(2)}, u32[]{:S(2)}) %collective-permute-start.5) | collective-permute-done | bytes 4128 | tf_op jit(solution)/shard_map/ppermute | solution.py:39
  61.1 9.6 %collective-permute-start.6 = (f32[8,128]{1,0:T(8,128)S(1)}, f32[8,128]{1,0:T(8,128)S(1)}, u32[]{:S(2)}, u32[]{:S(2)}) collective-permute-start(f32[8,128]{1,0:T(8,128)S(1)} %add.85), channel_id=1, source_target_pairs={{0,32},{4,36},{8,40},{12,44},{16,48},{20,52},{24,56},{28,60},{32,0... | collective-permute-start | bytes 12296 | tf_op jit(solution)/shard_map/ppermute | solution.py:39
  71.4 4.2 %collective-permute-done.6 = f32[8,128]{1,0:T(8,128)S(1)} collective-permute-done((f32[8,128]{1,0:T(8,128)S(1)}, f32[8,128]{1,0:T(8,128)S(1)}, u32[]{:S(2)}, u32[]{:S(2)}) %collective-permute-start.6) | collective-permute-done | bytes 4128 | tf_op jit(solution)/shard_map/ppermute | solution.py:39
  75.5 0.5 slice.17
  76.1 11.7 %psum.14 = f32[]{:T(128)} all-reduce(f32[]{:T(128)} %bitcast.15), channel_id=1, replica_groups=mesh['island'=4,'fsdp'=32,'tp'=4] {'tp'}, use_global_device_ids=true, to_apply=%region_1.2 | all-reduce | flops 1 | bytes 8 | tf_op jit(solution)/shard_map/psum | solution.py:40
  87.7 5.6 %psum.15 = f32[]{:T(128)} all-reduce(f32[]{:T(128)} %psum.14), channel_id=1, replica_groups={{0,64},{4,68},{8,72},{12,76},{16,80},{20,84},{24,88},{28,92},{32,96},{3..., use_global_device_ids=true, to_apply=%region_2.3 | all-reduce | flops 1 | bytes 8 | tf_op jit(solution)/shard_map/psum | solution.py:40
  94.0 0.0 collective-permute-done.2
  94.0 0.0 collective-permute-done.1
  94.0 0.0 copy-start.5
  94.0 0.7 copy-done.5
  94.7 0.0 collective-permute-done
  94.7 0.0 copy-done.2
  94.7 2.5 %fusion.12 = (bf16[192,1024]{1,0:T(8,128)(2,1)}, f32[192,1024]{1,0:T(8,128)S(1)}) fusion(bf16[192,1024]{1,0:T(8,128)(2,1)S(1)} %copy-done.2, pred[192]{0:T(512)(128)(4,1)S(1)} %broadcast_compare_fusion, bf16[192,1024]{1,0:T(8,128)(2,1)S(1)} %collective-permute-done.2, bf16[192,1024]{1,0:T(8,128)(2,1)} %copy-done.5, ...), kind=kLoop, calls=%fused_computation.30 | loop fusion | flops 3735552 | bytes 3539136 | tf_op jit(solution)/shard_map/convert_element_type | solution.py:186
  97.2 0.0 all-to-all-done.1.m_hbm
  97.2 0.0 all-gather.2.cloned.1.call-done
  97.2 9.5 %shard_map.129 = bf16[8,192,1152]{2,1,0:T(8,128)(2,1)S(1)} custom-call(f32[1]{0:T(128)} %bitcast.16.clip_ref, bf16[512,4096]{1,0:T(8,128)(2,1)} %bitcast.64, bf16[8,192,1280]{2,1,0:T(8,128)(2,1)} %all-to-all-done.1.m_hbm), custom_call_target="tpu_custom_call" | custom-call | flops 3221225472 | bytes 11534336 | tf_op jit(solution)/shard_map/pallas_call | solution.py:120
  106.8 47.3 %all_to_all.20 = bf16[8,192,1152]{2,1,0:T(8,128)(2,1)S(1)} all-to-all(bf16[8,192,1152]{2,1,0:T(8,128)(2,1)S(1)} %shard_map.129), channel_id=1, replica_groups={{0,1,2,3,64,65,66,67},{4,5,6,7,68,69,70,71},{8,9,10,11,72,73,74,75},{12..., dimensions={0} | all-to-all | bytes 7077888 | tf_op jit(solution)/shard_map/all_to_all | solution.py:31
  154.1 0.4 convert_reduce_fusion
  154.5 0.9 fusion.13
  155.4 2.1 %fusion.15 = (bf16[1,192,1024]{2,1,0:T(8,128)(2,1)}, bf16[1,192,1024]{2,1,0:T(8,128)(2,1)}) fusion(bf16[192,1024]{1,0:T(8,128)(2,1)S(1)} %bitcast.66, bf16[192,1024]{1,0:T(8,128)(2,1)S(1)} %bitcast.68, s32[1024]{0:T(1024)S(1)} %get-tuple-element.30, s32[1024]{0:T(1024)S(1)} %get-tuple-element.31, s32[1024]{0:T(1024)S(1)} %get-tuple-element.28, ...), kind=kOutput, calls=%fused_computation.33 | convolution fusion | flops 424935424 | bytes 1993732 | tf_op jit(solution)/shard_map/dot_general | solution.py:192
  (20 shorter events, 0.1 us)
Async XLA Ops:
  7.2 1.2 copy-start
  7.2 90.0 %all-gather.2.cloned.1.call-start = ((), (), s32[]{:S(2)}) async-start(), calls=%async_computation.3 | async-start | bytes 4456448 | tf_op jit(solution)/shard_map/all_gather | solution.py:158
  24.0 1.0 copy-start.1
  27.5 14.3 %copy-start.3 = (bf16[1,192,1024]{2,1,0:T(8,128)(2,1)S(1)}, bf16[1,192,1024]{2,1,0:T(8,128)(2,1)}, u32[]{:S(2)}) copy-start(bf16[1,192,1024]{2,1,0:T(8,128)(2,1)} %param.15) | copy-start | bytes 1179652
  27.5 60.2 %copy-start.6 = (s32[192]{0:T(256)S(1)}, s32[192]{0:T(256)}, u32[]{:S(2)}) copy-start(s32[192]{0:T(256)} %param.17) | copy-start | bytes 2308
  27.5 67.2 %copy-start.2 = (bf16[192,1024]{1,0:T(8,128)(2,1)S(1)}, bf16[192,1024]{1,0:T(8,128)(2,1)}, u32[]{:S(2)}) copy-start(bf16[192,1024]{1,0:T(8,128)(2,1)} %param.16) | copy-start | bytes 1179652
  27.5 67.2 %copy-start.4 = (bf16[1,192,1024]{2,1,0:T(8,128)(2,1)S(1)}, bf16[1,192,1024]{2,1,0:T(8,128)(2,1)}, u32[]{:S(2)}) copy-start(bf16[1,192,1024]{2,1,0:T(8,128)(2,1)} %param.10) | copy-start | bytes 1179652
  27.5 69.7 %all-to-all-start.1 = ((bf16[8,192,1280]{2,1,0:T(8,128)(2,1)}), bf16[8,192,1280]{2,1,0:T(8,128)(2,1)}, u32[]{:S(2)}, u32[]{:S(2)}) async-start(bf16[8,192,1280]{2,1,0:T(8,128)(2,1)} %pad_maximum_fusion), calls=%async_computation.1 | async-start | bytes 7864320 | tf_op jit(solution)/shard_map/all_to_all | solution.py:31
  33.7 5.5 %collective-permute-start.3 = (f32[8,128]{1,0:T(8,128)S(1)}, f32[8,128]{1,0:T(8,128)S(1)}, u32[]{:S(2)}, u32[]{:S(2)}) collective-permute-start(f32[8,128]{1,0:T(8,128)S(1)} %broadcast_in_dim.37), channel_id=1, source_target_pairs={{0,4},{4,0},{8,12},{12,8},{16,20},{20,16},{24,28},{28,24},{32,36},... | collective-permute-start | bytes 12296 | tf_op jit(solution)/shard_map/ppermute | solution.py:39
  39.9 11.1 %collective-permute-start.4 = (f32[8,128]{1,0:T(8,128)S(1)}, f32[8,128]{1,0:T(8,128)S(1)}, u32[]{:S(2)}, u32[]{:S(2)}) collective-permute-start(f32[8,128]{1,0:T(8,128)S(1)} %broadcast_add_fusion), channel_id=1, source_target_pairs={{0,8},{4,12},{8,0},{12,4},{16,24},{20,28},{24,16},{28,20},{32,40},... | collective-permute-start | bytes 12296 | tf_op jit(solution)/shard_map/ppermute | solution.py:39
  41.8 52.2 %collective-permute-start.2 = (bf16[192,1024]{1,0:T(8,128)(2,1)S(1)}, bf16[192,1024]{1,0:T(8,128)(2,1)S(1)}, u32[]{:S(2)}, u32[]{:S(2)}) collective-permute-start(bf16[192,1024]{1,0:T(8,128)(2,1)S(1)} %bitcast.60), channel_id=1, source_target_pairs={{0,384},{128,256},{256,128},{384,0},{1,385},{129,257},{257,129},{3... | collective-permute-start | bytes 1179656 | tf_op jit(solution)/shard_map/ppermute | solution.py:178
  44.0 50.0 %collective-permute-start.1 = (bf16[192,1024]{1,0:T(8,128)(2,1)S(1)}, bf16[192,1024]{1,0:T(8,128)(2,1)S(1)}, u32[]{:S(2)}, u32[]{:S(2)}) collective-permute-start(bf16[192,1024]{1,0:T(8,128)(2,1)S(1)} %bitcast.61), channel_id=1, source_target_pairs={{0,256},{128,384},{256,0},{384,128},{1,257},{129,385},{257,1},{385... | collective-permute-start | bytes 1179656 | tf_op jit(solution)/shard_map/ppermute | solution.py:178
  48.5 46.2 %collective-permute-start = (bf16[192,1024]{1,0:T(8,128)(2,1)S(1)}, bf16[192,1024]{1,0:T(8,128)(2,1)}, u32[]{:S(2)}, u32[]{:S(2)}) collective-permute-start(bf16[192,1024]{1,0:T(8,128)(2,1)S(1)} %bitcast.62), channel_id=1, source_target_pairs={{0,128},{128,0},{256,384},{384,256},{1,129},{129,1},{257,385},{385... | collective-permute-start | bytes 1179656 | tf_op jit(solution)/shard_map/ppermute | solution.py:178
  51.6 9.5 %collective-permute-start.5 = (f32[8,128]{1,0:T(8,128)S(1)}, f32[8,128]{1,0:T(8,128)S(1)}, u32[]{:S(2)}, u32[]{:S(2)}) collective-permute-start(f32[8,128]{1,0:T(8,128)S(1)} %fusion.33), channel_id=1, source_target_pairs={{0,16},{4,20},{8,24},{12,28},{16,0},{20,4},{24,8},{28,12},{32,48},... | collective-permute-start | bytes 12296 | tf_op jit(solution)/shard_map/ppermute | solution.py:39
  61.1 14.4 %collective-permute-start.6 = (f32[8,128]{1,0:T(8,128)S(1)}, f32[8,128]{1,0:T(8,128)S(1)}, u32[]{:S(2)}, u32[]{:S(2)}) collective-permute-start(f32[8,128]{1,0:T(8,128)S(1)} %add.85), channel_id=1, source_target_pairs={{0,32},{4,36},{8,40},{12,44},{16,48},{20,52},{24,56},{28,60},{32,0... | collective-permute-start | bytes 12296 | tf_op jit(solution)/shard_map/ppermute | solution.py:39
  94.0 0.7 copy-start.5
  154.1 1.3 copy-start.7
  154.1 1.3 copy-start.8
Sparse Core Ops, SparseCore 0:
  21.8 75.3 all-gather.1

commit v6 on v5

--- a/solution.py
+++ b/solution.py
@@ -57,10 +57,12 @@
     m_copies = []
     for t in range(XS):
         lanes = pl.ds(t * 1024, 1024)
-        b_copies.append(pltpu.make_async_copy(b_hbm.at[:, lanes], b_ref.at[:, lanes], b_sem.at[t]))
-        b_copies[-1].start()
         for u in range(YS):
             at = u * XS + t
+            b_copies.append(
+                pltpu.make_async_copy(b_hbm.at[:, at], b_ref.at[u, :, :, lanes], b_sem.at[at])
+            )
+            b_copies[-1].start()
             a_copies.append(
                 pltpu.make_async_copy(
                     m_hbm.at[at, :, pl.ds(0, 1024)], a_ref.at[pl.ds(u * 192, 192), lanes], a_sem.at[at]
@@ -78,12 +80,12 @@
             m_copies[-1].start()
     acc = None
     for t in range(XS):
-        b_copies[t].wait()
-        for u in range(YS):
+        for u in range(YS):
+            b_copies[t * YS + u].wait()
             a_copies[t * YS + u].wait()
         part = lax.dot_general(
             a_ref[:, t * 1024 : (t + 1) * 1024],
-            b_ref[:, t * 1024 : (t + 1) * 1024],
+            b_ref[:, :, :, t * 1024 : (t + 1) * 1024].reshape(512, 1024),
             (((1,), (1,)), ((), ())),
             preferred_element_type=jnp.float32,
         )
@@ -103,7 +105,9 @@
     out_copies = []
     for t in range(XS):
         update = jnp.dot(
-            dir_ref[...], b_ref[:, t * 1024 : (t + 1) * 1024], preferred_element_type=jnp.float32
+            dir_ref[...],
+            b_ref[:, :, :, t * 1024 : (t + 1) * 1024].reshape(512, 1024),
+            preferred_element_type=jnp.float32
         ).astype(jnp.bfloat16)
         for u in range(YS):
             at = u * XS + t
@@ -123,12 +127,12 @@
         in_specs=[smem, hbm, hbm],
         out_specs=hbm,
         scratch_shapes=[
-            pltpu.VMEM((512, K), jnp.bfloat16),
+            pltpu.VMEM((YS, ZS, 16, K), jnp.bfloat16),
             pltpu.VMEM((384, K), jnp.bfloat16),
             pltpu.VMEM((XS, 384, 256), jnp.bfloat16),
             pltpu.VMEM((384, 512), jnp.bfloat16),
             pltpu.VMEM((PLANE, 192, 1152), jnp.bfloat16),
-            pltpu.SemaphoreType.DMA((XS,)),
+            pltpu.SemaphoreType.DMA((PLANE,)),
             pltpu.SemaphoreType.DMA((PLANE,)),
             pltpu.SemaphoreType.DMA((PLANE,)),
             pltpu.SemaphoreType.DMA((PLANE,)),
@@ -154,9 +158,8 @@
 ):
     chosen = lax.dynamic_index_in_dim(bases[0], block_map[0], 0, keepdims=False)
     mixed = plane_exchange(chosen.T)
-    mixed = mixed.reshape(YS, XS, 16, 1024).transpose(0, 2, 1, 3).reshape(YS, 16, K)
-    basis = lax.all_gather(mixed, "fsdp", axis=1, axis_index_groups=Z_GROUPS, tiled=True)
-    basis = basis.reshape(512, K)
+    basis = lax.all_gather(mixed, "fsdp", axis=0, axis_index_groups=Z_GROUPS, tiled=True)
+    basis = basis.reshape(ZS, PLANE, 16, 1024)
     mixed, grad, first, second = lax.optimization_barrier(
         (mixed, grads[0], first_moment[0], second_moment[0])
     )

time: 165 us -> 164 us (level)
  the two profiles are of different devices: /device:TPU:224 before, /device:TPU:416 now
where the time goes in v6:
time: 164 us; the launch traced here: 163 us
  blocking collectives  75.7 us (46%)
  starting transfers between devices  32 us (20%)
  between operations  16.4 us (10%)
  waiting for transfers between devices  13.9 us (8%)
  Pallas kernels  9.23 us (6%)
  other arithmetic  8.02 us (5%)
  matrix products  4.32 us (3%)
  local copies, waits for them, and re-layouts  3.91 us (2%)
    all_to_all x2, blocking collectives, plane_exchange(): lax.all_to_all(value, BOTH, split_axis=0, concat_axis=0, axis_index_group...  58.3 us
    ppermute x4, starting transfers between devices, total_squares(): lax.ppermute(total, 'fsdp', [(f, f ^ bit) for f in range(YS * ZS)])  18.2 us
    ppermute x4, waiting for transfers between devices, total_squares(): lax.ppermute(total, 'fsdp', [(f, f ^ bit) for f in range(YS * ZS)])  13.9 us
    psum x1, blocking collectives, total_squares(): lax.psum(total[0, 0], 'tp')  11.8 us
    pallas_call x1, Pallas kernels, core(): pl.pallas_call(core_kernel, out_shape=jax.ShapeDtypeStruct((PLANE, 192, 1...  9.23 us
    ppermute x3, starting transfers between devices, on_device(): lax.ppermute(delta, 'island', [(i, i ^ bit) for i in range(4)])  9.09 us
    psum x1, blocking collectives, total_squares(): lax.psum(lax.psum(total[0, 0], 'tp'), 'fsdp', axis_index_groups=Y_GROUPS)  5.56 us
    all_to_all x1, starting transfers between devices, plane_exchange(): lax.all_to_all(value, BOTH, split_axis=0, concat_axis=0, axis_index_group...  4.67 us
  transfers between devices with their start and end apart: 9, of which 3 were waited for; matrix products, arithmetic and copies ran while one was open for 7% of the time, Pallas kernels for 0%

profile of v6, /device:TPU:416, one launch (start us, length us, event | category | flops | bytes accessed | tf_op | source)
XLA Modules:
  0.0 163.3 jit_solution(1875727201779944368)
XLA Ops:
  7.2 0.0 copy-start
  7.2 0.0 all-gather.2.cloned.1.call-start
  8.0 0.5 copy-done
  8.4 0.1 copy.14
  8.6 12.5 %all_to_all.22 = bf16[8,16,1024]{2,1,0:T(8,128)(2,1)} all-to-all(bf16[8,16,1024]{2,1,0:T(8,128)(2,1)S(1)} %bitcast.54), channel_id=1, replica_groups={{0,1,2,3,64,65,66,67},{4,5,6,7,68,69,70,71},{8,9,10,11,72,73,74,75},{12..., dimensions={0} | all-to-all | bytes 524288 | tf_op jit(solution)/shard_map/all_to_all | solution.py:31
  21.1 0.0 all-gather.2.cloned.1.call-update
  21.2 2.2 %fusion.5 = bf16[48,8,8,128]{3,1,2,0:T(8,128)(2,1)S(1)} fusion(bf16[192,1024]{1,0:T(8,128)(2,1)} %bitcast.60, bf16[192,1024]{1,0:T(8,128)(2,1)} %bitcast.62, s32[1024]{0:T(1024)S(1)} %get-tuple-element.30, s32[1024]{0:T(1024)S(1)} %get-tuple-element.31, s32[1024]{0:T(1024)S(1)} %get-tuple-element.28, s32[1024]{0:T(1024)S(1)} %get-tuple-element.34, ...), kind=kOutput, calls=%fused_computation.13 | convolution fusion | flops 827195392 | bytes 1600512 | tf_op jit(solution)/shard_map/dot_general | solution.py:169
  23.4 0.0 copy-start.1
  23.4 0.2 copy.18
  23.6 0.1 copy.26
  23.8 0.1 slice_bitcast_fusion.2
  23.8 0.6 copy-done.1
  24.4 0.4 broadcast_in_dim.35
  24.8 2.1 %pad_maximum_fusion = bf16[8,192,1280]{2,1,0:T(8,128)(2,1)} fusion(bf16[8,192,128]{2,1,0:T(8,128)(2,1)S(1)} %get-tuple-element.27, bf16[8,192,128]{2,1,0:T(8,128)(2,1)S(1)} %get-tuple-element.26, bf16[8,192,1024]{2,1,0:T(8,128)(2,1)S(1)} %broadcast_in_dim.35), kind=kLoop, calls=%fused_computation.11 | loop fusion | flops 11796480 | bytes 7864320 | tf_op jit(solution)/shard_map/concatenate | solution.py:172
  26.9 4.7 %all-to-all-start.1 = ((bf16[8,192,1280]{2,1,0:T(8,128)(2,1)}), bf16[8,192,1280]{2,1,0:T(8,128)(2,1)}, u32[]{:S(2)}, u32[]{:S(2)}) async-start(bf16[8,192,1280]{2,1,0:T(8,128)(2,1)} %pad_maximum_fusion), calls=%async_computation.1 | async-start | bytes 7864320 | tf_op jit(solution)/shard_map/all_to_all | solution.py:31
  31.6 0.8 multiply_reduce_fusion
  32.4 0.6 broadcast_in_dim.37
  33.1 2.9 %collective-permute-start.3 = (f32[8,128]{1,0:T(8,128)S(1)}, f32[8,128]{1,0:T(8,128)S(1)}, u32[]{:S(2)}, u32[]{:S(2)}) collective-permute-start(f32[8,128]{1,0:T(8,128)S(1)} %broadcast_in_dim.37), channel_id=1, source_target_pairs={{0,4},{4,0},{8,12},{12,8},{16,20},{20,16},{24,28},{28,24},{32,36},... | collective-permute-start | bytes 12296 | tf_op jit(solution)/shard_map/ppermute | solution.py:39
  36.0 2.6 %collective-permute-done.3 = f32[8,128]{1,0:T(8,128)S(1)} collective-permute-done((f32[8,128]{1,0:T(8,128)S(1)}, f32[8,128]{1,0:T(8,128)S(1)}, u32[]{:S(2)}, u32[]{:S(2)}) %collective-permute-start.3) | collective-permute-done | bytes 4128 | tf_op jit(solution)/shard_map/ppermute | solution.py:39
  38.6 0.6 broadcast_add_fusion
  39.2 3.4 %collective-permute-start.4 = (f32[8,128]{1,0:T(8,128)S(1)}, f32[8,128]{1,0:T(8,128)S(1)}, u32[]{:S(2)}, u32[]{:S(2)}) collective-permute-start(f32[8,128]{1,0:T(8,128)S(1)} %broadcast_add_fusion), channel_id=1, source_target_pairs={{0,8},{4,12},{8,0},{12,4},{16,24},{20,28},{24,16},{28,20},{32,40},... | collective-permute-start | bytes 12296 | tf_op jit(solution)/shard_map/ppermute | solution.py:39
  42.7 0.0 copy-done.3
  42.7 1.9 %collective-permute-start.2 = (bf16[192,1024]{1,0:T(8,128)(2,1)S(1)}, bf16[192,1024]{1,0:T(8,128)(2,1)S(1)}, u32[]{:S(2)}, u32[]{:S(2)}) collective-permute-start(bf16[192,1024]{1,0:T(8,128)(2,1)S(1)} %bitcast.55), channel_id=1, source_target_pairs={{0,384},{128,256},{256,128},{384,0},{1,385},{129,257},{257,129},{3... | collective-permute-start | bytes 1179656 | tf_op jit(solution)/shard_map/ppermute | solution.py:181
  44.6 4.8 %collective-permute-start.1 = (bf16[192,1024]{1,0:T(8,128)(2,1)S(1)}, bf16[192,1024]{1,0:T(8,128)(2,1)S(1)}, u32[]{:S(2)}, u32[]{:S(2)}) collective-permute-start(bf16[192,1024]{1,0:T(8,128)(2,1)S(1)} %bitcast.56), channel_id=1, source_target_pairs={{0,256},{128,384},{256,0},{384,128},{1,257},{129,385},{257,1},{385... | collective-permute-start | bytes 1179656 | tf_op jit(solution)/shard_map/ppermute | solution.py:181
  49.4 2.4 %collective-permute-start = (bf16[192,1024]{1,0:T(8,128)(2,1)S(1)}, bf16[192,1024]{1,0:T(8,128)(2,1)}, u32[]{:S(2)}, u32[]{:S(2)}) collective-permute-start(bf16[192,1024]{1,0:T(8,128)(2,1)S(1)} %bitcast.57), channel_id=1, source_target_pairs={{0,128},{128,0},{256,384},{384,256},{1,129},{129,1},{257,385},{385... | collective-permute-start | bytes 1179656 | tf_op jit(solution)/shard_map/ppermute | solution.py:181
  51.8 0.0 collective-permute-done.4
  51.8 0.7 fusion.33
  52.5 5.4 %collective-permute-start.5 = (f32[8,128]{1,0:T(8,128)S(1)}, f32[8,128]{1,0:T(8,128)S(1)}, u32[]{:S(2)}, u32[]{:S(2)}) collective-permute-start(f32[8,128]{1,0:T(8,128)S(1)} %fusion.33), channel_id=1, source_target_pairs={{0,16},{4,20},{8,24},{12,28},{16,0},{20,4},{24,8},{28,12},{32,48},... | collective-permute-start | bytes 12296 | tf_op jit(solution)/shard_map/ppermute | solution.py:39
  57.9 4.0 %collective-permute-done.5 = f32[8,128]{1,0:T(8,128)S(1)} collective-permute-done((f32[8,128]{1,0:T(8,128)S(1)}, f32[8,128]{1,0:T(8,128)S(1)}, u32[]{:S(2)}, u32[]{:S(2)}) %collective-permute-start.5) | collective-permute-done | bytes 4128 | tf_op jit(solution)/shard_map/ppermute | solution.py:39
  61.9 6.4 %collective-permute-start.6 = (f32[8,128]{1,0:T(8,128)S(1)}, f32[8,128]{1,0:T(8,128)S(1)}, u32[]{:S(2)}, u32[]{:S(2)}) collective-permute-start(f32[8,128]{1,0:T(8,128)S(1)} %add.85), channel_id=1, source_target_pairs={{0,32},{4,36},{8,40},{12,44},{16,48},{20,52},{24,56},{28,60},{32,0... | collective-permute-start | bytes 12296 | tf_op jit(solution)/shard_map/ppermute | solution.py:39
  68.9 7.3 %collective-permute-done.6 = f32[8,128]{1,0:T(8,128)S(1)} collective-permute-done((f32[8,128]{1,0:T(8,128)S(1)}, f32[8,128]{1,0:T(8,128)S(1)}, u32[]{:S(2)}, u32[]{:S(2)}) %collective-permute-start.6) | collective-permute-done | bytes 4128 | tf_op jit(solution)/shard_map/ppermute | solution.py:39
  76.2 0.5 slice.17
  76.7 11.8 %psum.14 = f32[]{:T(128)} all-reduce(f32[]{:T(128)} %bitcast.14), channel_id=1, replica_groups=mesh['island'=4,'fsdp'=32,'tp'=4] {'tp'}, use_global_device_ids=true, to_apply=%region_1.2 | all-reduce | flops 1 | bytes 8 | tf_op jit(solution)/shard_map/psum | solution.py:40
  88.5 0.0 copy-done.6
  88.5 5.6 %psum.15 = f32[]{:T(128)} all-reduce(f32[]{:T(128)} %psum.14), channel_id=1, replica_groups={{0,64},{4,68},{8,72},{12,76},{16,80},{20,84},{24,88},{28,92},{32,96},{3..., use_global_device_ids=true, to_apply=%region_2.3 | all-reduce | flops 1 | bytes 8 | tf_op jit(solution)/shard_map/psum | solution.py:40
  94.7 0.0 collective-permute-done.2
  94.8 0.0 collective-permute-done.1
  94.8 0.0 copy-start.5
  94.8 0.7 copy-done.5
  95.5 0.0 collective-permute-done
  95.5 2.5 %fusion.12 = (bf16[192,1024]{1,0:T(8,128)(2,1)}, f32[192,1024]{1,0:T(8,128)S(1)}) fusion(bf16[192,1024]{1,0:T(8,128)(2,1)S(1)} %copy-done.2, pred[192]{0:T(512)(128)(4,1)S(1)} %broadcast_compare_fusion, bf16[192,1024]{1,0:T(8,128)(2,1)S(1)} %collective-permute-done.2, bf16[192,1024]{1,0:T(8,128)(2,1)} %copy-done.5, ...), kind=kLoop, calls=%fused_computation.30 | loop fusion | flops 3735552 | bytes 3539136 | tf_op jit(solution)/shard_map/convert_element_type | solution.py:189
  98.0 0.0 all-to-all-done.1.m_hbm
  98.0 9.2 %shard_map.129 = bf16[8,192,1152]{2,1,0:T(8,128)(2,1)S(1)} custom-call(f32[1]{0:T(128)} %bitcast.15.clip_ref, bf16[16,8,16,1024]{3,2,1,0:T(8,128)(2,1)} %bitcast.59, bf16[8,192,1280]{2,1,0:T(8,128)(2,1)} %all-to-all-done.1.m_hbm), custom_call_target="tpu_custom_call" | custom-call | flops 3221225472 | bytes 11534336 | tf_op jit(solution)/shard_map/pallas_call | solution.py:124
  107.2 45.8 %all_to_all.23 = bf16[8,192,1152]{2,1,0:T(8,128)(2,1)S(1)} all-to-all(bf16[8,192,1152]{2,1,0:T(8,128)(2,1)S(1)} %shard_map.129), channel_id=1, replica_groups={{0,1,2,3,64,65,66,67},{4,5,6,7,68,69,70,71},{8,9,10,11,72,73,74,75},{12..., dimensions={0} | all-to-all | bytes 7077888 | tf_op jit(solution)/shard_map/all_to_all | solution.py:31
  153.1 0.4 convert_reduce_fusion
  153.5 0.9 fusion.13
  154.4 0.0 copy-done.8
  154.4 2.1 %fusion.15 = (bf16[1,192,1024]{2,1,0:T(8,128)(2,1)}, bf16[1,192,1024]{2,1,0:T(8,128)(2,1)}) fusion(bf16[192,1024]{1,0:T(8,128)(2,1)S(1)} %bitcast.61, bf16[192,1024]{1,0:T(8,128)(2,1)S(1)} %bitcast.63, s32[1024]{0:T(1024)S(1)} %get-tuple-element.30, s32[1024]{0:T(1024)S(1)} %get-tuple-element.31, s32[1024]{0:T(1024)S(1)} %get-tuple-element.28, ...), kind=kOutput, calls=%fused_computation.33 | convolution fusion | flops 424935424 | bytes 1993732 | tf_op jit(solution)/shard_map/dot_general | solution.py:195
  (19 shorter events, 0.1 us)
Async XLA Ops:
  7.2 1.2 copy-start
  7.2 90.8 %all-gather.2.cloned.1.call-start = ((), (), s32[]{:S(2)}) async-start(), calls=%async_computation.3 | async-start | bytes 4456448 | tf_op jit(solution)/shard_map/all_gather | solution.py:161
  23.4 1.0 copy-start.1
  26.9 15.8 %copy-start.3 = (bf16[1,192,1024]{2,1,0:T(8,128)(2,1)S(1)}, bf16[1,192,1024]{2,1,0:T(8,128)(2,1)}, u32[]{:S(2)}) copy-start(bf16[1,192,1024]{2,1,0:T(8,128)(2,1)} %param.15) | copy-start | bytes 1179652
  26.9 61.6 %copy-start.6 = (s32[192]{0:T(256)S(1)}, s32[192]{0:T(256)}, u32[]{:S(2)}) copy-start(s32[192]{0:T(256)} %param.17) | copy-start | bytes 2308
  26.9 68.6 %copy-start.2 = (bf16[192,1024]{1,0:T(8,128)(2,1)S(1)}, bf16[192,1024]{1,0:T(8,128)(2,1)}, u32[]{:S(2)}) copy-start(bf16[192,1024]{1,0:T(8,128)(2,1)} %param.16) | copy-start | bytes 1179652
  26.9 68.6 %copy-start.4 = (bf16[1,192,1024]{2,1,0:T(8,128)(2,1)S(1)}, bf16[1,192,1024]{2,1,0:T(8,128)(2,1)}, u32[]{:S(2)}) copy-start(bf16[1,192,1024]{2,1,0:T(8,128)(2,1)} %param.10) | copy-start | bytes 1179652
  26.9 71.1 %all-to-all-start.1 = ((bf16[8,192,1280]{2,1,0:T(8,128)(2,1)}), bf16[8,192,1280]{2,1,0:T(8,128)(2,1)}, u32[]{:S(2)}, u32[]{:S(2)}) async-start(bf16[8,192,1280]{2,1,0:T(8,128)(2,1)} %pad_maximum_fusion), calls=%async_computation.1 | async-start | bytes 7864320 | tf_op jit(solution)/shard_map/all_to_all | solution.py:31
  33.1 5.5 %collective-permute-start.3 = (f32[8,128]{1,0:T(8,128)S(1)}, f32[8,128]{1,0:T(8,128)S(1)}, u32[]{:S(2)}, u32[]{:S(2)}) collective-permute-start(f32[8,128]{1,0:T(8,128)S(1)} %broadcast_in_dim.37), channel_id=1, source_target_pairs={{0,4},{4,0},{8,12},{12,8},{16,20},{20,16},{24,28},{28,24},{32,36},... | collective-permute-start | bytes 12296 | tf_op jit(solution)/shard_map/ppermute | solution.py:39
  39.2 12.6 %collective-permute-start.4 = (f32[8,128]{1,0:T(8,128)S(1)}, f32[8,128]{1,0:T(8,128)S(1)}, u32[]{:S(2)}, u32[]{:S(2)}) collective-permute-start(f32[8,128]{1,0:T(8,128)S(1)} %broadcast_add_fusion), channel_id=1, source_target_pairs={{0,8},{4,12},{8,0},{12,4},{16,24},{20,28},{24,16},{28,20},{32,40},... | collective-permute-start | bytes 12296 | tf_op jit(solution)/shard_map/ppermute | solution.py:39
  42.7 52.1 %collective-permute-start.2 = (bf16[192,1024]{1,0:T(8,128)(2,1)S(1)}, bf16[192,1024]{1,0:T(8,128)(2,1)S(1)}, u32[]{:S(2)}, u32[]{:S(2)}) collective-permute-start(bf16[192,1024]{1,0:T(8,128)(2,1)S(1)} %bitcast.55), channel_id=1, source_target_pairs={{0,384},{128,256},{256,128},{384,0},{1,385},{129,257},{257,129},{3... | collective-permute-start | bytes 1179656 | tf_op jit(solution)/shard_map/ppermute | solution.py:181
  44.6 50.2 %collective-permute-start.1 = (bf16[192,1024]{1,0:T(8,128)(2,1)S(1)}, bf16[192,1024]{1,0:T(8,128)(2,1)S(1)}, u32[]{:S(2)}, u32[]{:S(2)}) collective-permute-start(bf16[192,1024]{1,0:T(8,128)(2,1)S(1)} %bitcast.56), channel_id=1, source_target_pairs={{0,256},{128,384},{256,0},{384,128},{1,257},{129,385},{257,1},{385... | collective-permute-start | bytes 1179656 | tf_op jit(solution)/shard_map/ppermute | solution.py:181
  49.4 46.1 %collective-permute-start = (bf16[192,1024]{1,0:T(8,128)(2,1)S(1)}, bf16[192,1024]{1,0:T(8,128)(2,1)}, u32[]{:S(2)}, u32[]{:S(2)}) collective-permute-start(bf16[192,1024]{1,0:T(8,128)(2,1)S(1)} %bitcast.57), channel_id=1, source_target_pairs={{0,128},{128,0},{256,384},{384,256},{1,129},{129,1},{257,385},{385... | collective-permute-start | bytes 1179656 | tf_op jit(solution)/shard_map/ppermute | solution.py:181
  52.5 9.4 %collective-permute-start.5 = (f32[8,128]{1,0:T(8,128)S(1)}, f32[8,128]{1,0:T(8,128)S(1)}, u32[]{:S(2)}, u32[]{:S(2)}) collective-permute-start(f32[8,128]{1,0:T(8,128)S(1)} %fusion.33), channel_id=1, source_target_pairs={{0,16},{4,20},{8,24},{12,28},{16,0},{20,4},{24,8},{28,12},{32,48},... | collective-permute-start | bytes 12296 | tf_op jit(solution)/shard_map/ppermute | solution.py:39
  61.9 14.3 %collective-permute-start.6 = (f32[8,128]{1,0:T(8,128)S(1)}, f32[8,128]{1,0:T(8,128)S(1)}, u32[]{:S(2)}, u32[]{:S(2)}) collective-permute-start(f32[8,128]{1,0:T(8,128)S(1)} %add.85), channel_id=1, source_target_pairs={{0,32},{4,36},{8,40},{12,44},{16,48},{20,52},{24,56},{28,60},{32,0... | collective-permute-start | bytes 12296 | tf_op jit(solution)/shard_map/ppermute | solution.py:39
  94.8 0.7 copy-start.5
  153.1 1.3 copy-start.7
  153.1 1.3 copy-start.8
Sparse Core Ops, SparseCore 0:
  21.2 73.6 all-gather.1

commit v7 on v6

--- a/solution.py
+++ b/solution.py
@@ -137,7 +137,7 @@
             pltpu.SemaphoreType.DMA((PLANE,)),
             pltpu.SemaphoreType.DMA((PLANE,)),
         ],
-        compiler_params=pltpu.CompilerParams(vmem_limit_bytes=48 * 2**20),
+        compiler_params=pltpu.CompilerParams(vmem_limit_bytes=24 * 2**20),
         cost_estimate=pl.CostEstimate(
             flops=4 * 384 * 4096 * 512, bytes_accessed=11 * 2**20, transcendentals=384 * 512
         ),

time: 164 us -> 166 us (1.012)
  local copies, waits for them, and re-layouts: 3.91 us -> 6.09 us
    unnamed x19 -> x21, local copies, waits for them, and re-layouts: 2 us -> 4.18 us
where the time goes in v7:
time: 166 us; the launch traced here: 165 us
  blocking collectives  75.7 us (46%)
  starting transfers between devices  31.9 us (19%)
  between operations  16.4 us (10%)
  waiting for transfers between devices  13.9 us (8%)
  Pallas kernels  8.68 us (5%)
  other arithmetic  8 us (5%)
  local copies, waits for them, and re-layouts  6.09 us (4%)
  matrix products  4.32 us (3%)
    all_to_all x2, blocking collectives, plane_exchange(): lax.all_to_all(value, BOTH, split_axis=0, concat_axis=0, axis_index_group...  58.3 us
    ppermute x4, starting transfers between devices, total_squares(): lax.ppermute(total, 'fsdp', [(f, f ^ bit) for f in range(YS * ZS)])  18.1 us
    ppermute x4, waiting for transfers between devices, total_squares(): lax.ppermute(total, 'fsdp', [(f, f ^ bit) for f in range(YS * ZS)])  13.8 us
    psum x1, blocking collectives, total_squares(): lax.psum(total[0, 0], 'tp')  11.9 us
    ppermute x3, starting transfers between devices, on_device(): lax.ppermute(delta, 'island', [(i, i ^ bit) for i in range(4)])  9.09 us
    pallas_call x1, Pallas kernels, core(): pl.pallas_call(core_kernel, out_shape=jax.ShapeDtypeStruct((PLANE, 192, 1...  8.68 us
    psum x1, blocking collectives, total_squares(): lax.psum(lax.psum(total[0, 0], 'tp'), 'fsdp', axis_index_groups=Y_GROUPS)  5.56 us
    all_to_all x1, starting transfers between devices, plane_exchange(): lax.all_to_all(value, BOTH, split_axis=0, concat_axis=0, axis_index_group...  4.67 us
  transfers between devices with their start and end apart: 9, of which 3 were waited for; matrix products, arithmetic and copies ran while one was open for 7% of the time, Pallas kernels for 0%

profile of v7, /device:TPU:416, one launch (start us, length us, event | category | flops | bytes accessed | tf_op | source)
XLA Modules:
  0.0 164.9 jit_solution(11872497555661810896)
XLA Ops:
  7.2 0.0 copy-start
  7.2 0.0 all-gather.2.cloned.1.call-start
  8.0 0.5 copy-done
  8.4 0.1 copy.14
  8.6 12.5 %all_to_all.22 = bf16[8,16,1024]{2,1,0:T(8,128)(2,1)} all-to-all(bf16[8,16,1024]{2,1,0:T(8,128)(2,1)S(1)} %bitcast.55), channel_id=1, replica_groups={{0,1,2,3,64,65,66,67},{4,5,6,7,68,69,70,71},{8,9,10,11,72,73,74,75},{12..., dimensions={0} | all-to-all | bytes 524288 | tf_op jit(solution)/shard_map/all_to_all | solution.py:31
  21.1 0.0 all-gather.2.cloned.1.call-update
  21.2 2.2 %fusion.5 = bf16[48,8,8,128]{3,1,2,0:T(8,128)(2,1)S(1)} fusion(bf16[192,1024]{1,0:T(8,128)(2,1)} %bitcast.60, bf16[192,1024]{1,0:T(8,128)(2,1)} %bitcast.62, s32[1024]{0:T(1024)S(1)} %get-tuple-element.30, s32[1024]{0:T(1024)S(1)} %get-tuple-element.31, s32[1024]{0:T(1024)S(1)} %get-tuple-element.28, s32[1024]{0:T(1024)S(1)} %get-tuple-element.34, ...), kind=kOutput, calls=%fused_computation.13 | convolution fusion | flops 827195392 | bytes 1600512 | tf_op jit(solution)/shard_map/dot_general | solution.py:169
  23.4 0.0 copy-start.2
  23.4 0.2 copy.18
  23.6 0.1 copy.26
  23.8 0.1 slice_bitcast_fusion.2
  23.8 0.6 copy-done.2
  24.4 0.4 broadcast_in_dim.35
  24.8 2.1 %pad_maximum_fusion = bf16[8,192,1280]{2,1,0:T(8,128)(2,1)} fusion(bf16[8,192,128]{2,1,0:T(8,128)(2,1)S(1)} %get-tuple-element.27, bf16[8,192,128]{2,1,0:T(8,128)(2,1)S(1)} %get-tuple-element.26, bf16[8,192,1024]{2,1,0:T(8,128)(2,1)S(1)} %broadcast_in_dim.35), kind=kLoop, calls=%fused_computation.11 | loop fusion | flops 11796480 | bytes 7864320 | tf_op jit(solution)/shard_map/concatenate | solution.py:172
  26.9 4.7 %all-to-all-start.1 = ((bf16[8,192,1280]{2,1,0:T(8,128)(2,1)}), bf16[8,192,1280]{2,1,0:T(8,128)(2,1)}, u32[]{:S(2)}, u32[]{:S(2)}) async-start(bf16[8,192,1280]{2,1,0:T(8,128)(2,1)} %pad_maximum_fusion), calls=%async_computation.1 | async-start | bytes 7864320 | tf_op jit(solution)/shard_map/all_to_all | solution.py:31
  31.6 0.8 multiply_reduce_fusion
  32.4 0.6 broadcast_in_dim.37
  33.0 2.9 %collective-permute-start.3 = (f32[8,128]{1,0:T(8,128)S(1)}, f32[8,128]{1,0:T(8,128)S(1)}, u32[]{:S(2)}, u32[]{:S(2)}) collective-permute-start(f32[8,128]{1,0:T(8,128)S(1)} %broadcast_in_dim.37), channel_id=1, source_target_pairs={{0,4},{4,0},{8,12},{12,8},{16,20},{20,16},{24,28},{28,24},{32,36},... | collective-permute-start | bytes 12296 | tf_op jit(solution)/shard_map/ppermute | solution.py:39
  36.0 2.6 %collective-permute-done.3 = f32[8,128]{1,0:T(8,128)S(1)} collective-permute-done((f32[8,128]{1,0:T(8,128)S(1)}, f32[8,128]{1,0:T(8,128)S(1)}, u32[]{:S(2)}, u32[]{:S(2)}) %collective-permute-start.3) | collective-permute-done | bytes 4128 | tf_op jit(solution)/shard_map/ppermute | solution.py:39
  38.5 0.6 broadcast_add_fusion
  39.2 3.4 %collective-permute-start.4 = (f32[8,128]{1,0:T(8,128)S(1)}, f32[8,128]{1,0:T(8,128)S(1)}, u32[]{:S(2)}, u32[]{:S(2)}) collective-permute-start(f32[8,128]{1,0:T(8,128)S(1)} %broadcast_add_fusion), channel_id=1, source_target_pairs={{0,8},{4,12},{8,0},{12,4},{16,24},{20,28},{24,16},{28,20},{32,40},... | collective-permute-start | bytes 12296 | tf_op jit(solution)/shard_map/ppermute | solution.py:39
  42.6 1.9 %collective-permute-start.2 = (bf16[192,1024]{1,0:T(8,128)(2,1)S(1)}, bf16[192,1024]{1,0:T(8,128)(2,1)S(1)}, u32[]{:S(2)}, u32[]{:S(2)}) collective-permute-start(bf16[192,1024]{1,0:T(8,128)(2,1)S(1)} %bitcast.56), channel_id=1, source_target_pairs={{0,384},{128,256},{256,128},{384,0},{1,385},{129,257},{257,129},{3... | collective-permute-start | bytes 1179656 | tf_op jit(solution)/shard_map/ppermute | solution.py:181
  44.6 4.8 %collective-permute-start.1 = (bf16[192,1024]{1,0:T(8,128)(2,1)S(1)}, bf16[192,1024]{1,0:T(8,128)(2,1)S(1)}, u32[]{:S(2)}, u32[]{:S(2)}) collective-permute-start(bf16[192,1024]{1,0:T(8,128)(2,1)S(1)} %bitcast.57), channel_id=1, source_target_pairs={{0,256},{128,384},{256,0},{384,128},{1,257},{129,385},{257,1},{385... | collective-permute-start | bytes 1179656 | tf_op jit(solution)/shard_map/ppermute | solution.py:181
  49.4 2.4 %collective-permute-start = (bf16[192,1024]{1,0:T(8,128)(2,1)S(1)}, bf16[192,1024]{1,0:T(8,128)(2,1)}, u32[]{:S(2)}, u32[]{:S(2)}) collective-permute-start(bf16[192,1024]{1,0:T(8,128)(2,1)S(1)} %bitcast.58), channel_id=1, source_target_pairs={{0,128},{128,0},{256,384},{384,256},{1,129},{129,1},{257,385},{385... | collective-permute-start | bytes 1179656 | tf_op jit(solution)/shard_map/ppermute | solution.py:181
  51.8 0.0 collective-permute-done.4
  51.8 0.7 fusion.33
  52.4 5.4 %collective-permute-start.5 = (f32[8,128]{1,0:T(8,128)S(1)}, f32[8,128]{1,0:T(8,128)S(1)}, u32[]{:S(2)}, u32[]{:S(2)}) collective-permute-start(f32[8,128]{1,0:T(8,128)S(1)} %fusion.33), channel_id=1, source_target_pairs={{0,16},{4,20},{8,24},{12,28},{16,0},{20,4},{24,8},{28,12},{32,48},... | collective-permute-start | bytes 12296 | tf_op jit(solution)/shard_map/ppermute | solution.py:39
  57.8 4.0 %collective-permute-done.5 = f32[8,128]{1,0:T(8,128)S(1)} collective-permute-done((f32[8,128]{1,0:T(8,128)S(1)}, f32[8,128]{1,0:T(8,128)S(1)}, u32[]{:S(2)}, u32[]{:S(2)}) %collective-permute-start.5) | collective-permute-done | bytes 4128 | tf_op jit(solution)/shard_map/ppermute | solution.py:39
  61.9 6.4 %collective-permute-start.6 = (f32[8,128]{1,0:T(8,128)S(1)}, f32[8,128]{1,0:T(8,128)S(1)}, u32[]{:S(2)}, u32[]{:S(2)}) collective-permute-start(f32[8,128]{1,0:T(8,128)S(1)} %add.85), channel_id=1, source_target_pairs={{0,32},{4,36},{8,40},{12,44},{16,48},{20,52},{24,56},{28,60},{32,0... | collective-permute-start | bytes 12296 | tf_op jit(solution)/shard_map/ppermute | solution.py:39
  68.9 7.2 %collective-permute-done.6 = f32[8,128]{1,0:T(8,128)S(1)} collective-permute-done((f32[8,128]{1,0:T(8,128)S(1)}, f32[8,128]{1,0:T(8,128)S(1)}, u32[]{:S(2)}, u32[]{:S(2)}) %collective-permute-start.6) | collective-permute-done | bytes 4128 | tf_op jit(solution)/shard_map/ppermute | solution.py:39
  76.1 0.5 slice.17
  76.6 11.9 %psum.14 = f32[]{:T(128)} all-reduce(f32[]{:T(128)} %bitcast.14), channel_id=1, replica_groups=mesh['island'=4,'fsdp'=32,'tp'=4] {'tp'}, use_global_device_ids=true, to_apply=%region_1.2 | all-reduce | flops 1 | bytes 8 | tf_op jit(solution)/shard_map/psum | solution.py:40
  88.5 5.6 %psum.15 = f32[]{:T(128)} all-reduce(f32[]{:T(128)} %psum.14), channel_id=1, replica_groups={{0,64},{4,68},{8,72},{12,76},{16,80},{20,84},{24,88},{28,92},{32,96},{3..., use_global_device_ids=true, to_apply=%region_2.3 | all-reduce | flops 1 | bytes 8 | tf_op jit(solution)/shard_map/psum | solution.py:40
  94.7 0.0 collective-permute-done.2
  94.8 0.0 collective-permute-done.1
  94.8 0.0 copy-start.6
  94.8 0.7 copy-done.6
  95.5 0.0 collective-permute-done
  95.5 0.0 copy-done.3
  95.5 2.5 %fusion.12 = (bf16[192,1024]{1,0:T(8,128)(2,1)}, f32[192,1024]{1,0:T(8,128)S(1)}) fusion(bf16[192,1024]{1,0:T(8,128)(2,1)S(1)} %copy-done.3, pred[192]{0:T(512)(128)(4,1)S(1)} %broadcast_compare_fusion, bf16[192,1024]{1,0:T(8,128)(2,1)S(1)} %collective-permute-done.2, bf16[192,1024]{1,0:T(8,128)(2,1)} %copy-done.6, ...), kind=kLoop, calls=%fused_computation.30 | loop fusion | flops 3735552 | bytes 3539136 | tf_op jit(solution)/shard_map/convert_element_type | solution.py:189
  98.0 0.0 all-to-all-done.1.m_hbm
  98.0 2.2 %copy-done.1 = bf16[2048,1024]{1,0:T(8,128)(2,1)S(1)} copy-done((bf16[2048,1024]{1,0:T(8,128)(2,1)S(1)}, bf16[2048,1024]{1,0:T(8,128)(2,1)}, u32[]{:S(2)}) %copy-start.1) | copy-done | bytes 4194328
  100.2 8.7 %shard_map.129 = bf16[8,192,1152]{2,1,0:T(8,128)(2,1)S(1)} custom-call(f32[1]{0:T(128)} %bitcast.15.clip_ref, bf16[16,8,16,1024]{3,2,1,0:T(8,128)(2,1)S(1)} %bitcast.49, bf16[8,192,1280]{2,1,0:T(8,128)(2,1)} %all-to-all-done.1.m_hbm), custom_call_target="tpu_custom_call" | custom-call | flops 3221225472 | bytes 11534336 | tf_op jit(solution)/shard_map/pallas_call | solution.py:124
  108.9 45.8 %all_to_all.23 = bf16[8,192,1152]{2,1,0:T(8,128)(2,1)S(1)} all-to-all(bf16[8,192,1152]{2,1,0:T(8,128)(2,1)S(1)} %shard_map.129), channel_id=1, replica_groups={{0,1,2,3,64,65,66,67},{4,5,6,7,68,69,70,71},{8,9,10,11,72,73,74,75},{12..., dimensions={0} | all-to-all | bytes 7077888 | tf_op jit(solution)/shard_map/all_to_all | solution.py:31
  154.7 0.4 convert_reduce_fusion
  155.1 0.9 fusion.13
  156.0 0.0 copy-done.8
  156.0 2.1 %fusion.15 = (bf16[1,192,1024]{2,1,0:T(8,128)(2,1)}, bf16[1,192,1024]{2,1,0:T(8,128)(2,1)}) fusion(bf16[192,1024]{1,0:T(8,128)(2,1)S(1)} %bitcast.61, bf16[192,1024]{1,0:T(8,128)(2,1)S(1)} %bitcast.63, s32[1024]{0:T(1024)S(1)} %get-tuple-element.30, s32[1024]{0:T(1024)S(1)} %get-tuple-element.31, s32[1024]{0:T(1024)S(1)} %get-tuple-element.28, ...), kind=kOutput, calls=%fused_computation.33 | convolution fusion | flops 424935424 | bytes 1993732 | tf_op jit(solution)/shard_map/dot_general | solution.py:195
  (21 shorter events, 0.1 us)
Async XLA Ops:
  7.2 1.2 copy-start
  7.2 90.8 %all-gather.2.cloned.1.call-start = ((), (), s32[]{:S(2)}) async-start(), calls=%async_computation.3 | async-start | bytes 4456448 | tf_op jit(solution)/shard_map/all_gather | solution.py:161
  23.4 1.0 copy-start.2
  26.9 15.7 %copy-start.4 = (bf16[1,192,1024]{2,1,0:T(8,128)(2,1)S(1)}, bf16[1,192,1024]{2,1,0:T(8,128)(2,1)}, u32[]{:S(2)}) copy-start(bf16[1,192,1024]{2,1,0:T(8,128)(2,1)} %param.15) | copy-start | bytes 1179652
  26.9 61.6 %copy-start.7 = (s32[192]{0:T(256)S(1)}, s32[192]{0:T(256)}, u32[]{:S(2)}) copy-start(s32[192]{0:T(256)} %param.17) | copy-start | bytes 2308
  26.9 68.6 %copy-start.3 = (bf16[192,1024]{1,0:T(8,128)(2,1)S(1)}, bf16[192,1024]{1,0:T(8,128)(2,1)}, u32[]{:S(2)}) copy-start(bf16[192,1024]{1,0:T(8,128)(2,1)} %param.16) | copy-start | bytes 1179652
  26.9 68.6 %copy-start.5 = (bf16[1,192,1024]{2,1,0:T(8,128)(2,1)S(1)}, bf16[1,192,1024]{2,1,0:T(8,128)(2,1)}, u32[]{:S(2)}) copy-start(bf16[1,192,1024]{2,1,0:T(8,128)(2,1)} %param.10) | copy-start | bytes 1179652
  26.9 71.1 %all-to-all-start.1 = ((bf16[8,192,1280]{2,1,0:T(8,128)(2,1)}), bf16[8,192,1280]{2,1,0:T(8,128)(2,1)}, u32[]{:S(2)}, u32[]{:S(2)}) async-start(bf16[8,192,1280]{2,1,0:T(8,128)(2,1)} %pad_maximum_fusion), calls=%async_computation.1 | async-start | bytes 7864320 | tf_op jit(solution)/shard_map/all_to_all | solution.py:31
  33.0 5.5 %collective-permute-start.3 = (f32[8,128]{1,0:T(8,128)S(1)}, f32[8,128]{1,0:T(8,128)S(1)}, u32[]{:S(2)}, u32[]{:S(2)}) collective-permute-start(f32[8,128]{1,0:T(8,128)S(1)} %broadcast_in_dim.37), channel_id=1, source_target_pairs={{0,4},{4,0},{8,12},{12,8},{16,20},{20,16},{24,28},{28,24},{32,36},... | collective-permute-start | bytes 12296 | tf_op jit(solution)/shard_map/ppermute | solution.py:39
  39.2 12.6 %collective-permute-start.4 = (f32[8,128]{1,0:T(8,128)S(1)}, f32[8,128]{1,0:T(8,128)S(1)}, u32[]{:S(2)}, u32[]{:S(2)}) collective-permute-start(f32[8,128]{1,0:T(8,128)S(1)} %broadcast_add_fusion), channel_id=1, source_target_pairs={{0,8},{4,12},{8,0},{12,4},{16,24},{20,28},{24,16},{28,20},{32,40},... | collective-permute-start | bytes 12296 | tf_op jit(solution)/shard_map/ppermute | solution.py:39
  42.6 52.1 %collective-permute-start.2 = (bf16[192,1024]{1,0:T(8,128)(2,1)S(1)}, bf16[192,1024]{1,0:T(8,128)(2,1)S(1)}, u32[]{:S(2)}, u32[]{:S(2)}) collective-permute-start(bf16[192,1024]{1,0:T(8,128)(2,1)S(1)} %bitcast.56), channel_id=1, source_target_pairs={{0,384},{128,256},{256,128},{384,0},{1,385},{129,257},{257,129},{3... | collective-permute-start | bytes 1179656 | tf_op jit(solution)/shard_map/ppermute | solution.py:181
  44.6 50.2 %collective-permute-start.1 = (bf16[192,1024]{1,0:T(8,128)(2,1)S(1)}, bf16[192,1024]{1,0:T(8,128)(2,1)S(1)}, u32[]{:S(2)}, u32[]{:S(2)}) collective-permute-start(bf16[192,1024]{1,0:T(8,128)(2,1)S(1)} %bitcast.57), channel_id=1, source_target_pairs={{0,256},{128,384},{256,0},{384,128},{1,257},{129,385},{257,1},{385... | collective-permute-start | bytes 1179656 | tf_op jit(solution)/shard_map/ppermute | solution.py:181
  49.4 46.1 %collective-permute-start = (bf16[192,1024]{1,0:T(8,128)(2,1)S(1)}, bf16[192,1024]{1,0:T(8,128)(2,1)}, u32[]{:S(2)}, u32[]{:S(2)}) collective-permute-start(bf16[192,1024]{1,0:T(8,128)(2,1)S(1)} %bitcast.58), channel_id=1, source_target_pairs={{0,128},{128,0},{256,384},{384,256},{1,129},{129,1},{257,385},{385... | collective-permute-start | bytes 1179656 | tf_op jit(solution)/shard_map/ppermute | solution.py:181
  52.4 9.4 %collective-permute-start.5 = (f32[8,128]{1,0:T(8,128)S(1)}, f32[8,128]{1,0:T(8,128)S(1)}, u32[]{:S(2)}, u32[]{:S(2)}) collective-permute-start(f32[8,128]{1,0:T(8,128)S(1)} %fusion.33), channel_id=1, source_target_pairs={{0,16},{4,20},{8,24},{12,28},{16,0},{20,4},{24,8},{28,12},{32,48},... | collective-permute-start | bytes 12296 | tf_op jit(solution)/shard_map/ppermute | solution.py:39
  61.9 14.3 %collective-permute-start.6 = (f32[8,128]{1,0:T(8,128)S(1)}, f32[8,128]{1,0:T(8,128)S(1)}, u32[]{:S(2)}, u32[]{:S(2)}) collective-permute-start(f32[8,128]{1,0:T(8,128)S(1)} %add.85), channel_id=1, source_target_pairs={{0,32},{4,36},{8,40},{12,44},{16,48},{20,52},{24,56},{28,60},{32,0... | collective-permute-start | bytes 12296 | tf_op jit(solution)/shard_map/ppermute | solution.py:39
  94.8 0.7 copy-start.6
  98.0 2.2 %copy-start.1 = (bf16[2048,1024]{1,0:T(8,128)(2,1)S(1)}, bf16[2048,1024]{1,0:T(8,128)(2,1)}, u32[]{:S(2)}) copy-start(bf16[2048,1024]{1,0:T(8,128)(2,1)} %all-gather.2.cloned.1.call-done) | copy-start | bytes 12582916
  154.7 1.3 copy-start.8
  154.7 1.3 copy-start.9
Sparse Core Ops, SparseCore 0:
  21.2 73.1 all-gather.1
